TPU v7x, 128 devices: a whole 4x4x4 slice. The times are simulated.
128 devices in a mesh: lon: 16 (over y, x_lo, core), lat: 8 (over z, x_hi).
Axes of the slice: x: 4 (x_hi: 2, x_lo: 2; x = x_hi * 2 + x_lo), y: 4, z: 4, core: 2. Of those that a mesh axis runs over, the one named last changes fastest.
Arguments:
- queries: bfloat16 [8, 32, 64, 1024], P('lat', 'lon'), may hold values from -6 to 6
- keys: bfloat16 [8, 32, 64, 1024], P('lat', 'lon'), may hold values from -6 to 6
- values: bfloat16 [8, 32, 64, 1024], P('lat', 'lon'), may hold values from -6 to 6
- season: bfloat16 [8, 32, 64, 1024], P('lat', 'lon'), may hold values from -6 to 6
- cloud: int32 [8, 32], replicated, may hold values 0 or 1
- pairing: int32 [8, 32, 64], P('lat', 'lon'), may hold values from 0 to 63
Outputs:
- loss_map: float32 [8, 32, 64], P('lat', 'lon')
- query_grad: bfloat16 [8, 32, 64, 1024], P('lat', 'lon')
- key_grad: bfloat16 [8, 32, 64, 1024], P('lat', 'lon')
- value_grad: bfloat16 [8, 32, 64, 1024], P('lat', 'lon')
All inputs are finite; a program needn't handle non-finite values.
Results may differ from a plain program's by a relative error of at most 0.017.
The roundings to bfloat16 on the way count: a program that leaves them out, or rounds other values in their place, can miss the bound.
Values may be sent and summed in bfloat16 or wider, within the bound.
No kernel may reach another device: no remote copies, remote signals or barrier semaphores. Data moves between devices by JAX's collectives and lax.ppermute only.
A program may use at most 128 MiB of HBM per device.

v0:
```python
import jax
import jax.numpy as jnp
from jax import lax
from jax.sharding import PartitionSpec as P

HEADS = 16


NEG_FILL = -1e30


def with_halo(value, sides, width):
    for axis, dim in sides:
        size, length = (lax.axis_size(axis), value.shape[dim])
        up = [(i, (i + 1) % size) for i in range(size)]
        down = [(j, i) for i, j in up]
        last = lax.slice_in_dim(value, length - width, length, axis=dim)
        leading = lax.slice_in_dim(value, 0, width, axis=dim)
        before = lax.ppermute(last, axis, up)
        after = lax.ppermute(leading, axis, down)
        value = jnp.concatenate([before, value, after], axis=dim)
    return value


def shifted_2(value, axis, steps):
    count = lax.axis_size(axis)
    pairs = [(source, (source + steps) % count) for source in range(count)]
    return lax.ppermute(value, axis, pairs)


def passed_along(value, axis, steps):
    count = lax.axis_size(axis)
    leading, last = (max(0, -steps), min(count, count - steps))
    return lax.ppermute(value, axis, [(source, source + steps) for source in range(leading, last)])


def offsets():
    return [(lat_step, lon_step) for lat_step in (-1, 0, 1) for lon_step in (-1, 0, 1)]


def allowed_table(cloud):
    grid_rows = cloud.shape[0]
    row_ids = jnp.arange(grid_rows, dtype=jnp.int32)[:, None]
    columns = []
    for lat_step, lon_step in offsets():
        inside = (row_ids + lat_step >= 0) & (row_ids + lat_step < grid_rows)
        shifted = jnp.roll(cloud, (-lat_step, -lon_step), axis=(0, 1))
        if lat_step == 0 and lon_step == 0:
            usable = jnp.ones(cloud.shape, dtype=jnp.bool_)
        else:
            usable = shifted == 1
        columns.append(inside & usable)
    return jnp.stack(columns, axis=-1)


def window(extended, row_index, block_cols):
    pieces = []
    for lat_step, lon_step in offsets():
        lat_line = extended[row_index + 1 + lat_step]
        pieces.append(lat_line[1 + lon_step : 1 + lon_step + block_cols])
    return jnp.stack(pieces, axis=1)


def split_heads(array, rows_total, head_count):
    return array.reshape(array.shape[0], rows_total, head_count, -1)


def attend(query, key_win, value_win, opened, head_count):
    block_cols, patches, width = query.shape
    head_size = width // head_count
    query_heads = split_heads(query, patches, head_count)
    key_heads = split_heads(key_win, 9 * patches, head_count)
    value_heads = split_heads(value_win, 9 * patches, head_count)
    scores = jnp.einsum(
        "bqhd,bkhd->bhqk", query_heads, key_heads, preferred_element_type=jnp.float32
    ) * head_size ** (-0.5)
    key_mask = jnp.repeat(opened, patches, axis=1)[:, None, None, :]
    scores = jnp.where(key_mask, scores, NEG_FILL)
    highest = jnp.max(scores, axis=-1, keepdims=True)
    log_total = highest + jnp.log(jnp.sum(jnp.exp(scores - highest), axis=-1, keepdims=True))
    attn_weights = jnp.exp(scores - log_total).astype(jnp.bfloat16)
    attention_output = jnp.einsum(
        "bhqk,bkhd->bqhd", attn_weights, value_heads, preferred_element_type=jnp.float32
    )
    return (
        attention_output.reshape(block_cols, patches, width).astype(jnp.bfloat16),
        log_total[..., 0],
    )


def contrast(attention_output, season_window, opened, pair_row):
    block_cols, patches, width = attention_output.shape
    season_flattened = season_window.reshape(block_cols, 9 * patches, width)
    similarity_scores = jnp.einsum(
        "cmu,cju->cmj", attention_output, season_flattened, preferred_element_type=jnp.float32
    )
    key_mask = jnp.repeat(opened, patches, axis=1)[:, None, :]
    similarity_scores = jnp.where(key_mask, similarity_scores, NEG_FILL)
    highest = jnp.max(similarity_scores, axis=-1, keepdims=True)
    contrast_total = highest + jnp.log(
        jnp.sum(jnp.exp(similarity_scores - highest), axis=-1, keepdims=True)
    )
    positive_indicator = pair_row[..., None] == jnp.arange(patches, dtype=jnp.int32)
    chosen = jnp.sum(
        jnp.where(positive_indicator, similarity_scores[:, :, 4 * patches : 5 * patches], 0.0),
        axis=-1,
    )
    loss_row = contrast_total[..., 0] - chosen
    contrastive_weight_table = jnp.exp(similarity_scores - contrast_total).astype(jnp.bfloat16)
    gathered_neighbours = jnp.einsum(
        "cim,cmo->cio",
        contrastive_weight_table,
        season_flattened,
        preferred_element_type=jnp.float32,
    )
    matching_pair = jnp.einsum(
        "yga,yar->ygr",
        positive_indicator.astype(jnp.bfloat16),
        season_window[:, 4],
        preferred_element_type=jnp.float32,
    )
    return (loss_row, (gathered_neighbours - matching_pair).astype(jnp.bfloat16))


def row_delta(attention_output, attended_grad, head_count):
    block_cols, patches, width = attention_output.shape
    product = attention_output.astype(jnp.float32) * attended_grad.astype(jnp.float32)
    summed = jnp.sum(product.reshape(block_cols, patches, head_count, width // head_count), axis=-1)
    return jnp.transpose(summed, (0, 2, 1))


def score_grads(query, key_win, value_win, opened, log_total, deltas, attended_grad, head_count):
    block_cols, patches, width = query.shape
    head_size = width // head_count
    query_heads = split_heads(query, patches, head_count)
    key_heads = split_heads(key_win, 9 * patches, head_count)
    value_heads = split_heads(value_win, 9 * patches, head_count)
    grad_heads = split_heads(attended_grad, patches, head_count)
    scores = jnp.einsum(
        "bqhd,bkhd->bhqk", query_heads, key_heads, preferred_element_type=jnp.float32
    ) * head_size ** (-0.5)
    key_mask = jnp.repeat(opened, patches, axis=1)[:, None, None, :]
    scores = jnp.where(key_mask, scores, NEG_FILL)
    attn_prob = jnp.exp(scores - log_total[..., None])
    grad_dot = jnp.einsum(
        "bqhd,bkhd->bhqk", grad_heads, value_heads, preferred_element_type=jnp.float32
    )
    score_grad = (attn_prob * (grad_dot - deltas[..., None])).astype(jnp.bfloat16)
    result = jnp.einsum(
        "bhqk,bkhd->bqhd", score_grad, key_heads, preferred_element_type=jnp.float32
    ) * head_size ** (-0.5)
    return (
        result.reshape(block_cols, patches, width).astype(jnp.bfloat16),
        score_grad,
        attn_prob.astype(jnp.bfloat16),
    )


def placed_terms(part_rows, target_row):
    total = None
    for slot_index, (lat_step, lon_step) in enumerate(offsets()):
        if 1 + lat_step == target_row:
            padded = jnp.pad(
                part_rows[0][:, slot_index], ((1 + lon_step, 1 - lon_step), (0, 0), (0, 0))
            )
            total = padded if total is None else total + padded
    return total


def body(queries, keys, values, season, cloud, pairing):
    block_rows, block_cols, patches, width = queries.shape
    head_count = HEADS
    head_size = width // head_count
    lat_start = lax.axis_index("lat") * block_rows
    lon_start = lax.axis_index("lon") * block_cols
    query_open = lax.dynamic_slice(
        allowed_table(cloud), (lat_start, lon_start, 0), (block_rows, block_cols, 9)
    )
    key_ext, value_ext, season_ext = (
        with_halo(keys, (("lon", 1), ("lat", 0)), 1),
        with_halo(values, (("lon", 1), ("lat", 0)), 1),
        with_halo(season, (("lon", 1), ("lat", 0)), 1),
    )
    loss_rows, grad_rows, total_rows, delta_rows, key_wins, value_wins = ([], [], [], [], [], [])
    row_index = 0
    opened = query_open[row_index]
    key_win = window(key_ext, row_index, block_cols)
    value_win = window(value_ext, row_index, block_cols)
    attention_output, log_total = attend(queries[row_index], key_win, value_win, opened, head_count)
    loss_row, grad_row = contrast(
        attention_output, window(season_ext, row_index, block_cols), opened, pairing[row_index]
    )
    loss_rows.append(loss_row)
    grad_rows.append(grad_row)
    total_rows.append(log_total)
    delta_rows.append(row_delta(attention_output, grad_row, head_count))
    key_wins.append(key_win)
    value_wins.append(value_win)
    loss_map = jnp.stack(loss_rows)
    key_parts, value_parts = ([], [])
    row_index = 0
    query_row, score_grad, attn_weights = score_grads(
        queries[row_index],
        key_wins[row_index],
        value_wins[row_index],
        query_open[row_index],
        total_rows[row_index],
        delta_rows[row_index],
        grad_rows[row_index],
        head_count,
    )
    query_list = [query_row]
    query_heads = split_heads(queries[row_index], patches, head_count)
    grad_heads = split_heads(grad_rows[row_index], patches, head_count)
    key_part = jnp.einsum(
        "bhqk,bqhd->bkhd", score_grad, query_heads, preferred_element_type=jnp.float32
    ) * head_size ** (-0.5)
    value_part = jnp.einsum(
        "bhqk,bqhd->bkhd", attn_weights, grad_heads, preferred_element_type=jnp.float32
    )
    key_parts.append(key_part.reshape(block_cols, 9, patches, width))
    value_parts.append(value_part.reshape(block_cols, 9, patches, width))
    key_full = jnp.stack(
        [placed_terms(key_parts, target_row) for target_row in range(block_rows + 2)]
    )
    value_full = jnp.stack(
        [placed_terms(value_parts, target_row) for target_row in range(block_rows + 2)]
    )
    west_key, west_value = (
        shifted_2(key_full[:, block_cols + 1].astype(jnp.bfloat16), "lon", 1).astype(jnp.float32),
        shifted_2(value_full[:, block_cols + 1].astype(jnp.bfloat16), "lon", 1).astype(jnp.float32),
    )
    east_key, east_value = (
        shifted_2(key_full[:, 0].astype(jnp.bfloat16), "lon", -1).astype(jnp.float32),
        shifted_2(value_full[:, 0].astype(jnp.bfloat16), "lon", -1).astype(jnp.float32),
    )
    key_trim = key_full[:, 1 : block_cols + 1]
    value_trim = value_full[:, 1 : block_cols + 1]
    key_trim = key_trim.at[:, 0].add(west_key)
    value_trim = value_trim.at[:, 0].add(west_value)
    key_trim = key_trim.at[:, block_cols - 1].add(east_key)
    value_trim = value_trim.at[:, block_cols - 1].add(east_value)
    north_key, north_value = (
        passed_along(key_trim[block_rows + 1].astype(jnp.bfloat16), "lat", 1).astype(jnp.float32),
        passed_along(value_trim[block_rows + 1].astype(jnp.bfloat16), "lat", 1).astype(jnp.float32),
    )
    south_key, south_value = (
        passed_along(key_trim[0].astype(jnp.bfloat16), "lat", -1).astype(jnp.float32),
        passed_along(value_trim[0].astype(jnp.bfloat16), "lat", -1).astype(jnp.float32),
    )
    key_inner = key_trim[1 : block_rows + 1]
    value_inner = value_trim[1 : block_rows + 1]
    key_inner = key_inner.at[0].add(north_key)
    value_inner = value_inner.at[0].add(north_value)
    key_inner = key_inner.at[block_rows - 1].add(south_key)
    value_inner = value_inner.at[block_rows - 1].add(south_value)
    key_grad = key_inner.astype(jnp.bfloat16)
    value_grad = value_inner.astype(jnp.bfloat16)
    query_grad = jnp.stack(query_list)
    return (loss_map, query_grad, key_grad, value_grad)


def solution(mesh):
    return jax.shard_map(
        body,
        mesh=mesh,
        in_specs=(
            P("lat", "lon", None, None),
            P("lat", "lon", None, None),
            P("lat", "lon", None, None),
            P("lat", "lon", None, None),
            P(),
            P("lat", "lon", None),
        ),
        out_specs=(
            P("lat", "lon", None),
            P("lat", "lon", None, None),
            P("lat", "lon", None, None),
            P("lat", "lon", None, None),
        ),
        check_vma=False,
    )
```

profile of v0, /device:TPU:1, one launch (start us, length us, event | category | flops | bytes accessed | tf_op | source)
XLA Modules:
  0.0 239.1 jit_solution(14980628248595094143)
XLA Ops:
  0.7 1.0 fusion.70
  1.7 1.5 collective-permute-start.5
  3.2 1.3 collective-permute-start.4
  4.5 1.0 fusion.71
  5.4 2.3 collective-permute-start.1
  7.7 1.0 fusion.69
  9.1 0.8 slice_bitcast_fusion.60
  9.8 0.8 slice_bitcast_fusion.52
  10.7 0.8 slice_bitcast_fusion.53
  11.5 0.8 slice_bitcast_fusion.61
  13.7 1.2 copy.181
  14.9 4.6 %collective-permute-start.9 = (bf16[1,1,64,1024]{3,2,1,0:T(8,128)(2,1)S(1)}, bf16[1,1,64,1024]{3,2,1,0:T(8,128)(2,1)S(1)}, u32[]{:S(2)}, u32[]{:S(2)}) collective-permute-start(bf16[1,1,64,1024]{3,2,1,0:T(8,128)(2,1)S(1)} %get-tuple-element.140), channel_id=1, source_target_pairs={{8,0},{16,8},{24,16},{32,24},{40,32},{48,40},{56,48},{64,56},{72,6... | collective-permute-start | bytes 393224 | tf_op jit(solution)/shard_map/ppermute | solution.py:20
  19.5 0.9 collective-permute-done.9
  20.5 2.5 %collective-permute-start.10 = (bf16[1,4,64,1024]{3,2,1,0:T(8,128)(2,1)S(1)}, bf16[1,4,64,1024]{3,2,1,0:T(8,128)(2,1)S(1)}, u32[]{:S(2)}, u32[]{:S(2)}) collective-permute-start(bf16[1,4,64,1024]{3,2,1,0:T(8,128)(2,1)S(1)} %constant_dynamic-update-slice_fusion.15), channel_id=1, source_target_pairs={{0,1},{1,2},{2,3},{3,4},{4,5},{5,6},{6,7},{7,0},{8,9},{9,10},{10,1... | collective-permute-start | bytes 1572872 | tf_op jit(solution)/shard_map/ppermute | solution.py:19
  25.1 3.5 %collective-permute-start.7 = (bf16[1,4,64,1024]{3,2,1,0:T(8,128)(2,1)}, bf16[1,4,64,1024]{3,2,1,0:T(8,128)(2,1)}, u32[]{:S(2)}, u32[]{:S(2)}) collective-permute-start(bf16[1,4,64,1024]{3,2,1,0:T(8,128)(2,1)} %constant_dynamic-update-slice_fusion.12), channel_id=1, source_target_pairs={{1,0},{2,1},{3,2},{4,3},{5,4},{6,5},{7,6},{0,7},{9,8},{10,9},{11,1... | collective-permute-start | bytes 1572872 | tf_op jit(solution)/shard_map/ppermute | solution.py:20
  28.7 5.1 %collective-permute-start.3 = (bf16[1,4,64,1024]{3,2,1,0:T(8,128)(2,1)S(1)}, bf16[1,4,64,1024]{3,2,1,0:T(8,128)(2,1)S(1)}, u32[]{:S(2)}, u32[]{:S(2)}) collective-permute-start(bf16[1,4,64,1024]{3,2,1,0:T(8,128)(2,1)S(1)} %constant_dynamic-update-slice_fusion.9), channel_id=1, source_target_pairs={{1,0},{2,1},{3,2},{4,3},{5,4},{6,5},{7,6},{0,7},{9,8},{10,9},{11,1... | collective-permute-start | bytes 1572872 | tf_op jit(solution)/shard_map/ppermute | solution.py:20
  33.9 1.7 collective-permute-done.10
  35.6 3.4 %collective-permute-start.11 = (bf16[1,4,64,1024]{3,2,1,0:T(8,128)(2,1)S(1)}, bf16[1,4,64,1024]{3,2,1,0:T(8,128)(2,1)S(1)}, u32[]{:S(2)}, u32[]{:S(2)}) collective-permute-start(bf16[1,4,64,1024]{3,2,1,0:T(8,128)(2,1)S(1)} %constant_dynamic-update-slice_fusion.15), channel_id=1, source_target_pairs={{1,0},{2,1},{3,2},{4,3},{5,4},{6,5},{7,6},{0,7},{9,8},{10,9},{11,1... | collective-permute-start | bytes 1572872 | tf_op jit(solution)/shard_map/ppermute | solution.py:20
  39.1 0.9 fusion.24
  40.1 40.5 %collective-permute-done.2 = bf16[1,4,64,1024]{3,2,1,0:T(8,128)(2,1)S(1)} collective-permute-done((bf16[1,4,64,1024]{3,2,1,0:T(8,128)(2,1)S(1)}, bf16[1,4,64,1024]{3,2,1,0:T(8,128)(2,1)S(1)}, u32[]{:S(2)}, u32[]{:S(2)}) %collective-permute-start.2) | collective-permute-done | bytes 524320 | tf_op jit(solution)/shard_map/ppermute | solution.py:19
  80.7 9.5 %collective-permute-done.11 = bf16[1,4,64,1024]{3,2,1,0:T(8,128)(2,1)S(1)} collective-permute-done((bf16[1,4,64,1024]{3,2,1,0:T(8,128)(2,1)S(1)}, bf16[1,4,64,1024]{3,2,1,0:T(8,128)(2,1)S(1)}, u32[]{:S(2)}, u32[]{:S(2)}) %collective-permute-start.11) | collective-permute-done | bytes 524320 | tf_op jit(solution)/shard_map/ppermute | solution.py:20
  90.4 0.7 fusion.37
  92.6 1.7 copy.116
  94.6 4.9 %reshape.890 = bf16[2,576,16,64]{3,2,1,0:T(8,128)(2,1)} reshape(bf16[2,9,64,1024]{3,2,1,0:T(8,128)(2,1)S(1)} %copy.111) | data formatting | bytes 4718592 | tf_op jit(solution)/shard_map/reshape | solution.py:65
  99.4 7.0 %copy.115 = bf16[2,576,16,64]{1,3,2,0:T(8,128)(2,1)} copy(bf16[2,576,16,64]{3,2,1,0:T(8,128)(2,1)} %reshape.890) | data formatting | bytes 4718592 | tf_op jit(solution)/shard_map/reshape | solution.py:65
  108.6 1.7 fusion.30
  110.2 1.7 fusion.29
  111.9 1.7 fusion.28
  113.6 2.0 copy.112
  115.6 4.7 %reshape.891 = bf16[2,576,16,64]{3,2,1,0:T(8,128)(2,1)} reshape(bf16[2,9,64,1024]{3,2,1,0:T(8,128)(2,1)S(1)} %copy.112) | data formatting | bytes 4718592 | tf_op jit(solution)/shard_map/reshape | solution.py:65
  120.3 6.0 %copy.113 = bf16[2,576,16,64]{1,3,2,0:T(8,128)(2,1)S(1)} copy(bf16[2,576,16,64]{3,2,1,0:T(8,128)(2,1)} %reshape.891) | data formatting | bytes 4718592 | tf_op jit(solution)/shard_map/reshape | solution.py:65
  126.3 1.0 bitcast_reduce_fusion
  127.8 1.3 fusion.1
  129.1 1.3 copy-done
  130.4 1.0 copy-done.6
  131.4 2.3 convolution_convert_fusion
  133.7 1.2 copy.120
  134.9 2.0 fusion.72
  139.8 6.3 %convolution_bitcast_fusion = f32[2,576,16,64]{1,3,2,0:T(8,128)} fusion(bf16[2,64,16,64]{1,3,2,0:T(8,128)(2,1)S(1)} %bitcast.360, f32[2,16,576,64]{2,3,1,0:T(8,128)} %copy-done, f32[2,16,64]{2,1,0:T(8,128)S(1)} %log_add_fusion, pred[2,576]{1,0:T(4,128)(4,1)S(1)} %broadcast_in_dim.47), kind=kOutput, calls=%fused_computation.12 | convolution fusion | flops 155713536 | bytes 9708672 | tf_op jit(solution)/shard_map/bhqk,bqhd->bkhd/dot_general | solution.py:218
  146.2 2.0 multiply_convert_fusion
  148.1 1.5 copy-done.3
  149.7 3.1 %multiply_bitcast_fusion = f32[2,576,16,64]{1,3,2,0:T(8,128)} fusion(bf16[2,64,16,64]{1,3,2,0:T(8,128)(2,1)S(1)} %bitcast.359, bf16[2,16,64,576]{3,2,1,0:T(8,128)(2,1)S(1)} %multiply_convert_fusion), kind=kOutput, calls=%fused_computation.6 | convolution fusion | flops 152174592 | bytes 7340032 | tf_op jit(solution)/shard_map/bhqk,bqhd->bkhd/dot_general | solution.py:215
  152.8 8.5 %copy.124 = f32[2,576,16,64]{3,2,1,0:T(8,128)} copy(f32[2,576,16,64]{1,3,2,0:T(8,128)} %multiply_bitcast_fusion) | data formatting | bytes 9437184 | tf_op jit(solution)/shard_map/mul | solution.py:215
  161.3 8.9 %reshape.895 = f32[2,9,64,1024]{3,2,1,0:T(8,128)} reshape(f32[2,576,16,64]{3,2,1,0:T(8,128)} %copy.124) | data formatting | bytes 9437184 | tf_op jit(solution)/shard_map/reshape | solution.py:221
  170.1 3.0 %slice_bitcast_fusion.21 = (f32[2,64,1024]{2,1,0:T(8,128)S(1)}, f32[2,64,1024]{2,1,0:T(8,128)S(1)}, f32[2,64,1024]{2,1,0:T(8,128)S(1)}, f32[2,64,1024]{2,1,0:T(8...) fusion(f32[2,9,64,1024]{3,2,1,0:T(8,128)} %reshape.895), kind=kLoop, calls=%fused_computation.60 | loop fusion | bytes 9437184 | tf_op jit(solution)/shard_map/squeeze | solution.py:164
  174.3 0.9 slice_bitcast_fusion.24
  175.2 5.1 %collective-permute-start.13 = (bf16[3,64,1024]{2,1,0:T(8,128)(2,1)S(1)}, bf16[3,64,1024]{2,1,0:T(8,128)(2,1)}, u32[]{:S(2)}, u32[]{:S(2)}) collective-permute-start(bf16[3,64,1024]{2,1,0:T(8,128)(2,1)S(1)} %get-tuple-element.134), channel_id=1, source_target_pairs={{0,120},{8,0},{16,8},{24,16},{32,24},{40,32},{48,40},{56,48},{64,5... | collective-permute-start | bytes 1179656 | tf_op jit(solution)/shard_map/ppermute | solution.py:28
  180.6 8.5 %copy.139 = f32[2,576,16,64]{3,2,1,0:T(8,128)} copy(f32[2,576,16,64]{1,3,2,0:T(8,128)} %convolution_bitcast_fusion) | data formatting | bytes 9437184 | tf_op jit(solution)/shard_map/bhqk,bqhd->bkhd/transpose | solution.py:218
  189.1 8.9 %reshape.900 = f32[2,9,64,1024]{3,2,1,0:T(8,128)} reshape(f32[2,576,16,64]{3,2,1,0:T(8,128)} %copy.139) | data formatting | bytes 9437184 | tf_op jit(solution)/shard_map/reshape | solution.py:222
  197.9 3.0 %slice_bitcast_fusion.11 = (f32[2,64,1024]{2,1,0:T(8,128)S(1)}, f32[2,64,1024]{2,1,0:T(8,128)S(1)}, f32[2,64,1024]{2,1,0:T(8,128)S(1)}, f32[2,64,1024]{2,1,0:T(8...) fusion(f32[2,9,64,1024]{3,2,1,0:T(8,128)} %reshape.900), kind=kLoop, calls=%fused_computation.47 | loop fusion | bytes 9437184 | tf_op jit(solution)/shard_map/squeeze | solution.py:164
  201.7 3.4 %collective-permute-start.17 = (bf16[3,64,1024]{2,1,0:T(8,128)(2,1)S(1)}, bf16[3,64,1024]{2,1,0:T(8,128)(2,1)S(1)}, u32[]{:S(2)}, u32[]{:S(2)}) collective-permute-start(bf16[3,64,1024]{2,1,0:T(8,128)(2,1)S(1)} %get-tuple-element.132), channel_id=1, source_target_pairs={{0,120},{8,0},{16,8},{24,16},{32,24},{40,32},{48,40},{56,48},{64,5... | collective-permute-start | bytes 1179656 | tf_op jit(solution)/shard_map/ppermute | solution.py:28
  205.9 1.3 fusion.11
  207.2 1.2 fusion.9
  208.5 0.8 slice_bitcast_fusion.29
  209.4 4.4 %collective-permute-start.14 = (bf16[2,64,1024]{2,1,0:T(8,128)(2,1)}, bf16[2,64,1024]{2,1,0:T(8,128)(2,1)S(1)}, u32[]{:S(2)}, u32[]{:S(2)}) collective-permute-start(bf16[2,64,1024]{2,1,0:T(8,128)(2,1)} %get-tuple-element.138), channel_id=1, source_target_pairs={{0,1},{1,2},{2,3},{3,4},{4,5},{5,6},{6,7},{8,9},{9,10},{10,11},{11... | collective-permute-start | bytes 786440 | tf_op jit(solution)/shard_map/ppermute | solution.py:34
  213.7 1.3 collective-permute-start.15
  215.5 0.8 slice_bitcast_fusion.27
  216.3 6.3 %collective-permute-start.18 = (bf16[2,64,1024]{2,1,0:T(8,128)(2,1)}, bf16[2,64,1024]{2,1,0:T(8,128)(2,1)}, u32[]{:S(2)}, u32[]{:S(2)}) collective-permute-start(bf16[2,64,1024]{2,1,0:T(8,128)(2,1)} %get-tuple-element.136), channel_id=1, source_target_pairs={{0,1},{1,2},{2,3},{3,4},{4,5},{5,6},{6,7},{8,9},{9,10},{10,11},{11... | collective-permute-start | bytes 786440 | tf_op jit(solution)/shard_map/ppermute | solution.py:34
  222.6 1.3 collective-permute-start.19
  224.0 1.8 fusion.4
  225.7 1.9 copy.153
  227.7 1.8 fusion.17
  229.4 7.9 %collective-permute-done.19 = bf16[2,64,1024]{2,1,0:T(8,128)(2,1)} collective-permute-done((bf16[2,64,1024]{2,1,0:T(8,128)(2,1)}, bf16[2,64,1024]{2,1,0:T(8,128)(2,1)}, u32[]{:S(2)}, u32[]{:S(2)}) %collective-permute-start.19) | collective-permute-done | bytes 262176 | tf_op jit(solution)/shard_map/ppermute | solution.py:34
  237.3 1.8 fusion.14
  (144 shorter events, 14.7 us)
Async XLA Ops:
  0.6 23.1 %copy-start.11 = (bf16[1,2,64,1024]{3,2,1,0:T(8,128)(2,1)S(1)}, bf16[1,2,64,1024]{3,2,1,0:T(8,128)(2,1)}, u32[]{:S(2)}) copy-start(bf16[1,2,64,1024]{3,2,1,0:T(8,128)(2,1)} %param.23) | copy-start | bytes 786436
  0.6 18.9 %copy-start.9 = (bf16[1,2,64,1024]{3,2,1,0:T(8,128)(2,1)S(1)}, bf16[1,2,64,1024]{3,2,1,0:T(8,128)(2,1)}, u32[]{:S(2)}) copy-start(bf16[1,2,64,1024]{3,2,1,0:T(8,128)(2,1)} %param.25) | copy-start | bytes 786436
  1.7 26.9 %copy-start.10 = (bf16[1,2,64,1024]{3,2,1,0:T(8,128)(2,1)S(1)}, bf16[1,2,64,1024]{3,2,1,0:T(8,128)(2,1)}, u32[]{:S(2)}) copy-start(bf16[1,2,64,1024]{3,2,1,0:T(8,128)(2,1)} %param.24) | copy-start | bytes 786436
  1.7 22.7 %collective-permute-start.5 = (bf16[1,1,64,1024]{3,2,1,0:T(8,128)(2,1)S(1)}, bf16[1,1,64,1024]{3,2,1,0:T(8,128)(2,1)S(1)}, u32[]{:S(2)}, u32[]{:S(2)}) collective-permute-start(bf16[1,1,64,1024]{3,2,1,0:T(8,128)(2,1)S(1)} %get-tuple-element.142), channel_id=1, source_target_pairs={{8,0},{16,8},{24,16},{32,24},{40,32},{48,40},{56,48},{64,56},{72,6... | collective-permute-start | bytes 393224 | tf_op jit(solution)/shard_map/ppermute | solution.py:20
  3.2 19.8 %collective-permute-start.4 = (bf16[1,1,64,1024]{3,2,1,0:T(8,128)(2,1)S(1)}, bf16[1,1,64,1024]{3,2,1,0:T(8,128)(2,1)S(1)}, u32[]{:S(2)}, u32[]{:S(2)}) collective-permute-start(bf16[1,1,64,1024]{3,2,1,0:T(8,128)(2,1)S(1)} %get-tuple-element.143), channel_id=1, source_target_pairs={{0,8},{8,16},{16,24},{24,32},{32,40},{40,48},{48,56},{56,64},{64,7... | collective-permute-start | bytes 393224 | tf_op jit(solution)/shard_map/ppermute | solution.py:19
  5.4 23.2 %collective-permute-start.1 = (bf16[1,1,64,1024]{3,2,1,0:T(8,128)(2,1)S(1)}, bf16[1,1,64,1024]{3,2,1,0:T(8,128)(2,1)S(1)}, u32[]{:S(2)}, u32[]{:S(2)}) collective-permute-start(bf16[1,1,64,1024]{3,2,1,0:T(8,128)(2,1)S(1)} %get-tuple-element.144), channel_id=1, source_target_pairs={{8,0},{16,8},{24,16},{32,24},{40,32},{48,40},{56,48},{64,56},{72,6... | collective-permute-start | bytes 393224 | tf_op jit(solution)/shard_map/ppermute | solution.py:20
  7.7 20.9 %collective-permute-start = (bf16[1,1,64,1024]{3,2,1,0:T(8,128)(2,1)S(1)}, bf16[1,1,64,1024]{3,2,1,0:T(8,128)(2,1)S(1)}, u32[]{:S(2)}, u32[]{:S(2)}) collective-permute-start(bf16[1,1,64,1024]{3,2,1,0:T(8,128)(2,1)S(1)} %get-tuple-element.145), channel_id=1, source_target_pairs={{0,8},{8,16},{16,24},{24,32},{32,40},{40,48},{48,56},{56,64},{64,7... | collective-permute-start | bytes 393224 | tf_op jit(solution)/shard_map/ppermute | solution.py:19
  8.7 6.2 %collective-permute-start.8 = (bf16[1,1,64,1024]{3,2,1,0:T(8,128)(2,1)S(1)}, bf16[1,1,64,1024]{3,2,1,0:T(8,128)(2,1)S(1)}, u32[]{:S(2)}, u32[]{:S(2)}) collective-permute-start(bf16[1,1,64,1024]{3,2,1,0:T(8,128)(2,1)S(1)} %get-tuple-element.141), channel_id=1, source_target_pairs={{0,8},{8,16},{16,24},{24,32},{32,40},{40,48},{48,56},{56,64},{64,7... | collective-permute-start | bytes 393224 | tf_op jit(solution)/shard_map/ppermute | solution.py:19
  14.9 18.9 %copy-start.18 = (bf16[1,1,64,1024]{3,2,1,0:T(8,128)(2,1)}, bf16[1,1,64,1024]{3,2,1,0:T(8,128)(2,1)S(1)}, u32[]{:S(2)}) copy-start(bf16[1,1,64,1024]{3,2,1,0:T(8,128)(2,1)S(1)} %collective-permute-done.8) | copy-start | bytes 393220
  14.9 5.5 %collective-permute-start.9 = (bf16[1,1,64,1024]{3,2,1,0:T(8,128)(2,1)S(1)}, bf16[1,1,64,1024]{3,2,1,0:T(8,128)(2,1)S(1)}, u32[]{:S(2)}, u32[]{:S(2)}) collective-permute-start(bf16[1,1,64,1024]{3,2,1,0:T(8,128)(2,1)S(1)} %get-tuple-element.140), channel_id=1, source_target_pairs={{8,0},{16,8},{24,16},{32,24},{40,32},{48,40},{56,48},{64,56},{72,6... | collective-permute-start | bytes 393224 | tf_op jit(solution)/shard_map/ppermute | solution.py:20
  20.5 15.1 %collective-permute-start.10 = (bf16[1,4,64,1024]{3,2,1,0:T(8,128)(2,1)S(1)}, bf16[1,4,64,1024]{3,2,1,0:T(8,128)(2,1)S(1)}, u32[]{:S(2)}, u32[]{:S(2)}) collective-permute-start(bf16[1,4,64,1024]{3,2,1,0:T(8,128)(2,1)S(1)} %constant_dynamic-update-slice_fusion.15), channel_id=1, source_target_pairs={{0,1},{1,2},{2,3},{3,4},{4,5},{5,6},{6,7},{7,0},{8,9},{9,10},{10,1... | collective-permute-start | bytes 1572872 | tf_op jit(solution)/shard_map/ppermute | solution.py:19
  23.0 10.8 %copy-start.12 = (bf16[1,1,64,1024]{3,2,1,0:T(8,128)(2,1)}, bf16[1,1,64,1024]{3,2,1,0:T(8,128)(2,1)S(1)}, u32[]{:S(2)}) copy-start(bf16[1,1,64,1024]{3,2,1,0:T(8,128)(2,1)S(1)} %collective-permute-done.4) | copy-start | bytes 393220
  25.1 83.5 %collective-permute-start.7 = (bf16[1,4,64,1024]{3,2,1,0:T(8,128)(2,1)}, bf16[1,4,64,1024]{3,2,1,0:T(8,128)(2,1)}, u32[]{:S(2)}, u32[]{:S(2)}) collective-permute-start(bf16[1,4,64,1024]{3,2,1,0:T(8,128)(2,1)} %constant_dynamic-update-slice_fusion.12), channel_id=1, source_target_pairs={{1,0},{2,1},{3,2},{4,3},{5,4},{6,5},{7,6},{0,7},{9,8},{10,9},{11,1... | collective-permute-start | bytes 1572872 | tf_op jit(solution)/shard_map/ppermute | solution.py:20
  28.6 61.8 %collective-permute-start.6 = (bf16[1,4,64,1024]{3,2,1,0:T(8,128)(2,1)}, bf16[1,4,64,1024]{3,2,1,0:T(8,128)(2,1)S(1)}, u32[]{:S(2)}, u32[]{:S(2)}) collective-permute-start(bf16[1,4,64,1024]{3,2,1,0:T(8,128)(2,1)} %constant_dynamic-update-slice_fusion.12), channel_id=1, source_target_pairs={{0,1},{1,2},{2,3},{3,4},{4,5},{5,6},{6,7},{7,0},{8,9},{9,10},{10,1... | collective-permute-start | bytes 1572872 | tf_op jit(solution)/shard_map/ppermute | solution.py:19
  28.6 5.3 %copy-start.16 = (bf16[1,1,64,1024]{3,2,1,0:T(8,128)(2,1)}, bf16[1,1,64,1024]{3,2,1,0:T(8,128)(2,1)S(1)}, u32[]{:S(2)}) copy-start(bf16[1,1,64,1024]{3,2,1,0:T(8,128)(2,1)S(1)} %collective-permute-done) | copy-start | bytes 393220
  28.7 5.2 %copy-start.14 = (bf16[1,1,64,1024]{3,2,1,0:T(8,128)(2,1)}, bf16[1,1,64,1024]{3,2,1,0:T(8,128)(2,1)S(1)}, u32[]{:S(2)}) copy-start(bf16[1,1,64,1024]{3,2,1,0:T(8,128)(2,1)S(1)} %collective-permute-done.1) | copy-start | bytes 393220
  28.7 61.6 %collective-permute-start.3 = (bf16[1,4,64,1024]{3,2,1,0:T(8,128)(2,1)S(1)}, bf16[1,4,64,1024]{3,2,1,0:T(8,128)(2,1)S(1)}, u32[]{:S(2)}, u32[]{:S(2)}) collective-permute-start(bf16[1,4,64,1024]{3,2,1,0:T(8,128)(2,1)S(1)} %constant_dynamic-update-slice_fusion.9), channel_id=1, source_target_pairs={{1,0},{2,1},{3,2},{4,3},{5,4},{6,5},{7,6},{0,7},{9,8},{10,9},{11,1... | collective-permute-start | bytes 1572872 | tf_op jit(solution)/shard_map/ppermute | solution.py:20
  33.8 46.7 %collective-permute-start.2 = (bf16[1,4,64,1024]{3,2,1,0:T(8,128)(2,1)S(1)}, bf16[1,4,64,1024]{3,2,1,0:T(8,128)(2,1)S(1)}, u32[]{:S(2)}, u32[]{:S(2)}) collective-permute-start(bf16[1,4,64,1024]{3,2,1,0:T(8,128)(2,1)S(1)} %constant_dynamic-update-slice_fusion.9), channel_id=1, source_target_pairs={{0,1},{1,2},{2,3},{3,4},{4,5},{5,6},{6,7},{7,0},{8,9},{9,10},{10,1... | collective-permute-start | bytes 1572872 | tf_op jit(solution)/shard_map/ppermute | solution.py:19
  35.6 54.6 %collective-permute-start.11 = (bf16[1,4,64,1024]{3,2,1,0:T(8,128)(2,1)S(1)}, bf16[1,4,64,1024]{3,2,1,0:T(8,128)(2,1)S(1)}, u32[]{:S(2)}, u32[]{:S(2)}) collective-permute-start(bf16[1,4,64,1024]{3,2,1,0:T(8,128)(2,1)S(1)} %constant_dynamic-update-slice_fusion.15), channel_id=1, source_target_pairs={{1,0},{2,1},{3,2},{4,3},{5,4},{6,5},{7,6},{0,7},{9,8},{10,9},{11,1... | collective-permute-start | bytes 1572872 | tf_op jit(solution)/shard_map/ppermute | solution.py:20
  39.0 41.6 %copy-start.17 = (bf16[1,1,64,1024]{3,2,1,0:T(8,128)(2,1)S(1)}, bf16[1,1,64,1024]{3,2,1,0:T(8,128)(2,1)}, u32[]{:S(2)}) copy-start(bf16[1,1,64,1024]{3,2,1,0:T(8,128)(2,1)} %copy-done.16) | copy-start | bytes 393220
  40.0 50.2 %copy-start.15 = (bf16[1,1,64,1024]{3,2,1,0:T(8,128)(2,1)S(1)}, bf16[1,1,64,1024]{3,2,1,0:T(8,128)(2,1)}, u32[]{:S(2)}) copy-start(bf16[1,1,64,1024]{3,2,1,0:T(8,128)(2,1)} %copy-done.14) | copy-start | bytes 393220
  99.4 7.0 %copy-start.13 = (bf16[1,1,64,1024]{3,2,1,0:T(8,128)(2,1)S(1)}, bf16[1,1,64,1024]{3,2,1,0:T(8,128)(2,1)}, u32[]{:S(2)}) copy-start(bf16[1,1,64,1024]{3,2,1,0:T(8,128)(2,1)} %copy-done.12) | copy-start | bytes 393220
  126.3 1.5 copy-start.1
  127.8 2.7 %copy-start = (f32[2,16,576,64]{2,3,1,0:T(8,128)}, f32[2,16,576,64]{2,3,1,0:T(8,128)S(1)}, u32[]{:S(2)}) copy-start(f32[2,16,576,64]{2,3,1,0:T(8,128)S(1)} %get-tuple-element.167) | copy-start | bytes 14155780
  127.8 3.6 %copy-start.6 = (bf16[2,576,16,64]{1,3,2,0:T(8,128)(2,1)S(1)}, bf16[2,576,16,64]{1,3,2,0:T(8,128)(2,1)}, u32[]{:S(2)}) copy-start(bf16[2,576,16,64]{1,3,2,0:T(8,128)(2,1)} %copy.115) | copy-start | bytes 7077892
  131.4 3.5 %copy-start.5 = (bf16[2,9,64,1024]{3,2,1,0:T(8,128)(2,1)S(1)}, bf16[2,9,64,1024]{3,2,1,0:T(8,128)(2,1)}, u32[]{:S(2)}) copy-start(bf16[2,9,64,1024]{3,2,1,0:T(8,128)(2,1)} %copy.116) | copy-start | bytes 7077892
  133.7 3.5 %copy-start.19 = (s32[1,2,64]{2,1,0:T(2,128)S(1)}, s32[1,2,64]{2,1,0:T(2,128)}, u32[]{:S(2)}) copy-start(s32[1,2,64]{2,1,0:T(2,128)} %param.27) | copy-start | bytes 1540
  139.5 6.6 %slice-start = ((s8[5242880]{0:T(1024)(128)(4,1)}), s8[1048576]{0:T(1024)(128)(4,1)S(1)}, s32[]{:S(2)}) async-start(s8[5242880]{0:T(1024)(128)(4,1)} %bitcast.354), calls=%async_computation | async-start | bytes 2097152
  139.8 6.4 %slice-start.1 = ((s8[5242880]{0:T(1024)(128)(4,1)}), s8[4194304]{0:T(1024)(128)(4,1)S(1)}, s32[]{:S(2)}) async-start(s8[5242880]{0:T(1024)(128)(4,1)} %bitcast.354), calls=%async_computation.1 | async-start | bytes 8388608
  139.8 6.3 %copy-start.7 = (bf16[2,576,16,64]{1,3,2,0:T(8,128)(2,1)S(1)}, bf16[2,576,16,64]{1,3,2,0:T(8,128)(2,1)}, u32[]{:S(2)}) copy-start(bf16[2,576,16,64]{1,3,2,0:T(8,128)(2,1)} %copy.115) | copy-start | bytes 7077892
  148.1 1.6 copy-start.3
  174.3 6.1 %copy-start.8 = (f32[3,4,64,1024]{3,2,1,0:T(8,128)}, f32[3,4,64,1024]{3,2,1,0:T(8,128)S(1)}, u32[]{:S(2)}) copy-start(f32[3,4,64,1024]{3,2,1,0:T(8,128)S(1)} %pad_maximum_fusion) | copy-start | bytes 9437188
  175.2 32.0 %collective-permute-start.13 = (bf16[3,64,1024]{2,1,0:T(8,128)(2,1)S(1)}, bf16[3,64,1024]{2,1,0:T(8,128)(2,1)}, u32[]{:S(2)}, u32[]{:S(2)}) collective-permute-start(bf16[3,64,1024]{2,1,0:T(8,128)(2,1)S(1)} %get-tuple-element.134), channel_id=1, source_target_pairs={{0,120},{8,0},{16,8},{24,16},{32,24},{40,32},{48,40},{56,48},{64,5... | collective-permute-start | bytes 1179656 | tf_op jit(solution)/shard_map/ppermute | solution.py:28
  180.3 25.6 %collective-permute-start.12 = (bf16[3,64,1024]{2,1,0:T(8,128)(2,1)}, bf16[3,64,1024]{2,1,0:T(8,128)(2,1)}, u32[]{:S(2)}, u32[]{:S(2)}) collective-permute-start(bf16[3,64,1024]{2,1,0:T(8,128)(2,1)} %get-tuple-element.135), channel_id=1, source_target_pairs={{0,8},{8,16},{16,24},{24,32},{32,40},{40,48},{48,56},{56,64},{64,7... | collective-permute-start | bytes 1179656 | tf_op jit(solution)/shard_map/ppermute | solution.py:28
  201.7 13.4 %collective-permute-start.17 = (bf16[3,64,1024]{2,1,0:T(8,128)(2,1)S(1)}, bf16[3,64,1024]{2,1,0:T(8,128)(2,1)S(1)}, u32[]{:S(2)}, u32[]{:S(2)}) collective-permute-start(bf16[3,64,1024]{2,1,0:T(8,128)(2,1)S(1)} %get-tuple-element.132), channel_id=1, source_target_pairs={{0,120},{8,0},{16,8},{24,16},{32,24},{40,32},{48,40},{56,48},{64,5... | collective-permute-start | bytes 1179656 | tf_op jit(solution)/shard_map/ppermute | solution.py:28
  205.2 9.9 %collective-permute-start.16 = (bf16[3,64,1024]{2,1,0:T(8,128)(2,1)S(1)}, bf16[3,64,1024]{2,1,0:T(8,128)(2,1)S(1)}, u32[]{:S(2)}, u32[]{:S(2)}) collective-permute-start(bf16[3,64,1024]{2,1,0:T(8,128)(2,1)S(1)} %get-tuple-element.133), channel_id=1, source_target_pairs={{0,8},{8,16},{16,24},{24,32},{32,40},{40,48},{48,56},{56,64},{64,7... | collective-permute-start | bytes 1179656 | tf_op jit(solution)/shard_map/ppermute | solution.py:28
  209.4 18.3 %collective-permute-start.14 = (bf16[2,64,1024]{2,1,0:T(8,128)(2,1)}, bf16[2,64,1024]{2,1,0:T(8,128)(2,1)S(1)}, u32[]{:S(2)}, u32[]{:S(2)}) collective-permute-start(bf16[2,64,1024]{2,1,0:T(8,128)(2,1)} %get-tuple-element.138), channel_id=1, source_target_pairs={{0,1},{1,2},{2,3},{3,4},{4,5},{5,6},{6,7},{8,9},{9,10},{10,11},{11... | collective-permute-start | bytes 786440 | tf_op jit(solution)/shard_map/ppermute | solution.py:34
  213.7 13.9 %collective-permute-start.15 = (bf16[2,64,1024]{2,1,0:T(8,128)(2,1)}, bf16[2,64,1024]{2,1,0:T(8,128)(2,1)}, u32[]{:S(2)}, u32[]{:S(2)}) collective-permute-start(bf16[2,64,1024]{2,1,0:T(8,128)(2,1)} %get-tuple-element.139), channel_id=1, source_target_pairs={{1,0},{2,1},{3,2},{4,3},{5,4},{6,5},{7,6},{9,8},{10,9},{11,10},{12... | collective-permute-start | bytes 786440 | tf_op jit(solution)/shard_map/ppermute | solution.py:34
  215.1 8.8 %copy-start.2 = (bf16[2,576,16,64]{1,3,2,0:T(8,128)(2,1)S(1)}, bf16[2,576,16,64]{1,3,2,0:T(8,128)(2,1)}, u32[]{:S(2)}) copy-start(bf16[2,576,16,64]{1,3,2,0:T(8,128)(2,1)} %copy-done.1) | copy-start | bytes 7077892
  215.1 8.8 %copy-start.4 = (bf16[2,16,64,576]{3,2,1,0:T(8,128)(2,1)S(1)}, bf16[2,16,64,576]{3,2,1,0:T(8,128)(2,1)}, u32[]{:S(2)}) copy-start(bf16[2,16,64,576]{3,2,1,0:T(8,128)(2,1)} %copy-done.3) | copy-start | bytes 7077892
  216.3 13.1 %collective-permute-start.18 = (bf16[2,64,1024]{2,1,0:T(8,128)(2,1)}, bf16[2,64,1024]{2,1,0:T(8,128)(2,1)}, u32[]{:S(2)}, u32[]{:S(2)}) collective-permute-start(bf16[2,64,1024]{2,1,0:T(8,128)(2,1)} %get-tuple-element.136), channel_id=1, source_target_pairs={{0,1},{1,2},{2,3},{3,4},{4,5},{5,6},{6,7},{8,9},{9,10},{10,11},{11... | collective-permute-start | bytes 786440 | tf_op jit(solution)/shard_map/ppermute | solution.py:34
  222.6 14.7 %collective-permute-start.19 = (bf16[2,64,1024]{2,1,0:T(8,128)(2,1)}, bf16[2,64,1024]{2,1,0:T(8,128)(2,1)}, u32[]{:S(2)}, u32[]{:S(2)}) collective-permute-start(bf16[2,64,1024]{2,1,0:T(8,128)(2,1)} %get-tuple-element.137), channel_id=1, source_target_pairs={{1,0},{2,1},{3,2},{4,3},{5,4},{6,5},{7,6},{9,8},{10,9},{11,10},{12... | collective-permute-start | bytes 786440 | tf_op jit(solution)/shard_map/ppermute | solution.py:34
where the time goes:
time: 243 us; the launch traced here: 239 us
  local copies, waits for them, and re-layouts  97.1 us (40%)
  waiting for transfers between devices  60.6 us (25%)
  starting transfers between devices  46.3 us (19%)
  matrix products  19.4 us (8%)
  other arithmetic  14.5 us (6%)
    ppermute x6, waiting for transfers between devices, with_halo(): before = lax.ppermute(last, axis, up)  42.2 us
    reshape x5, local copies, waits for them, and re-layouts, split_heads(): return array.reshape(array.shape[0], rows_total, head_count, -1)  22.8 us
    ppermute x6, starting transfers between devices, with_halo(): after = lax.ppermute(leading, axis, down)  20.4 us
    unnamed x72, local copies, waits for them, and re-layouts  14.7 us
    ppermute x4, starting transfers between devices, passed_along(): lax.ppermute(value, axis, [(source, source + steps) for source in range(l...  13.3 us
    ppermute x6, waiting for transfers between devices, with_halo(): after = lax.ppermute(leading, axis, down)  10.5 us
    reshape x1, local copies, waits for them, and re-layouts, body(): value_parts.append(value_part.reshape(block_cols, 9, patches, width))  8.87 us
    reshape x1, local copies, waits for them, and re-layouts, body(): key_parts.append(key_part.reshape(block_cols, 9, patches, width))  8.85 us
  transfers between devices with their start and end apart: 20, of which 5 were waited for; matrix products, arithmetic and copies ran while one was open for 26% of the time, Pallas kernels for 0%

commit v1 on v0

v1 whole, which is shorter than its diff:
```python
import functools

import jax
import jax.numpy as jnp
from jax import lax
from jax.experimental import pallas as pl
from jax.experimental.pallas import tpu as pltpu
from jax.sharding import PartitionSpec as P

HEADS = 16
HDIM = 64
PP = 64
WIDTH = HEADS * HDIM
GROUP = 4
GW = GROUP * HDIM
GROUPS = HEADS // GROUP
ROWS = GROUP * PP
WIN = 9 * PP
REG = 12 * PP
EXT = WIDTH + 128
NEG_FILL = -1e30
SCALE = HDIM ** -0.5
AXES = ("lon", "lat")
VMEM_LIMIT = 48 * 1024 * 1024
BF = jnp.bfloat16
F32 = jnp.float32

NT = (((1,), (1,)), ((), ()))
NN = (((1,), (0,)), ((), ()))


def dot(a, b, dims):
    return lax.dot_general(a, b, dims, preferred_element_type=F32)


def routes(rows, cols):
    def at(r, c):
        return (c % cols) * rows + r

    cells = [(r, c) for r in range(rows) for c in range(cols)]

    def away(c):
        return c + 1 if c % 2 else c - 1

    def hop(r):
        return r + 2 if r % 2 == 0 else r - 2

    return dict(
        swap=[(at(r, c), at(r ^ 1, c)) for r, c in cells],
        off=[(at(r, c), at(r, away(c))) for r, c in cells],
        cor=[(at(r, c), at(r ^ 1, away(c))) for r, c in cells],
        far=[(at(r, c), at(hop(r), c)) for r, c in cells if 0 <= hop(r) < rows],
        twin=[(at(r, c), at(r, c ^ 1)) for r, c in cells],
    )


def exchange(own, near, face_of, way):
    swap = lax.ppermute(own, AXES, way["swap"])
    off = lax.ppermute(near, AXES, way["off"])
    cor = lax.ppermute(near, AXES, way["cor"])
    far = lax.ppermute(jnp.concatenate([swap, cor], axis=0), AXES, way["far"])
    facing = jnp.concatenate([face_of(own), face_of(swap), face_of(far)], axis=0)
    twin = lax.ppermute(facing, AXES, way["twin"])
    return (own, swap, far, off, cor, twin)


def region_piece(pieces, n, row, col):
    own, swap, far, off, cor, twin = pieces
    if col == 0:
        return (off.at[0], cor.at[0], far.at[2])[row]
    if col == 3:
        return twin.at[row]
    base = (own, swap, far)[row]
    return base.at[n if col == 1 else 1 - n]


def window_copies(pieces, n, dst, sems, first):
    out = []
    for t in range(2):
        mine = []
        for row in range(3):
            for col in range(3):
                slot = row * 3 + col
                mine.append(
                    pltpu.make_async_copy(
                        region_piece(pieces, n, row, col + t),
                        dst.at[t, pl.ds(slot * PP, PP), :],
                        sems.at[first + t * 9 + slot],
                    )
                )
        out.append(mine)
    return out


def begin(copies):
    for c in copies:
        c.start()


def finish(copies):
    for c in copies:
        c.wait()


def spread(x):
    lane = lax.broadcasted_iota(jnp.int32, x.shape, 1) // HDIM
    return jnp.concatenate([jnp.where(lane == h, x, jnp.zeros_like(x)) for h in range(GROUP)], axis=0)


def gather_heads(y):
    lane = lax.broadcasted_iota(jnp.int32, (PP, GW), 1) // HDIM
    out = y[0:PP]
    for h in range(1, GROUP):
        out = jnp.where(lane == h, y[h * PP : (h + 1) * PP], out)
    return out


def group_slice(g):
    return pl.ds(pl.multiple_of(g * GW, GW), GW)


def attend_kernel(n_ref, q_ref, mask_ref, *rest):
    k_pieces, v_pieces = rest[0:6], rest[6:12]
    att_ref, stat_ref, k9, v9, sems = rest[12:]
    n = n_ref[0]
    kc = window_copies(k_pieces, n, k9, sems, 0)
    vc = window_copies(v_pieces, n, v9, sems, 18)
    for t in range(2):
        begin(kc[t])
        begin(vc[t])
    for t in range(2):
        finish(kc[t])
        finish(vc[t])
        qt = n if t == 0 else 1 - n
        stat_ref[t] = jnp.zeros((PP, 128), F32)

        def step(g, carry):
            fs = group_slice(g)
            q = spread(q_ref[qt, :, fs] * SCALE)
            s = dot(q, k9[t, :, fs], NT) + mask_ref[t : t + 1, :]
            m = jnp.max(s, axis=1, keepdims=True)
            e = jnp.exp(s - m)
            total = jnp.sum(e, axis=1, keepdims=True)
            p = (e * (1.0 / total)).astype(BF)
            lse = m + jnp.log(total)
            att_ref[t, :, fs] = gather_heads(dot(p, v9[t, :, fs], NN)).astype(BF)
            lane = lax.broadcasted_iota(jnp.int32, (PP, 128), 1)
            stat = stat_ref[t]
            for h in range(GROUP):
                stat = jnp.where(lane == g * GROUP + h, lse[h * PP : (h + 1) * PP], stat)
            stat_ref[t] = stat
            return carry

        lax.fori_loop(0, GROUPS, step, 0)


def contrast_kernel(n_ref, att_ref, stat_ref, mask_ref, pos_ref, *rest):
    pieces = rest[0:6]
    loss_ref, grad_ref, stats_ref, s12, sems = rest[6:]
    n = n_ref[0]
    copies = []
    for row in range(3):
        for col in range(4):
            slot = row * 4 + col
            copies.append(
                pltpu.make_async_copy(
                    region_piece(pieces, n, row, col), s12.at[pl.ds(slot * PP, PP), :], sems.at[slot]
                )
            )
    begin(copies)
    finish(copies)
    att = jnp.concatenate([att_ref[0], att_ref[1]], axis=0)
    side = lax.broadcasted_iota(jnp.int32, (2 * PP, REG), 0) < PP
    mask = jnp.where(side, mask_ref[0:1, :], mask_ref[1:2, :])
    logits = dot(att, s12[...], NT) + mask
    m = jnp.max(logits, axis=1, keepdims=True)
    e = jnp.exp(logits - m)
    total = jnp.sum(e, axis=1, keepdims=True)
    w = (e * (1.0 / total)).astype(BF)
    ctotal = m + jnp.log(total)
    pos = pos_ref[...]
    hit = lax.broadcasted_iota(jnp.int32, (2 * PP, 4 * PP), 1) == pos
    chosen = jnp.sum(jnp.where(hit, logits[:, 0 : 4 * PP], 0.0), axis=1, keepdims=True)
    loss_ref[...] = ctotal - chosen
    acc = dot(w, s12[...], NN) - dot(hit.astype(F32).astype(BF), s12[0 : 4 * PP, :], NN)
    grad = acc.astype(BF)
    prod = grad.astype(F32) * att.astype(F32)
    high = prod.astype(BF)
    low = (prod - high.astype(F32)).astype(BF)
    feat = lax.broadcasted_iota(jnp.int32, (WIDTH, 128), 0) // HDIM
    lane = lax.broadcasted_iota(jnp.int32, (WIDTH, 128), 1)
    pick = (lane == feat + HEADS).astype(F32).astype(BF)
    delta = dot(high, pick, NN) + dot(low, pick, NN)
    stat = jnp.concatenate([stat_ref[0], stat_ref[1]], axis=0) + delta
    part0 = stat.astype(BF).astype(F32)
    part1 = (stat - part0).astype(BF).astype(F32)
    part2 = (stat - part0 - part1).astype(BF).astype(F32)
    packed = part0 + pltpu.roll(part1, 32, 1) + pltpu.roll(part2, 64, 1)
    packed = packed.astype(BF)
    for t in range(2):
        rows = slice(t * PP, (t + 1) * PP)
        grad_ref[t, :, 0:WIDTH] = grad[rows]
        grad_ref[t, :, WIDTH:EXT] = packed[rows]
        stats_ref[t] = stat[rows]


def head_column(stat, index):
    lane = lax.broadcasted_iota(jnp.int32, (PP, 128), 1)
    cols = [
        jnp.sum(jnp.where(lane == index + h, stat, 0.0), axis=1, keepdims=True) for h in range(GROUP)
    ]
    return jnp.concatenate(cols, axis=0)


def query_kernel(n_ref, q_ref, grad_ref, stats_ref, mask_ref, *rest):
    k_pieces, v_pieces = rest[0:6], rest[6:12]
    out_ref, k9, v9, sems = rest[12:]
    n = n_ref[0]
    kc = window_copies(k_pieces, n, k9, sems, 0)
    vc = window_copies(v_pieces, n, v9, sems, 18)
    for t in range(2):
        begin(kc[t])
        begin(vc[t])
    for t in range(2):
        finish(kc[t])
        finish(vc[t])
        qt = n if t == 0 else 1 - n

        def step(g, carry):
            fs = group_slice(g)
            q = spread(q_ref[qt, :, fs] * SCALE)
            stat = stats_ref[t]
            lse = head_column(stat, g * GROUP)
            delta = head_column(stat, g * GROUP + HEADS)
            s = dot(q, k9[t, :, fs], NT) + mask_ref[t : t + 1, :]
            p = jnp.exp(s - lse)
            gd = dot(spread(grad_ref[t, :, fs]), v9[t, :, fs], NT)
            ds = (p * (gd - delta)).astype(BF)
            out = gather_heads(dot(ds, k9[t, :, fs], NN)) * SCALE
            out_ref[qt, :, fs] = out.astype(BF)
            return carry

        lax.fori_loop(0, GROUPS, step, 0)


def key_kernel(n_ref, k_ref, v_ref, mask_ref, *rest):
    q_pieces, g_pieces = rest[0:6], rest[6:12]
    kout_ref, vout_ref, q9, g9, rows_ref, sems = rest[12:]
    n = n_ref[0]
    qc = window_copies(q_pieces, n, q9, sems, 0)
    gc = window_copies(g_pieces, 0, g9, sems, 18)
    for t in range(2):
        begin(qc[t])
        begin(gc[t])
    for t in range(2):
        finish(qc[t])
        finish(gc[t])
        kt = n if t == 0 else 1 - n
        parts = jnp.transpose(g9[t, :, WIDTH:EXT].astype(F32))
        stats = parts[0:32] + parts[32:64] + parts[64:96]
        rows_ref[0:HEADS] = stats[0:HEADS] + mask_ref[t : t + 1, :]
        rows_ref[HEADS : 2 * HEADS] = stats[HEADS : 2 * HEADS]

        def step(g, carry):
            fs = group_slice(g)
            ks = spread(k_ref[kt, :, fs] * SCALE)
            vs = spread(v_ref[kt, :, fs])
            qw = q9[t, :, fs]
            gw = g9[t, :, fs]
            s = dot(ks, qw, NT)
            gd = dot(vs, gw, NT)
            ps, dss = [], []
            for h in range(GROUP):
                part = slice(h * PP, (h + 1) * PP)
                lse = rows_ref[pl.ds(g * GROUP + h, 1), :]
                delta = rows_ref[pl.ds(HEADS + g * GROUP + h, 1), :]
                p = jnp.exp(s[part] - lse)
                ps.append(p.astype(BF))
                dss.append((p * (gd[part] - delta)).astype(BF))
            p = jnp.concatenate(ps, axis=0)
            ds = jnp.concatenate(dss, axis=0)
            kout_ref[kt, :, fs] = (gather_heads(dot(ds, qw, NN)) * SCALE).astype(BF)
            vout_ref[kt, :, fs] = gather_heads(dot(p, gw, NN)).astype(BF)
            return carry

        lax.fori_loop(0, GROUPS, step, 0)


SMEM = pl.BlockSpec(memory_space=pltpu.SMEM)
VMEM = pl.BlockSpec(memory_space=pltpu.VMEM)
ANY = pl.BlockSpec(memory_space=pl.ANY)


def call(kernel, name, in_specs, out_shape, scratch, flops):
    return pl.pallas_call(
        kernel,
        name=name,
        out_shape=out_shape,
        in_specs=in_specs,
        out_specs=jax.tree.map(lambda _: VMEM, out_shape),
        scratch_shapes=scratch,
        compiler_params=pltpu.CompilerParams(vmem_limit_bytes=VMEM_LIMIT),
        cost_estimate=pl.CostEstimate(flops=flops, bytes_accessed=6_000_000, transcendentals=0),
    )


def shape(dims, dtype):
    return jax.ShapeDtypeStruct(dims, dtype)


def body(way, queries, keys, values, season, cloud, pairing):
    grid_rows, grid_cols = cloud.shape
    lat = lax.axis_index("lat")
    lon = lax.axis_index("lon")
    odd = lon % 2
    q, k, v, s = (x[0] for x in (queries, keys, values, season))

    def near_of(x):
        return lax.dynamic_slice_in_dim(x, odd, 1, axis=0)

    def face_of(x):
        return lax.dynamic_slice_in_dim(x, 1 - odd, 1, axis=0)

    sign = 2 * odd - 1
    near_col = 2 * lon + odd
    reg_cols = jnp.stack([near_col + sign, near_col, near_col - sign, near_col - 2 * sign]) % grid_cols
    outer = jnp.where(lat % 2 == 0, lat - 1, lat + 1)
    reg_rows = jnp.stack([lat, lat ^ 1, outer])
    inside = (reg_rows >= 0) & (reg_rows < grid_rows)
    clear = cloud[jnp.clip(reg_rows, 0, grid_rows - 1)][:, reg_cols] == 1
    clear = clear & inside[:, None]
    itself = jnp.zeros((3, 3), jnp.bool_).at[0, 1].set(True)
    q_open = jnp.stack([clear[:, 0:3] | itself, clear[:, 1:4] | itself])
    pad = jnp.zeros((3, 1), jnp.bool_)
    c_open = jnp.stack(
        [jnp.concatenate([q_open[0], pad], axis=1), jnp.concatenate([pad, q_open[1]], axis=1)]
    )
    own_clear = jnp.stack([clear[0, 1], clear[0, 2]])
    k_open = (own_clear[:, None, None] & inside[None, :, None]) | itself[None]
    q_mask = jnp.where(jnp.repeat(q_open.reshape(2, 9), PP, axis=1), 0.0, NEG_FILL)
    c_mask = jnp.where(jnp.repeat(c_open.reshape(2, 12), PP, axis=1), 0.0, NEG_FILL)
    k_mask = jnp.where(jnp.repeat(k_open.reshape(2, 9), PP, axis=1), 0.0, -NEG_FILL)
    n = odd.astype(jnp.int32).reshape(1)
    pair = pairing[0]
    pair = jnp.where(odd == 1, pair[::-1], pair)
    pos = (pair + jnp.array([[PP], [2 * PP]], jnp.int32)).reshape(2 * PP, 1)

    kp = exchange(k, near_of(k), face_of, way)
    vp = exchange(v, near_of(v), face_of, way)
    sp = exchange(s, near_of(s), face_of, way)
    qp = exchange(q, near_of(q), face_of, way)

    att, stat = call(
        attend_kernel,
        "attend",
        [SMEM, VMEM, VMEM] + [ANY] * 12,
        (shape((2, PP, WIDTH), BF), shape((2, PP, 128), F32)),
        [pltpu.VMEM((2, WIN, WIDTH), BF)] * 2 + [pltpu.SemaphoreType.DMA((36,))],
        2_400_000_000,
    )(n, q, q_mask, *kp, *vp)

    loss, grad, stats = call(
        contrast_kernel,
        "contrast",
        [SMEM, VMEM, VMEM, VMEM, VMEM] + [ANY] * 6,
        (shape((2 * PP, 1), F32), shape((2, PP, EXT), BF), shape((2, PP, 128), F32)),
        [pltpu.VMEM((REG, WIDTH), BF), pltpu.SemaphoreType.DMA((12,))],
        1_200_000_000,
    )(n, att, stat, c_mask, pos, *sp)

    gp = exchange(grad, grad[0:1], lambda x: x[1:2], way)

    query_grad = call(
        query_kernel,
        "query_grads",
        [SMEM, VMEM, VMEM, VMEM, VMEM] + [ANY] * 12,
        shape((2, PP, WIDTH), BF),
        [pltpu.VMEM((2, WIN, WIDTH), BF)] * 2 + [pltpu.SemaphoreType.DMA((36,))],
        3_600_000_000,
    )(n, q, grad, stats, q_mask, *kp, *vp)

    key_grad, value_grad = call(
        key_kernel,
        "key_grads",
        [SMEM, VMEM, VMEM, VMEM] + [ANY] * 12,
        (shape((2, PP, WIDTH), BF), shape((2, PP, WIDTH), BF)),
        [
            pltpu.VMEM((2, WIN, WIDTH), BF),
            pltpu.VMEM((2, WIN, EXT), BF),
            pltpu.VMEM((2 * HEADS, WIN), F32),
            pltpu.SemaphoreType.DMA((36,)),
        ],
        4_800_000_000,
    )(n, k, v, k_mask, *qp, *gp)

    loss_map = loss.reshape(2, PP)
    loss_map = jnp.where(odd == 1, loss_map[::-1], loss_map)
    return (loss_map[None], query_grad[None], key_grad[None], value_grad[None])


def solution(mesh):
    block = P("lat", "lon", None, None)
    line = P("lat", "lon", None)
    way = routes(mesh.shape["lat"], mesh.shape["lon"])
    return jax.shard_map(
        functools.partial(body, way),
        mesh=mesh,
        in_specs=(block, block, block, block, P(), line),
        out_specs=(line, block, block, block),
        check_vma=False,
    )
```

time: 243 us -> 144 us (0.59)
  local copies, waits for them, and re-layouts: 97.1 us -> 17.8 us
  waiting for transfers between devices: 60.6 us -> 8.79 us
  Pallas kernels: 0 us -> 39.6 us
  matrix products: 19.4 us -> 0 us
  starting transfers between devices: 46.3 us -> 65 us
  other arithmetic: 14.5 us -> 8.82 us
    ppermute x20 -> x25, waiting for transfers between devices: 60.6 us -> 8.79 us  [the longest x5 8.65 us: exchange(): cor = lax.ppermute(near, AXES, way['cor'])]
    reshape x8 -> x2, local copies, waits for them, and re-layouts: 40.8 us -> 0.22 us  [the longest x1 0.14 us: body(): pos = (pair + jnp.array([[PP], [2 * PP]], jnp.int32)).reshape(2 * PP, 1)]
    pallas_call x0 -> x4, Pallas kernels: none -> 39.6 us  [the longest x1 12.4 us: body(): call(attend_kernel, 'attend', [SMEM, VMEM, VMEM] + [ANY] * 12, (shape((2,...]
    dot_general x9 -> x0, matrix products: 19.4 us -> none  [the longest x1 6.33 us: body(): jnp.einsum('bhqk,bqhd->bkhd', attn_weights, grad_heads, preferred_element...]
    ppermute x20 -> x25, starting transfers between devices: 46.3 us -> 65 us  [the longest x5 24.1 us: exchange(): twin = lax.ppermute(facing, AXES, way['twin'])]
    unnamed x72 -> x62, local copies, waits for them, and re-layouts: 14.7 us -> 5.88 us
    transpose x2 -> x0, local copies, waits for them, and re-layouts: 8.57 us -> none  [the longest x1 8.51 us: body(): jnp.einsum('bhqk,bqhd->bkhd', attn_weights, grad_heads, preferred_element...]
    mul x1 -> x0, local copies, waits for them, and re-layouts: 8.5 us -> none  [body(): jnp.einsum('bhqk,bqhd->bkhd', score_grad, query_heads, preferred_element_...]
  transfers between devices with their start and end apart: 20 -> 25, of which waited for: 5 -> 3; matrix products, arithmetic and copies ran while one was open for 26% -> 15% of each run, Pallas kernels for 0% -> 20%
where the time goes in v1:
time: 144 us; the launch traced here: 141 us
  starting transfers between devices  65 us (45%)
  Pallas kernels  39.6 us (28%)
  local copies, waits for them, and re-layouts  17.8 us (12%)
  other arithmetic  8.82 us (6%)
  waiting for transfers between devices  8.79 us (6%)
    ppermute x5, starting transfers between devices, exchange(): twin = lax.ppermute(facing, AXES, way['twin'])  24.1 us
    ppermute x5, starting transfers between devices, exchange(): far = lax.ppermute(jnp.concatenate([swap, cor], axis=0), AXES, way['far'])  18.4 us
    pallas_call x1, Pallas kernels, body(): call(attend_kernel, 'attend', [SMEM, VMEM, VMEM] + [ANY] * 12, (shape((2,...  12.4 us
    pallas_call x1, Pallas kernels, body(): call(query_kernel, 'query_grads', [SMEM, VMEM, VMEM, VMEM, VMEM] + [ANY]...  11.7 us
    pallas_call x1, Pallas kernels, body(): call(key_kernel, 'key_grads', [SMEM, VMEM, VMEM, VMEM] + [ANY] * 12, (sha...  11.1 us
    ppermute x5, starting transfers between devices, exchange(): swap = lax.ppermute(own, AXES, way['swap'])  9.63 us
    ppermute x5, waiting for transfers between devices, exchange(): cor = lax.ppermute(near, AXES, way['cor'])  8.65 us
    ppermute x5, starting transfers between devices, exchange(): cor = lax.ppermute(near, AXES, way['cor'])  8.13 us
  transfers between devices with their start and end apart: 25, of which 3 were waited for; matrix products, arithmetic and copies ran while one was open for 15% of the time, Pallas kernels for 20%

profile of v1, /device:TPU:1, one launch (start us, length us, event | category | flops | bytes accessed | tf_op | source)
XLA Modules:
  0.0 141.4 jit_solution(16367587809060963318)
XLA Ops:
  0.6 3.7 %collective-permute-start = (bf16[2,64,1024]{2,1,0:T(8,128)(2,1)}, bf16[2,64,1024]{2,1,0:T(8,128)(2,1)S(1)}, u32[]{:S(2)}, u32[]{:S(2)}) collective-permute-start(bf16[2,64,1024]{2,1,0:T(8,128)(2,1)} %bitcast.55), channel_id=1, source_target_pairs={{0,1},{8,9},{16,17},{24,25},{32,33},{40,41},{48,49},{56,57},{64,65... | collective-permute-start | bytes 786440 | tf_op jit(solution)/shard_map/ppermute | solution.py:58
  4.3 1.7 %dynamic-slice_bitcast_fusion.6 = (bf16[1,64,1024]{2,1,0:T(8,128)(2,1)}, bf16[1,64,1024]{2,1,0:T(8,128)(2,1)}) fusion(bf16[1,2,64,1024]{3,2,1,0:T(8,128)(2,1)} %param.10, s32[]{:T(128)S(6)} %select_n.110, s32[]{:T(128)S(6)} %select_n.109), kind=kLoop, calls=%fused_computation.18 | loop fusion | bytes 524296 | tf_op jit(solution)/shard_map/dynamic_slice | solution.py:322
  6.0 1.7 %collective-permute-start.1 = (bf16[1,64,1024]{2,1,0:T(8,128)(2,1)}, bf16[1,64,1024]{2,1,0:T(8,128)(2,1)S(1)}, u32[]{:S(2)}, u32[]{:S(2)}) collective-permute-start(bf16[1,64,1024]{2,1,0:T(8,128)(2,1)} %get-tuple-element.39), channel_id=1, source_target_pairs={{0,121},{8,17},{16,9},{24,33},{32,25},{40,49},{48,41},{56,65},{64,... | collective-permute-start | bytes 393224 | tf_op jit(solution)/shard_map/ppermute | solution.py:60
  7.7 1.2 collective-permute-start.5
  9.0 0.7 dynamic-slice_bitcast_fusion.4
  9.7 1.0 collective-permute-start.6
  10.7 1.7 %collective-permute-start.10 = (bf16[2,64,1024]{2,1,0:T(8,128)(2,1)S(1)}, bf16[2,64,1024]{2,1,0:T(8,128)(2,1)S(1)}, u32[]{:S(2)}, u32[]{:S(2)}) collective-permute-start(bf16[2,64,1024]{2,1,0:T(8,128)(2,1)S(1)} %bitcast.49), channel_id=1, source_target_pairs={{0,1},{8,9},{16,17},{24,25},{32,33},{40,41},{48,49},{56,57},{64,65... | collective-permute-start | bytes 786440 | tf_op jit(solution)/shard_map/ppermute | solution.py:58
  12.4 0.6 compare_reduce_fusion
  13.0 0.7 dynamic-slice_bitcast_fusion.2
  13.7 0.7 fusion.5
  14.4 0.6 gather_fusion
  15.2 0.7 copy-done.26
  15.9 0.6 gather_fusion.1
  16.5 2.0 %scatter.4 = pred[3,3]{0,1:T(4,128)(4,1)S(1)} dynamic-update-slice(pred[3,3]{0,1:T(4,128)(4,1)S(1)} %broadcast.186, pred[1,1]{0,1:T(4,128)(4,1)} %bitcast.15, s32[]{:T(128)} %bitcast.16, s32[]{:T(128)} %bitcast.17) | dynamic-update-slice | bytes 6 | tf_op jit(solution)/shard_map/scatter | solution.py:332
  18.6 0.6 copy-done.29
  19.3 0.5 fusion.4
  19.8 0.1 copy.20
  20.0 0.1 copy.19
  20.5 4.3 %collective-permute-done.1.rest_4_ = bf16[1,64,1024]{2,1,0:T(8,128)(2,1)S(1)} collective-permute-done((bf16[1,64,1024]{2,1,0:T(8,128)(2,1)}, bf16[1,64,1024]{2,1,0:T(8,128)(2,1)S(1)}, u32[]{:S(2)}, u32[]{:S(2)}) %collective-permute-start.1) | collective-permute-done | bytes 131104 | tf_op jit(solution)/shard_map/ppermute | solution.py:60
  24.8 2.2 %collective-permute-start.3 = (bf16[1,64,1024]{2,1,0:T(8,128)(2,1)}, bf16[1,64,1024]{2,1,0:T(8,128)(2,1)S(1)}, u32[]{:S(2)}, u32[]{:S(2)}) collective-permute-start(bf16[1,64,1024]{2,1,0:T(8,128)(2,1)} %get-tuple-element.39), channel_id=1, source_target_pairs={{0,120},{8,16},{16,8},{24,32},{32,24},{40,48},{48,40},{56,64},{64,... | collective-permute-start | bytes 393224 | tf_op jit(solution)/shard_map/ppermute | solution.py:59
  27.0 1.9 %collective-permute-start.11 = (bf16[1,64,1024]{2,1,0:T(8,128)(2,1)S(1)}, bf16[1,64,1024]{2,1,0:T(8,128)(2,1)S(1)}, u32[]{:S(2)}, u32[]{:S(2)}) collective-permute-start(bf16[1,64,1024]{2,1,0:T(8,128)(2,1)S(1)} %get-tuple-element.35), channel_id=1, source_target_pairs={{0,121},{8,17},{16,9},{24,33},{32,25},{40,49},{48,41},{56,65},{64,... | collective-permute-start | bytes 393224 | tf_op jit(solution)/shard_map/ppermute | solution.py:60
  29.0 0.9 collective-permute-start.8
  29.8 3.6 %collective-permute-start.2 = (bf16[3,64,1024]{2,1,0:T(8,128)(2,1)S(1)}, bf16[3,64,1024]{2,1,0:T(8,128)(2,1)S(1)}, u32[]{:S(2)}, u32[]{:S(2)}) collective-permute-start(bf16[3,64,1024]{2,1,0:T(8,128)(2,1)S(1)} %pad_maximum_fusion.2), channel_id=1, source_target_pairs={{0,2},{8,10},{16,18},{24,26},{32,34},{40,42},{48,50},{56,58},{64,6... | collective-permute-start | bytes 1179656 | tf_op jit(solution)/shard_map/ppermute | solution.py:61
  33.5 3.5 %collective-permute-start.7 = (bf16[3,64,1024]{2,1,0:T(8,128)(2,1)S(1)}, bf16[3,64,1024]{2,1,0:T(8,128)(2,1)S(1)}, u32[]{:S(2)}, u32[]{:S(2)}) collective-permute-start(bf16[3,64,1024]{2,1,0:T(8,128)(2,1)S(1)} %pad_maximum_fusion.4), channel_id=1, source_target_pairs={{0,2},{8,10},{16,18},{24,26},{32,34},{40,42},{48,50},{56,58},{64,6... | collective-permute-start | bytes 1179656 | tf_op jit(solution)/shard_map/ppermute | solution.py:61
  37.1 3.3 %collective-permute-start.12 = (bf16[3,64,1024]{2,1,0:T(8,128)(2,1)S(1)}, bf16[3,64,1024]{2,1,0:T(8,128)(2,1)S(1)}, u32[]{:S(2)}, u32[]{:S(2)}) collective-permute-start(bf16[3,64,1024]{2,1,0:T(8,128)(2,1)S(1)} %pad_maximum_fusion.6), channel_id=1, source_target_pairs={{0,2},{8,10},{16,18},{24,26},{32,34},{40,42},{48,50},{56,58},{64,6... | collective-permute-start | bytes 1179656 | tf_op jit(solution)/shard_map/ppermute | solution.py:61
  40.5 0.9 copy-done.21
  41.4 0.8 pad_maximum_fusion.3
  42.2 6.0 %collective-permute-start.4 = (bf16[3,64,1024]{2,1,0:T(8,128)(2,1)}, bf16[3,64,1024]{2,1,0:T(8,128)(2,1)}, u32[]{:S(2)}, u32[]{:S(2)}) collective-permute-start(bf16[3,64,1024]{2,1,0:T(8,128)(2,1)} %pad_maximum_fusion.3), channel_id=1, source_target_pairs={{0,8},{8,0},{16,24},{24,16},{32,40},{40,32},{48,56},{56,48},{64,72... | collective-permute-start | bytes 1179656 | tf_op jit(solution)/shard_map/ppermute | solution.py:63
  48.3 0.9 pad_maximum_fusion.5
  49.2 7.1 %collective-permute-start.9 = (bf16[3,64,1024]{2,1,0:T(8,128)(2,1)}, bf16[3,64,1024]{2,1,0:T(8,128)(2,1)}, u32[]{:S(2)}, u32[]{:S(2)}) collective-permute-start(bf16[3,64,1024]{2,1,0:T(8,128)(2,1)} %pad_maximum_fusion.5), channel_id=1, source_target_pairs={{0,8},{8,0},{16,24},{24,16},{32,40},{40,32},{48,56},{56,48},{64,72... | collective-permute-start | bytes 1179656 | tf_op jit(solution)/shard_map/ppermute | solution.py:63
  56.3 0.8 pad_maximum_fusion.7
  57.2 3.3 %collective-permute-start.14 = (bf16[3,64,1024]{2,1,0:T(8,128)(2,1)}, bf16[3,64,1024]{2,1,0:T(8,128)(2,1)}, u32[]{:S(2)}, u32[]{:S(2)}) collective-permute-start(bf16[3,64,1024]{2,1,0:T(8,128)(2,1)} %pad_maximum_fusion.7), channel_id=1, source_target_pairs={{0,8},{8,0},{16,24},{24,16},{32,40},{40,32},{48,56},{56,48},{64,72... | collective-permute-start | bytes 1179656 | tf_op jit(solution)/shard_map/ppermute | solution.py:63
  60.4 1.9 %pad_add_fusion = pred[2]{0:T(512)(128)(4,1)} fusion(pred[1]{0:T(512)(128)(4,1)} %bitcast.31, pred[1]{0:T(512)(128)(4,1)} %bitcast.30), kind=kLoop, calls=%fused_computation.36 | loop fusion | flops 2 | bytes 4 | tf_op jit(solution)/shard_map/stack | solution.py:338
  62.7 0.1 reshape.479.pos_ref
  62.8 0.8 dynamic-slice_bitcast_fusion
  63.6 0.1 copy-done.25
  63.7 1.5 %collective-permute-start.13 = (bf16[1,64,1024]{2,1,0:T(8,128)(2,1)S(1)}, bf16[1,64,1024]{2,1,0:T(8,128)(2,1)S(1)}, u32[]{:S(2)}, u32[]{:S(2)}) collective-permute-start(bf16[1,64,1024]{2,1,0:T(8,128)(2,1)S(1)} %copy-done.25), channel_id=1, source_target_pairs={{0,120},{8,16},{16,8},{24,32},{32,24},{40,48},{48,40},{56,64},{64,... | collective-permute-start | bytes 393224 | tf_op jit(solution)/shard_map/ppermute | solution.py:59
  65.3 0.7 copy-done.16
  65.9 2.2 %collective-permute-start.16 = (bf16[1,64,1024]{2,1,0:T(8,128)(2,1)}, bf16[1,64,1024]{2,1,0:T(8,128)(2,1)S(1)}, u32[]{:S(2)}, u32[]{:S(2)}) collective-permute-start(bf16[1,64,1024]{2,1,0:T(8,128)(2,1)} %get-tuple-element.33), channel_id=1, source_target_pairs={{0,121},{8,17},{16,9},{24,33},{32,25},{40,49},{48,41},{56,65},{64,... | collective-permute-start | bytes 393224 | tf_op jit(solution)/shard_map/ppermute | solution.py:60
  68.2 0.1 collective-permute-start.18
  68.3 1.8 %collective-permute-start.15 = (bf16[2,64,1024]{2,1,0:T(8,128)(2,1)S(1)}, bf16[2,64,1024]{2,1,0:T(8,128)(2,1)S(1)}, u32[]{:S(2)}, u32[]{:S(2)}) collective-permute-start(bf16[2,64,1024]{2,1,0:T(8,128)(2,1)S(1)} %bitcast.51), channel_id=1, source_target_pairs={{0,1},{8,9},{16,17},{24,25},{32,33},{40,41},{48,49},{56,57},{64,65... | collective-permute-start | bytes 786440 | tf_op jit(solution)/shard_map/ppermute | solution.py:58
  70.1 1.0 copy-done.10
  71.1 0.9 copy-done.17
  72.0 12.4 %attend.1 = (bf16[2,64,1024]{2,1,0:T(8,128)(2,1)S(1)}, f32[2,64,128]{2,1,0:T(8,128)S(1)}) custom-call(s32[1]{0:T(128)} %bitcast.n_ref, bf16[2,64,1024]{2,1,0:T(8,128)(2,1)S(1)} %bitcast.52, f32[2,576]{1,0:T(2,128)S(1)} %select_n.108.mask_ref, bf16[2,64,1024]{2,1,0:T(8,128)(2,1)S(1)} %bitcast.56, bf16[2,64,1024]{2,1,0:T(8,128)(2,1)S(1)} %collective-permute-done.rest_1_, ...), custom_call_target="tpu_custom_call" | custom-call | flops 2400000000 | bytes 6000000 | tf_op jit(solution)/shard_map/attend/pallas_call | solution.py:353
  84.4 4.4 %contrast.1 = (f32[128,1]{1,0:T(8,128)S(1)}, bf16[2,64,1152]{2,1,0:T(8,128)(2,1)S(1)}, f32[2,64,128]{2,1,0:T(8,128)S(1)}) custom-call(s32[1]{0:T(128)} %bitcast.n_ref, bf16[2,64,1024]{2,1,0:T(8,128)(2,1)S(1)} %get-tuple-element.23.att_ref, f32[2,64,128]{2,1,0:T(8,128)S(1)} %get-tuple-element.24.stat_ref, f32[2,768]{1,0:T(2,128)S(1)} %select_n.113.mask_ref, ...), custom_call_target="tpu_custom_call" | custom-call | flops 1200000000 | bytes 6000000 | tf_op jit(solution)/shard_map/contrast/pallas_call | solution.py:362
  88.8 1.2 collective-permute-start.20
  90.1 0.7 fusion.3
  90.8 1.3 collective-permute-start.21
  92.3 0.1 copy.24
  92.6 0.8 pad_maximum_fusion.8
  93.4 4.5 %collective-permute-start.17 = (bf16[3,64,1024]{2,1,0:T(8,128)(2,1)}, bf16[3,64,1024]{2,1,0:T(8,128)(2,1)}, u32[]{:S(2)}, u32[]{:S(2)}) collective-permute-start(bf16[3,64,1024]{2,1,0:T(8,128)(2,1)} %pad_maximum_fusion.8), channel_id=1, source_target_pairs={{0,2},{8,10},{16,18},{24,26},{32,34},{40,42},{48,50},{56,58},{64,6... | collective-permute-start | bytes 1179656 | tf_op jit(solution)/shard_map/ppermute | solution.py:61
  97.9 4.4 %collective-permute-done.21.rest_10_ = bf16[1,64,1152]{2,1,0:T(8,128)(2,1)S(1)} collective-permute-done((bf16[1,64,1152]{2,1,0:T(8,128)(2,1)}, bf16[1,64,1152]{2,1,0:T(8,128)(2,1)S(1)}, u32[]{:S(2)}, u32[]{:S(2)}) %collective-permute-start.21) | collective-permute-done | bytes 147488 | tf_op jit(solution)/shard_map/ppermute | solution.py:60
  102.3 0.9 pad_maximum_fusion
  103.2 3.6 %collective-permute-start.22 = (bf16[3,64,1152]{2,1,0:T(8,128)(2,1)}, bf16[3,64,1152]{2,1,0:T(8,128)(2,1)S(1)}, u32[]{:S(2)}, u32[]{:S(2)}) collective-permute-start(bf16[3,64,1152]{2,1,0:T(8,128)(2,1)} %pad_maximum_fusion), channel_id=1, source_target_pairs={{0,2},{8,10},{16,18},{24,26},{32,34},{40,42},{48,50},{56,58},{64,6... | collective-permute-start | bytes 1327112 | tf_op jit(solution)/shard_map/ppermute | solution.py:61
  106.9 1.0 constant_dynamic-slice_fusion
  107.9 0.8 pad_maximum_fusion.9
  108.7 3.8 %collective-permute-start.19 = (bf16[3,64,1024]{2,1,0:T(8,128)(2,1)}, bf16[3,64,1024]{2,1,0:T(8,128)(2,1)}, u32[]{:S(2)}, u32[]{:S(2)}) collective-permute-start(bf16[3,64,1024]{2,1,0:T(8,128)(2,1)} %pad_maximum_fusion.9), channel_id=1, source_target_pairs={{0,8},{8,0},{16,24},{24,16},{32,40},{40,32},{48,56},{56,48},{64,72... | collective-permute-start | bytes 1179656 | tf_op jit(solution)/shard_map/ppermute | solution.py:63
  112.6 0.1 reduce.7
  112.9 0.8 copy-done.19
  113.7 0.1 slice-done
  113.9 3.9 %collective-permute-start.24 = (bf16[3,64,1152]{2,1,0:T(8,128)(2,1)S(1)}, bf16[3,64,1152]{2,1,0:T(8,128)(2,1)S(1)}, u32[]{:S(2)}, u32[]{:S(2)}) collective-permute-start(bf16[3,64,1152]{2,1,0:T(8,128)(2,1)S(1)} %pad_maximum_fusion.1), channel_id=1, source_target_pairs={{0,8},{8,0},{16,24},{24,16},{32,40},{40,32},{48,56},{56,48},{64,72... | collective-permute-start | bytes 1327112 | tf_op jit(solution)/shard_map/ppermute | solution.py:63
  117.8 11.7 %query_grads.1 = bf16[2,64,1024]{2,1,0:T(8,128)(2,1)} custom-call(s32[1]{0:T(128)} %bitcast.n_ref, bf16[2,64,1024]{2,1,0:T(8,128)(2,1)S(1)} %bitcast.53, bf16[2,64,1152]{2,1,0:T(8,128)(2,1)S(1)} %get-tuple-element.26.grad_ref.rest_6_, f32[2,64,128]{2,1,0:T(8,128)S(1)} %get-tuple-element.27.stats_ref, f32[2,576]{1,0:T(2,128)S(1)} %select_n.108.mask_ref, ...), custom_call_target="tpu_custom_call" | custom-call | flops 3600000000 | bytes 6000000 | tf_op jit(solution)/shard_map/query_grads/pallas_call | solution.py:373
  129.5 0.6 select_bitcast_fusion
  130.1 11.1 %key_grads.1 = (bf16[2,64,1024]{2,1,0:T(8,128)(2,1)}, bf16[2,64,1024]{2,1,0:T(8,128)(2,1)}) custom-call(s32[1]{0:T(128)} %bitcast.n_ref, bf16[2,64,1024]{2,1,0:T(8,128)(2,1)S(1)} %bitcast.58, bf16[2,64,1024]{2,1,0:T(8,128)(2,1)S(1)} %bitcast.62, f32[2,576]{1,0:T(2,128)S(1)} %select_n.117.mask_ref, bf16[2,64,1024]{2,1,0:T(8,128)(2,1)S(1)} %bitcast.54, ...), custom_call_target="tpu_custom_call" | custom-call | flops 4800000000 | bytes 6000000 | tf_op jit(solution)/shard_map/key_grads/pallas_call | solution.py:382
  (124 shorter events, 2.5 us)
Async XLA Ops:
  0.6 13.8 %copy-start = (s32[8,32]{1,0:T(8,128)S(1)}, s32[8,32]{1,0:T(8,128)}, u32[]{:S(2)}) copy-start(s32[8,32]{1,0:T(8,128)} %param.13) | copy-start | bytes 3076
  0.6 26.4 %collective-permute-start = (bf16[2,64,1024]{2,1,0:T(8,128)(2,1)}, bf16[2,64,1024]{2,1,0:T(8,128)(2,1)S(1)}, u32[]{:S(2)}, u32[]{:S(2)}) collective-permute-start(bf16[2,64,1024]{2,1,0:T(8,128)(2,1)} %bitcast.55), channel_id=1, source_target_pairs={{0,1},{8,9},{16,17},{24,25},{32,33},{40,41},{48,49},{56,57},{64,65... | collective-permute-start | bytes 786440 | tf_op jit(solution)/shard_map/ppermute | solution.py:58
  4.3 3.4 %copy-start.6 = (bf16[1,2,64,1024]{3,2,1,0:T(8,128)(2,1)S(1)}, bf16[1,2,64,1024]{3,2,1,0:T(8,128)(2,1)}, u32[]{:S(2)}) copy-start(bf16[1,2,64,1024]{3,2,1,0:T(8,128)(2,1)} %param.11) | copy-start | bytes 786436
  6.0 18.8 %collective-permute-start.1 = (bf16[1,64,1024]{2,1,0:T(8,128)(2,1)}, bf16[1,64,1024]{2,1,0:T(8,128)(2,1)S(1)}, u32[]{:S(2)}, u32[]{:S(2)}) collective-permute-start(bf16[1,64,1024]{2,1,0:T(8,128)(2,1)} %get-tuple-element.39), channel_id=1, source_target_pairs={{0,121},{8,17},{16,9},{24,33},{32,25},{40,49},{48,41},{56,65},{64,... | collective-permute-start | bytes 393224 | tf_op jit(solution)/shard_map/ppermute | solution.py:60
  7.7 2.9 %copy-start.3 = (bf16[1,2,64,1024]{3,2,1,0:T(8,128)(2,1)S(1)}, bf16[1,2,64,1024]{3,2,1,0:T(8,128)(2,1)}, u32[]{:S(2)}) copy-start(bf16[1,2,64,1024]{3,2,1,0:T(8,128)(2,1)} %param.12) | copy-start | bytes 786436
  7.7 22.1 %collective-permute-start.5 = (bf16[2,64,1024]{2,1,0:T(8,128)(2,1)S(1)}, bf16[2,64,1024]{2,1,0:T(8,128)(2,1)S(1)}, u32[]{:S(2)}, u32[]{:S(2)}) collective-permute-start(bf16[2,64,1024]{2,1,0:T(8,128)(2,1)S(1)} %bitcast.59), channel_id=1, source_target_pairs={{0,1},{8,9},{16,17},{24,25},{32,33},{40,41},{48,49},{56,57},{64,65... | collective-permute-start | bytes 786440 | tf_op jit(solution)/shard_map/ppermute | solution.py:58
  9.7 19.3 %collective-permute-start.6 = (bf16[1,64,1024]{2,1,0:T(8,128)(2,1)}, bf16[1,64,1024]{2,1,0:T(8,128)(2,1)S(1)}, u32[]{:S(2)}, u32[]{:S(2)}) collective-permute-start(bf16[1,64,1024]{2,1,0:T(8,128)(2,1)} %get-tuple-element.37), channel_id=1, source_target_pairs={{0,121},{8,17},{16,9},{24,33},{32,25},{40,49},{48,41},{56,65},{64,... | collective-permute-start | bytes 393224 | tf_op jit(solution)/shard_map/ppermute | solution.py:60
  10.7 26.4 %collective-permute-start.10 = (bf16[2,64,1024]{2,1,0:T(8,128)(2,1)S(1)}, bf16[2,64,1024]{2,1,0:T(8,128)(2,1)S(1)}, u32[]{:S(2)}, u32[]{:S(2)}) collective-permute-start(bf16[2,64,1024]{2,1,0:T(8,128)(2,1)S(1)} %bitcast.49), channel_id=1, source_target_pairs={{0,1},{8,9},{16,17},{24,25},{32,33},{40,41},{48,49},{56,57},{64,65... | collective-permute-start | bytes 786440 | tf_op jit(solution)/shard_map/ppermute | solution.py:58
  13.7 15.3 %copy-start.24 = (bf16[1,64,1024]{2,1,0:T(8,128)(2,1)}, bf16[1,64,1024]{2,1,0:T(8,128)(2,1)S(1)}, u32[]{:S(2)}) copy-start(bf16[1,64,1024]{2,1,0:T(8,128)(2,1)S(1)} %get-tuple-element.35) | copy-start | bytes 393220
  15.2 0.7 copy-start.26
  18.6 0.7 copy-start.27
  18.6 0.7 copy-start.29
  24.8 38.8 %collective-permute-start.3 = (bf16[1,64,1024]{2,1,0:T(8,128)(2,1)}, bf16[1,64,1024]{2,1,0:T(8,128)(2,1)S(1)}, u32[]{:S(2)}, u32[]{:S(2)}) collective-permute-start(bf16[1,64,1024]{2,1,0:T(8,128)(2,1)} %get-tuple-element.39), channel_id=1, source_target_pairs={{0,120},{8,16},{16,8},{24,32},{32,24},{40,48},{48,40},{56,64},{64,... | collective-permute-start | bytes 393224 | tf_op jit(solution)/shard_map/ppermute | solution.py:59
  27.0 6.4 %collective-permute-start.11 = (bf16[1,64,1024]{2,1,0:T(8,128)(2,1)S(1)}, bf16[1,64,1024]{2,1,0:T(8,128)(2,1)S(1)}, u32[]{:S(2)}, u32[]{:S(2)}) collective-permute-start(bf16[1,64,1024]{2,1,0:T(8,128)(2,1)S(1)} %get-tuple-element.35), channel_id=1, source_target_pairs={{0,121},{8,17},{16,9},{24,33},{32,25},{40,49},{48,41},{56,65},{64,... | collective-permute-start | bytes 393224 | tf_op jit(solution)/shard_map/ppermute | solution.py:60
  29.0 36.3 %collective-permute-start.8 = (bf16[1,64,1024]{2,1,0:T(8,128)(2,1)}, bf16[1,64,1024]{2,1,0:T(8,128)(2,1)S(1)}, u32[]{:S(2)}, u32[]{:S(2)}) collective-permute-start(bf16[1,64,1024]{2,1,0:T(8,128)(2,1)} %get-tuple-element.37), channel_id=1, source_target_pairs={{0,120},{8,16},{16,8},{24,32},{32,24},{40,48},{48,40},{56,64},{64,... | collective-permute-start | bytes 393224 | tf_op jit(solution)/shard_map/ppermute | solution.py:59
  29.8 10.6 %collective-permute-start.2 = (bf16[3,64,1024]{2,1,0:T(8,128)(2,1)S(1)}, bf16[3,64,1024]{2,1,0:T(8,128)(2,1)S(1)}, u32[]{:S(2)}, u32[]{:S(2)}) collective-permute-start(bf16[3,64,1024]{2,1,0:T(8,128)(2,1)S(1)} %pad_maximum_fusion.2), channel_id=1, source_target_pairs={{0,2},{8,10},{16,18},{24,26},{32,34},{40,42},{48,50},{56,58},{64,6... | collective-permute-start | bytes 1179656 | tf_op jit(solution)/shard_map/ppermute | solution.py:61
  33.5 14.8 %collective-permute-start.7 = (bf16[3,64,1024]{2,1,0:T(8,128)(2,1)S(1)}, bf16[3,64,1024]{2,1,0:T(8,128)(2,1)S(1)}, u32[]{:S(2)}, u32[]{:S(2)}) collective-permute-start(bf16[3,64,1024]{2,1,0:T(8,128)(2,1)S(1)} %pad_maximum_fusion.4), channel_id=1, source_target_pairs={{0,2},{8,10},{16,18},{24,26},{32,34},{40,42},{48,50},{56,58},{64,6... | collective-permute-start | bytes 1179656 | tf_op jit(solution)/shard_map/ppermute | solution.py:61
  37.1 19.2 %collective-permute-start.12 = (bf16[3,64,1024]{2,1,0:T(8,128)(2,1)S(1)}, bf16[3,64,1024]{2,1,0:T(8,128)(2,1)S(1)}, u32[]{:S(2)}, u32[]{:S(2)}) collective-permute-start(bf16[3,64,1024]{2,1,0:T(8,128)(2,1)S(1)} %pad_maximum_fusion.6), channel_id=1, source_target_pairs={{0,2},{8,10},{16,18},{24,26},{32,34},{40,42},{48,50},{56,58},{64,6... | collective-permute-start | bytes 1179656 | tf_op jit(solution)/shard_map/ppermute | solution.py:61
  40.4 1.0 copy-start.21
  40.4 29.7 %copy-start.7 = (bf16[3,64,1024]{2,1,0:T(8,128)(2,1)}, bf16[3,64,1024]{2,1,0:T(8,128)(2,1)S(1)}, u32[]{:S(2)}) copy-start(bf16[3,64,1024]{2,1,0:T(8,128)(2,1)S(1)} %collective-permute-done.2.rest_2_) | copy-start | bytes 1179652
  42.2 6.1 %copy-start.20 = (bf16[1,64,1024]{2,1,0:T(8,128)(2,1)S(1)}, bf16[1,64,1024]{2,1,0:T(8,128)(2,1)}, u32[]{:S(2)}) copy-start(bf16[1,64,1024]{2,1,0:T(8,128)(2,1)} %get-tuple-element.36) | copy-start | bytes 393220
  42.2 26.0 %collective-permute-start.4 = (bf16[3,64,1024]{2,1,0:T(8,128)(2,1)}, bf16[3,64,1024]{2,1,0:T(8,128)(2,1)}, u32[]{:S(2)}, u32[]{:S(2)}) collective-permute-start(bf16[3,64,1024]{2,1,0:T(8,128)(2,1)} %pad_maximum_fusion.3), channel_id=1, source_target_pairs={{0,8},{8,0},{16,24},{24,16},{32,40},{40,32},{48,56},{56,48},{64,72... | collective-permute-start | bytes 1179656 | tf_op jit(solution)/shard_map/ppermute | solution.py:63
  48.2 0.9 copy-start.9
  49.2 7.1 %copy-start.22 = (bf16[1,64,1024]{2,1,0:T(8,128)(2,1)S(1)}, bf16[1,64,1024]{2,1,0:T(8,128)(2,1)}, u32[]{:S(2)}) copy-start(bf16[1,64,1024]{2,1,0:T(8,128)(2,1)} %get-tuple-element.34) | copy-start | bytes 393220
  49.2 19.1 %collective-permute-start.9 = (bf16[3,64,1024]{2,1,0:T(8,128)(2,1)}, bf16[3,64,1024]{2,1,0:T(8,128)(2,1)}, u32[]{:S(2)}, u32[]{:S(2)}) collective-permute-start(bf16[3,64,1024]{2,1,0:T(8,128)(2,1)} %pad_maximum_fusion.5), channel_id=1, source_target_pairs={{0,8},{8,0},{16,24},{24,16},{32,40},{40,32},{48,56},{56,48},{64,72... | collective-permute-start | bytes 1179656 | tf_op jit(solution)/shard_map/ppermute | solution.py:63
  56.3 0.9 copy-start.12
  56.3 6.5 %copy-start.4 = (bf16[1,2,64,1024]{3,2,1,0:T(8,128)(2,1)S(1)}, bf16[1,2,64,1024]{3,2,1,0:T(8,128)(2,1)}, u32[]{:S(2)}) copy-start(bf16[1,2,64,1024]{3,2,1,0:T(8,128)(2,1)} %param.9) | copy-start | bytes 786436
  57.2 27.2 %collective-permute-start.14 = (bf16[3,64,1024]{2,1,0:T(8,128)(2,1)}, bf16[3,64,1024]{2,1,0:T(8,128)(2,1)}, u32[]{:S(2)}, u32[]{:S(2)}) collective-permute-start(bf16[3,64,1024]{2,1,0:T(8,128)(2,1)} %pad_maximum_fusion.7), channel_id=1, source_target_pairs={{0,8},{8,0},{16,24},{24,16},{32,40},{40,32},{48,56},{56,48},{64,72... | collective-permute-start | bytes 1179656 | tf_op jit(solution)/shard_map/ppermute | solution.py:63
  62.8 0.9 copy-start.25
  62.8 7.3 %copy-start.5 = (bf16[1,2,64,1024]{3,2,1,0:T(8,128)(2,1)S(1)}, bf16[1,2,64,1024]{3,2,1,0:T(8,128)(2,1)}, u32[]{:S(2)}) copy-start(bf16[1,2,64,1024]{3,2,1,0:T(8,128)(2,1)} %param.10) | copy-start | bytes 786436
  63.7 20.7 %copy-start.14 = (bf16[1,64,1024]{2,1,0:T(8,128)(2,1)}, bf16[1,64,1024]{2,1,0:T(8,128)(2,1)S(1)}, u32[]{:S(2)}) copy-start(bf16[1,64,1024]{2,1,0:T(8,128)(2,1)S(1)} %collective-permute-done.3.rest_3_) | copy-start | bytes 393220
  63.7 20.7 %collective-permute-start.13 = (bf16[1,64,1024]{2,1,0:T(8,128)(2,1)S(1)}, bf16[1,64,1024]{2,1,0:T(8,128)(2,1)S(1)}, u32[]{:S(2)}, u32[]{:S(2)}) collective-permute-start(bf16[1,64,1024]{2,1,0:T(8,128)(2,1)S(1)} %copy-done.25), channel_id=1, source_target_pairs={{0,120},{8,16},{16,8},{24,32},{32,24},{40,48},{48,40},{56,64},{64,... | collective-permute-start | bytes 393224 | tf_op jit(solution)/shard_map/ppermute | solution.py:59
  65.3 0.7 copy-start.16
  65.9 26.7 %collective-permute-start.16 = (bf16[1,64,1024]{2,1,0:T(8,128)(2,1)}, bf16[1,64,1024]{2,1,0:T(8,128)(2,1)S(1)}, u32[]{:S(2)}, u32[]{:S(2)}) collective-permute-start(bf16[1,64,1024]{2,1,0:T(8,128)(2,1)} %get-tuple-element.33), channel_id=1, source_target_pairs={{0,121},{8,17},{16,9},{24,33},{32,25},{40,49},{48,41},{56,65},{64,... | collective-permute-start | bytes 393224 | tf_op jit(solution)/shard_map/ppermute | solution.py:60
  68.2 61.9 %collective-permute-start.18 = (bf16[1,64,1024]{2,1,0:T(8,128)(2,1)}, bf16[1,64,1024]{2,1,0:T(8,128)(2,1)}, u32[]{:S(2)}, u32[]{:S(2)}) collective-permute-start(bf16[1,64,1024]{2,1,0:T(8,128)(2,1)} %get-tuple-element.33), channel_id=1, source_target_pairs={{0,120},{8,16},{16,8},{24,32},{32,24},{40,48},{48,40},{56,64},{64,... | collective-permute-start | bytes 393224 | tf_op jit(solution)/shard_map/ppermute | solution.py:59
  68.3 24.3 %collective-permute-start.15 = (bf16[2,64,1024]{2,1,0:T(8,128)(2,1)S(1)}, bf16[2,64,1024]{2,1,0:T(8,128)(2,1)S(1)}, u32[]{:S(2)}, u32[]{:S(2)}) collective-permute-start(bf16[2,64,1024]{2,1,0:T(8,128)(2,1)S(1)} %bitcast.51), channel_id=1, source_target_pairs={{0,1},{8,9},{16,17},{24,25},{32,33},{40,41},{48,49},{56,57},{64,65... | collective-permute-start | bytes 786440 | tf_op jit(solution)/shard_map/ppermute | solution.py:58
  70.1 1.0 copy-start.10
  71.1 0.9 copy-start.17
  72.0 12.4 %copy-start.13 = (bf16[3,64,1024]{2,1,0:T(8,128)(2,1)S(1)}, bf16[3,64,1024]{2,1,0:T(8,128)(2,1)}, u32[]{:S(2)}) copy-start(bf16[3,64,1024]{2,1,0:T(8,128)(2,1)} %copy-done.12) | copy-start | bytes 1179652
  88.8 13.4 %collective-permute-start.20 = (bf16[2,64,1152]{2,1,0:T(8,128)(2,1)S(1)}, bf16[2,64,1152]{2,1,0:T(8,128)(2,1)S(1)}, u32[]{:S(2)}, u32[]{:S(2)}) collective-permute-start(bf16[2,64,1152]{2,1,0:T(8,128)(2,1)S(1)} %get-tuple-element.26.grad_ref.rest_6_), channel_id=1, source_target_pairs={{0,1},{8,9},{16,17},{24,25},{32,33},{40,41},{48,49},{56,57},{64,65... | collective-permute-start | bytes 884744 | tf_op jit(solution)/shard_map/ppermute | solution.py:58
  90.8 1.4 copy-start.30
  90.8 1.4 %copy-start.28 = (pred[3,3]{0,1:T(4,128)(4,1)S(1)}, pred[3,3]{0,1:T(4,128)(4,1)}, u32[]{:S(2)}) copy-start(pred[3,3]{0,1:T(4,128)(4,1)} %copy-done.27) | copy-start | bytes 31
  90.8 11.5 %collective-permute-start.21 = (bf16[1,64,1152]{2,1,0:T(8,128)(2,1)}, bf16[1,64,1152]{2,1,0:T(8,128)(2,1)S(1)}, u32[]{:S(2)}, u32[]{:S(2)}) collective-permute-start(bf16[1,64,1152]{2,1,0:T(8,128)(2,1)} %get-tuple-element.31), channel_id=1, source_target_pairs={{0,121},{8,17},{16,9},{24,33},{32,25},{40,49},{48,41},{56,65},{64,... | collective-permute-start | bytes 442376 | tf_op jit(solution)/shard_map/ppermute | solution.py:60
  93.4 13.5 %collective-permute-start.17 = (bf16[3,64,1024]{2,1,0:T(8,128)(2,1)}, bf16[3,64,1024]{2,1,0:T(8,128)(2,1)}, u32[]{:S(2)}, u32[]{:S(2)}) collective-permute-start(bf16[3,64,1024]{2,1,0:T(8,128)(2,1)} %pad_maximum_fusion.8), channel_id=1, source_target_pairs={{0,2},{8,10},{16,18},{24,26},{32,34},{40,42},{48,50},{56,58},{64,6... | collective-permute-start | bytes 1179656 | tf_op jit(solution)/shard_map/ppermute | solution.py:61
  102.3 10.5 %copy-start.1 = (bf16[2,64,1152]{2,1,0:T(8,128)(2,1)}, bf16[2,64,1152]{2,1,0:T(8,128)(2,1)S(1)}, u32[]{:S(2)}) copy-start(bf16[2,64,1152]{2,1,0:T(8,128)(2,1)S(1)} %collective-permute-done.20.rest_7_) | copy-start | bytes 884740
  103.2 9.7 %collective-permute-start.22 = (bf16[3,64,1152]{2,1,0:T(8,128)(2,1)}, bf16[3,64,1152]{2,1,0:T(8,128)(2,1)S(1)}, u32[]{:S(2)}, u32[]{:S(2)}) collective-permute-start(bf16[3,64,1152]{2,1,0:T(8,128)(2,1)} %pad_maximum_fusion), channel_id=1, source_target_pairs={{0,2},{8,10},{16,18},{24,26},{32,34},{40,42},{48,50},{56,58},{64,6... | collective-permute-start | bytes 1327112 | tf_op jit(solution)/shard_map/ppermute | solution.py:61
  106.9 1.0 copy-start.23
  108.7 21.3 %collective-permute-start.19 = (bf16[3,64,1024]{2,1,0:T(8,128)(2,1)}, bf16[3,64,1024]{2,1,0:T(8,128)(2,1)}, u32[]{:S(2)}, u32[]{:S(2)}) collective-permute-start(bf16[3,64,1024]{2,1,0:T(8,128)(2,1)} %pad_maximum_fusion.9), channel_id=1, source_target_pairs={{0,8},{8,0},{16,24},{24,16},{32,40},{40,32},{48,56},{56,48},{64,72... | collective-permute-start | bytes 1179656 | tf_op jit(solution)/shard_map/ppermute | solution.py:63
  112.6 17.5 %collective-permute-start.23 = (bf16[1,64,1152]{2,1,0:T(8,128)(2,1)}, bf16[1,64,1152]{2,1,0:T(8,128)(2,1)}, u32[]{:S(2)}, u32[]{:S(2)}) collective-permute-start(bf16[1,64,1152]{2,1,0:T(8,128)(2,1)} %get-tuple-element.31), channel_id=1, source_target_pairs={{0,120},{8,16},{16,8},{24,32},{32,24},{40,48},{48,40},{56,64},{64,... | collective-permute-start | bytes 442376 | tf_op jit(solution)/shard_map/ppermute | solution.py:59
  112.8 0.9 copy-start.19
  112.8 5.0 %copy-start.18 = (bf16[1,64,1024]{2,1,0:T(8,128)(2,1)S(1)}, bf16[1,64,1024]{2,1,0:T(8,128)(2,1)}, u32[]{:S(2)}) copy-start(bf16[1,64,1024]{2,1,0:T(8,128)(2,1)} %copy-done.16) | copy-start | bytes 393220
  112.8 1.0 slice-start
  112.9 4.9 %copy-start.15 = (bf16[1,64,1024]{2,1,0:T(8,128)(2,1)S(1)}, bf16[1,64,1024]{2,1,0:T(8,128)(2,1)}, u32[]{:S(2)}) copy-start(bf16[1,64,1024]{2,1,0:T(8,128)(2,1)} %copy-done.14) | copy-start | bytes 393220
  113.8 4.0 %copy-start.8 = (bf16[3,64,1024]{2,1,0:T(8,128)(2,1)S(1)}, bf16[3,64,1024]{2,1,0:T(8,128)(2,1)}, u32[]{:S(2)}) copy-start(bf16[3,64,1024]{2,1,0:T(8,128)(2,1)} %copy-done.7) | copy-start | bytes 1179652
  113.8 4.0 %copy-start.11 = (bf16[3,64,1024]{2,1,0:T(8,128)(2,1)S(1)}, bf16[3,64,1024]{2,1,0:T(8,128)(2,1)}, u32[]{:S(2)}) copy-start(bf16[3,64,1024]{2,1,0:T(8,128)(2,1)} %copy-done.9) | copy-start | bytes 1179652
  113.9 16.2 %collective-permute-start.24 = (bf16[3,64,1152]{2,1,0:T(8,128)(2,1)S(1)}, bf16[3,64,1152]{2,1,0:T(8,128)(2,1)S(1)}, u32[]{:S(2)}, u32[]{:S(2)}) collective-permute-start(bf16[3,64,1152]{2,1,0:T(8,128)(2,1)S(1)} %pad_maximum_fusion.1), channel_id=1, source_target_pairs={{0,8},{8,0},{16,24},{24,16},{32,40},{40,32},{48,56},{56,48},{64,72... | collective-permute-start | bytes 1327112 | tf_op jit(solution)/shard_map/ppermute | solution.py:63
  117.8 12.3 %copy-start.2 = (bf16[2,64,1152]{2,1,0:T(8,128)(2,1)S(1)}, bf16[2,64,1152]{2,1,0:T(8,128)(2,1)}, u32[]{:S(2)}) copy-start(bf16[2,64,1152]{2,1,0:T(8,128)(2,1)} %copy-done.1) | copy-start | bytes 884740

commit v2 on v1

v2 whole, which is shorter than its diff:
```python
import functools

import jax
import jax.numpy as jnp
from jax import lax
from jax.experimental import pallas as pl
from jax.experimental.pallas import tpu as pltpu
from jax.sharding import PartitionSpec as P

HEADS = 16
HDIM = 64
PP = 64
WIDTH = HEADS * HDIM
GROUP = 4
GW = GROUP * HDIM
GROUPS = HEADS // GROUP
ROWS = GROUP * PP
WIN = 9 * PP
REG = 12 * PP
EXT = WIDTH + 128
NEG_FILL = -1e30
SCALE = HDIM ** -0.5
AXES = ("lon", "lat")
VMEM_LIMIT = 48 * 1024 * 1024
BF = jnp.bfloat16
F32 = jnp.float32

NT = (((1,), (1,)), ((), ()))
NN = (((1,), (0,)), ((), ()))


def dot(a, b, dims):
    return lax.dot_general(a, b, dims, preferred_element_type=F32)


def routes(rows, cols):
    def at(r, c):
        return (c % cols) * rows + r

    cells = [(r, c) for r in range(rows) for c in range(cols)]

    def away(c):
        return c + 1 if c % 2 else c - 1

    def hop(r):
        return r + 2 if r % 2 == 0 else r - 2

    return dict(
        swap=[(at(r, c), at(r ^ 1, c)) for r, c in cells],
        off=[(at(r, c), at(r, away(c))) for r, c in cells],
        cor=[(at(r, c), at(r ^ 1, away(c))) for r, c in cells],
        far=[(at(r, c), at(hop(r), c)) for r, c in cells if 0 <= hop(r) < rows],
        twin=[(at(r, c), at(r, c ^ 1)) for r, c in cells],
    )


def exchange(own, near, face_of, way):
    swap = lax.ppermute(own, AXES, way["swap"])
    off = lax.ppermute(near, AXES, way["off"])
    cor = lax.ppermute(near, AXES, way["cor"])
    far = lax.ppermute(jnp.concatenate([swap, cor], axis=0), AXES, way["far"])
    facing = jnp.concatenate([face_of(own), face_of(swap), face_of(far)], axis=0)
    twin = lax.ppermute(facing, AXES, way["twin"])
    return (own, swap, far, off, cor, twin)


def region_block(pieces, n, row, col, fs):
    own, swap, far, off, cor, twin = pieces
    if col == 0:
        ref, index = ((off, 0), (cor, 0), (far, 2))[row]
    elif col == 3:
        ref, index = twin, row
    else:
        ref, index = (own, swap, far)[row], n if col == 1 else 1 - n
    return ref[index, :, fs]


def window(pieces, n, t, fs):
    return jnp.concatenate(
        [region_block(pieces, n, row, col + t, fs) for row in range(3) for col in range(3)], axis=0
    )


def spread(x):
    lane = lax.broadcasted_iota(jnp.int32, x.shape, 1) // HDIM
    return jnp.concatenate([jnp.where(lane == h, x, jnp.zeros_like(x)) for h in range(GROUP)], axis=0)


def gather_heads(y):
    lane = lax.broadcasted_iota(jnp.int32, (PP, GW), 1) // HDIM
    out = y[0:PP]
    for h in range(1, GROUP):
        out = jnp.where(lane == h, y[h * PP : (h + 1) * PP], out)
    return out


def group_slice(g):
    return pl.ds(pl.multiple_of(g * GW, GW), GW)


def region_flags(here_ref, cloud_ref):
    rows, cols = cloud_ref.shape
    lat, lon = here_ref[0], here_ref[1]
    odd = lon % 2
    sign = 2 * odd - 1
    near = 2 * lon + odd
    outer = jnp.where(lat % 2 == 0, lat - 1, lat + 1)
    within = (outer >= 0) & (outer < rows)
    partner = jnp.where(lat % 2 == 0, lat + 1, lat - 1)
    lines = (lat, partner, jnp.clip(outer, 0, rows - 1))
    inside = (True, True, within)
    clear = []
    for row in range(3):
        line = []
        for col in range(4):
            c = (near + sign * (1 - col) + cols) % cols
            flag = cloud_ref[lines[row], c] == 1
            line.append(flag & within if row == 2 else flag)
        clear.append(line)
    return odd, inside, clear


def segments(flags, fill):
    width = PP * len(flags)
    slot = lax.broadcasted_iota(jnp.int32, (1, width), 1) // PP
    out = jnp.zeros((1, width), F32)
    for i, flag in enumerate(flags):
        if flag is not True:
            value = fill if flag is False else jnp.where(flag, 0.0, fill)
            out = jnp.where(slot == i, value, out)
    return out


def query_flags(clear, t):
    return [
        True if (row, col) == (0, 1) else clear[row][col + t] for row in range(3) for col in range(3)
    ]


def attend_kernel(here_ref, cloud_ref, q_ref, *rest):
    k_pieces, v_pieces = rest[0:6], rest[6:12]
    att_ref, stat_ref = rest[12:]
    n, _, clear = region_flags(here_ref, cloud_ref)
    for t in range(2):
        qt = n if t == 0 else 1 - n
        stat_ref[t] = jnp.zeros((PP, 128), F32)
        mask = segments(query_flags(clear, t), NEG_FILL)

        def step(g, carry):
            fs = group_slice(g)
            q = spread(q_ref[qt, :, fs] * SCALE)
            kw = window(k_pieces, n, t, fs)
            s = dot(q, kw, NT) + mask
            m = jnp.max(s, axis=1, keepdims=True)
            e = jnp.exp(s - m)
            total = jnp.sum(e, axis=1, keepdims=True)
            p = (e * (1.0 / total)).astype(BF)
            lse = m + jnp.log(total)
            att_ref[t, :, fs] = gather_heads(dot(p, window(v_pieces, n, t, fs), NN)).astype(BF)
            lane = lax.broadcasted_iota(jnp.int32, (PP, 128), 1)
            stat = stat_ref[t]
            for h in range(GROUP):
                stat = jnp.where(lane == g * GROUP + h, lse[h * PP : (h + 1) * PP], stat)
            stat_ref[t] = stat
            return carry

        lax.fori_loop(0, GROUPS, step, 0, unroll=True)


def contrast_kernel(here_ref, cloud_ref, att_ref, stat_ref, pair_ref, *rest):
    pieces = rest[0:6]
    loss_ref, grad_ref, stats_ref = rest[6:]
    n, _, clear = region_flags(here_ref, cloud_ref)
    whole = slice(0, WIDTH)
    season = jnp.concatenate(
        [region_block(pieces, n, row, col, whole) for row in range(3) for col in range(4)], axis=0
    )
    att = jnp.concatenate([att_ref[0], att_ref[1]], axis=0)
    side = lax.broadcasted_iota(jnp.int32, (2 * PP, REG), 0) < PP
    sides = []
    for t in range(2):
        flags = query_flags(clear, t)
        line = []
        for row in range(3):
            mine = flags[row * 3 : row * 3 + 3]
            line += mine + [False] if t == 0 else [False] + mine
        sides.append(segments(line, NEG_FILL))
    mask = jnp.where(side, sides[0], sides[1])
    logits = dot(att, season, NT) + mask
    m = jnp.max(logits, axis=1, keepdims=True)
    e = jnp.exp(logits - m)
    total = jnp.sum(e, axis=1, keepdims=True)
    w = (e * (1.0 / total)).astype(BF)
    ctotal = m + jnp.log(total)
    key = lax.broadcasted_iota(jnp.int32, (4 * PP, PP), 0)
    hits = []
    for t in range(2):
        pair = pair_ref[pl.ds(n if t == 0 else 1 - n, 1), :]
        hits.append((key == pair + (1 + t) * PP).astype(F32))
    hit = jnp.transpose(jnp.concatenate(hits, axis=1)) > 0.5
    chosen = jnp.sum(jnp.where(hit, logits[:, 0 : 4 * PP], 0.0), axis=1, keepdims=True)
    loss = jnp.transpose(jnp.broadcast_to(ctotal - chosen, (2 * PP, 128)))
    for t in range(2):
        loss_ref[pl.ds(n if t == 0 else 1 - n, 1), :] = loss[0:1, t * PP : (t + 1) * PP]
    acc = dot(w, season, NN) - dot(hit.astype(F32).astype(BF), season[0 : 4 * PP], NN)
    grad = acc.astype(BF)
    prod = grad.astype(F32) * att.astype(F32)
    high = prod.astype(BF)
    low = (prod - high.astype(F32)).astype(BF)
    feat = lax.broadcasted_iota(jnp.int32, (WIDTH, 128), 0) // HDIM
    lane = lax.broadcasted_iota(jnp.int32, (WIDTH, 128), 1)
    pick = (lane == feat + HEADS).astype(F32).astype(BF)
    delta = dot(high, pick, NN) + dot(low, pick, NN)
    stat = jnp.concatenate([stat_ref[0], stat_ref[1]], axis=0) + delta
    part0 = stat.astype(BF).astype(F32)
    part1 = (stat - part0).astype(BF).astype(F32)
    part2 = (stat - part0 - part1).astype(BF).astype(F32)
    packed = part0 + pltpu.roll(part1, 32, 1) + pltpu.roll(part2, 64, 1)
    packed = packed.astype(BF)
    for t in range(2):
        rows = slice(t * PP, (t + 1) * PP)
        grad_ref[t, :, 0:WIDTH] = grad[rows]
        grad_ref[t, :, WIDTH:EXT] = packed[rows]
        stats_ref[t] = stat[rows]


def head_column(stat, index):
    lane = lax.broadcasted_iota(jnp.int32, (PP, 128), 1)
    cols = [
        jnp.sum(jnp.where(lane == index + h, stat, 0.0), axis=1, keepdims=True) for h in range(GROUP)
    ]
    return jnp.concatenate(cols, axis=0)


def query_kernel(here_ref, cloud_ref, q_ref, grad_ref, stats_ref, *rest):
    k_pieces, v_pieces = rest[0:6], rest[6:12]
    out_ref = rest[12]
    n, _, clear = region_flags(here_ref, cloud_ref)
    for t in range(2):
        qt = n if t == 0 else 1 - n
        mask = segments(query_flags(clear, t), NEG_FILL)

        def step(g, carry):
            fs = group_slice(g)
            q = spread(q_ref[qt, :, fs] * SCALE)
            stat = stats_ref[t]
            lse = head_column(stat, g * GROUP)
            delta = head_column(stat, g * GROUP + HEADS)
            kw = window(k_pieces, n, t, fs)
            s = dot(q, kw, NT) + mask
            p = jnp.exp(s - lse)
            gd = dot(spread(grad_ref[t, :, fs]), window(v_pieces, n, t, fs), NT)
            ds = (p * (gd - delta)).astype(BF)
            out = gather_heads(dot(ds, kw, NN)) * SCALE
            out_ref[qt, :, fs] = out.astype(BF)
            return carry

        lax.fori_loop(0, GROUPS, step, 0, unroll=True)


def key_kernel(here_ref, cloud_ref, k_ref, v_ref, *rest):
    q_pieces, g_pieces = rest[0:6], rest[6:12]
    kout_ref, vout_ref, rows_ref = rest[12:]
    n, inside, clear = region_flags(here_ref, cloud_ref)
    for t in range(2):
        kt = n if t == 0 else 1 - n
        parts = jnp.transpose(window(g_pieces, 0, t, slice(WIDTH, EXT)).astype(F32))
        stats = parts[0:32] + parts[32:64] + parts[64:96]
        seen = clear[0][1 + t]
        flags = [
            True if (row, col) == (0, 1) else (seen & inside[2] if row == 2 else seen)
            for row in range(3)
            for col in range(3)
        ]
        rows_ref[0:HEADS] = stats[0:HEADS] + segments(flags, -NEG_FILL)
        rows_ref[HEADS : 2 * HEADS] = stats[HEADS : 2 * HEADS]

        def step(g, carry):
            fs = group_slice(g)
            ks = spread(k_ref[kt, :, fs] * SCALE)
            vs = spread(v_ref[kt, :, fs])
            qw = window(q_pieces, n, t, fs)
            gw = window(g_pieces, 0, t, fs)
            s = dot(ks, qw, NT)
            gd = dot(vs, gw, NT)
            ps, dss = [], []
            for h in range(GROUP):
                part = slice(h * PP, (h + 1) * PP)
                lse = rows_ref[pl.ds(g * GROUP + h, 1), :]
                delta = rows_ref[pl.ds(HEADS + g * GROUP + h, 1), :]
                p = jnp.exp(s[part] - lse)
                ps.append(p.astype(BF))
                dss.append((p * (gd[part] - delta)).astype(BF))
            p = jnp.concatenate(ps, axis=0)
            ds = jnp.concatenate(dss, axis=0)
            kout_ref[kt, :, fs] = (gather_heads(dot(ds, qw, NN)) * SCALE).astype(BF)
            vout_ref[kt, :, fs] = gather_heads(dot(p, gw, NN)).astype(BF)
            return carry

        lax.fori_loop(0, GROUPS, step, 0, unroll=True)


SMEM = pl.BlockSpec(memory_space=pltpu.SMEM)
VMEM = pl.BlockSpec(memory_space=pltpu.VMEM)


def call(kernel, name, in_specs, out_shape, scratch, flops):
    return pl.pallas_call(
        kernel,
        name=name,
        out_shape=out_shape,
        in_specs=in_specs,
        out_specs=jax.tree.map(lambda _: VMEM, out_shape),
        scratch_shapes=scratch,
        compiler_params=pltpu.CompilerParams(vmem_limit_bytes=VMEM_LIMIT),
        cost_estimate=pl.CostEstimate(flops=flops, bytes_accessed=6_000_000, transcendentals=0),
    )


def shape(dims, dtype):
    return jax.ShapeDtypeStruct(dims, dtype)


def body(way, queries, keys, values, season, cloud, pairing):
    lat = lax.axis_index("lat")
    lon = lax.axis_index("lon")
    odd = lon % 2
    q, k, v, s = (x[0] for x in (queries, keys, values, season))

    def near_of(x):
        return lax.dynamic_slice_in_dim(x, odd, 1, axis=0)

    def face_of(x):
        return lax.dynamic_slice_in_dim(x, 1 - odd, 1, axis=0)

    here = jnp.stack([lat, lon]).astype(jnp.int32)

    kp = exchange(k, near_of(k), face_of, way)
    vp = exchange(v, near_of(v), face_of, way)
    sp = exchange(s, near_of(s), face_of, way)
    qp = exchange(q, near_of(q), face_of, way)

    att, stat = call(
        attend_kernel,
        "attend",
        [SMEM, SMEM, VMEM] + [VMEM] * 12,
        (shape((2, PP, WIDTH), BF), shape((2, PP, 128), F32)),
        [],
        2_400_000_000,
    )(here, cloud, q, *kp, *vp)

    loss, grad, stats = call(
        contrast_kernel,
        "contrast",
        [SMEM, SMEM, VMEM, VMEM, VMEM] + [VMEM] * 6,
        (shape((2, PP), F32), shape((2, PP, EXT), BF), shape((2, PP, 128), F32)),
        [],
        1_200_000_000,
    )(here, cloud, att, stat, pairing[0], *sp)

    gp = exchange(grad, grad[0:1], lambda x: x[1:2], way)

    query_grad = call(
        query_kernel,
        "query_grads",
        [SMEM, SMEM, VMEM, VMEM, VMEM] + [VMEM] * 12,
        shape((2, PP, WIDTH), BF),
        [],
        3_600_000_000,
    )(here, cloud, q, grad, stats, *kp, *vp)

    key_grad, value_grad = call(
        key_kernel,
        "key_grads",
        [SMEM, SMEM, VMEM, VMEM] + [VMEM] * 12,
        (shape((2, PP, WIDTH), BF), shape((2, PP, WIDTH), BF)),
        [pltpu.VMEM((2 * HEADS, WIN), F32)],
        4_800_000_000,
    )(here, cloud, k, v, *qp, *gp)

    return (loss[None], query_grad[None], key_grad[None], value_grad[None])


def solution(mesh):
    block = P("lat", "lon", None, None)
    line = P("lat", "lon", None)
    way = routes(mesh.shape["lat"], mesh.shape["lon"])
    return jax.shard_map(
        functools.partial(body, way),
        mesh=mesh,
        in_specs=(block, block, block, block, P(), line),
        out_specs=(line, block, block, block),
        check_vma=False,
    )
```

time: 144 us -> 119 us (0.83)
  the two profiles are of different devices: /device:TPU:1 before, /device:TPU:75 now
where the time goes in v2:
time: 119 us
  waiting for transfers between devices  55.3 us (46%)
  starting transfers between devices  43.5 us (37%)
  Pallas kernels  15.7 us (13%)
  local copies, waits for them, and re-layouts  2.65 us (2%)
    ppermute x5, waiting for transfers between devices, exchange(): far = lax.ppermute(jnp.concatenate([swap, cor], axis=0), AXES, way['far'])  31.9 us
    ppermute x5, waiting for transfers between devices, exchange(): cor = lax.ppermute(near, AXES, way['cor'])  21.3 us
    ppermute x5, starting transfers between devices, exchange(): far = lax.ppermute(jnp.concatenate([swap, cor], axis=0), AXES, way['far'])  13.1 us
    ppermute x5, starting transfers between devices, exchange(): off = lax.ppermute(near, AXES, way['off'])  11.9 us
    ppermute x5, starting transfers between devices, exchange(): swap = lax.ppermute(own, AXES, way['swap'])  11.4 us
    ppermute x5, starting transfers between devices, exchange(): cor = lax.ppermute(near, AXES, way['cor'])  6.18 us
    pallas_call x1, Pallas kernels, body(): call(key_kernel, 'key_grads', [SMEM, SMEM, VMEM, VMEM] + [VMEM] * 12, (sh...  4.94 us
    pallas_call x1, Pallas kernels, body(): call(query_kernel, 'query_grads', [SMEM, SMEM, VMEM, VMEM, VMEM] + [VMEM]...  4.45 us
  transfers between devices with their start and end apart: 25, of which 7 were waited for; matrix products, arithmetic and copies ran while one was open for 1% of the time, Pallas kernels for 9%

profile of v2, /device:TPU:75, one launch (start us, length us, event | category | flops | bytes accessed | tf_op | source)
XLA Modules:
  0.0 118.7 jit_solution(2587100245211035593)
XLA Ops:
  0.6 1.9 %collective-permute-start = (bf16[2,64,1024]{2,1,0:T(8,128)(2,1)}, bf16[2,64,1024]{2,1,0:T(8,128)(2,1)S(1)}, u32[]{:S(2)}, u32[]{:S(2)}) collective-permute-start(bf16[2,64,1024]{2,1,0:T(8,128)(2,1)} %bitcast.33), channel_id=1, source_target_pairs={{0,1},{8,9},{16,17},{24,25},{32,33},{40,41},{48,49},{56,57},{64,65... | collective-permute-start | bytes 786440 | tf_op jit(solution)/shard_map/ppermute | solution.py:58
  2.6 1.0 dynamic-slice_bitcast_fusion.6
  3.6 1.5 %collective-permute-start.1 = (bf16[1,64,1024]{2,1,0:T(8,128)(2,1)S(1)}, bf16[1,64,1024]{2,1,0:T(8,128)(2,1)S(1)}, u32[]{:S(2)}, u32[]{:S(2)}) collective-permute-start(bf16[1,64,1024]{2,1,0:T(8,128)(2,1)S(1)} %get-tuple-element.27), channel_id=1, source_target_pairs={{0,121},{8,17},{16,9},{24,33},{32,25},{40,49},{48,41},{56,65},{64,... | collective-permute-start | bytes 393224 | tf_op jit(solution)/shard_map/ppermute | solution.py:60
  5.1 3.3 %collective-permute-start.5 = (bf16[2,64,1024]{2,1,0:T(8,128)(2,1)S(1)}, bf16[2,64,1024]{2,1,0:T(8,128)(2,1)S(1)}, u32[]{:S(2)}, u32[]{:S(2)}) collective-permute-start(bf16[2,64,1024]{2,1,0:T(8,128)(2,1)S(1)} %bitcast.37), channel_id=1, source_target_pairs={{0,1},{8,9},{16,17},{24,25},{32,33},{40,41},{48,49},{56,57},{64,65... | collective-permute-start | bytes 786440 | tf_op jit(solution)/shard_map/ppermute | solution.py:58
  8.5 0.1 collective-permute-start.6
  8.6 1.7 %collective-permute-start.10 = (bf16[2,64,1024]{2,1,0:T(8,128)(2,1)S(1)}, bf16[2,64,1024]{2,1,0:T(8,128)(2,1)S(1)}, u32[]{:S(2)}, u32[]{:S(2)}) collective-permute-start(bf16[2,64,1024]{2,1,0:T(8,128)(2,1)S(1)} %bitcast.27), channel_id=1, source_target_pairs={{0,1},{8,9},{16,17},{24,25},{32,33},{40,41},{48,49},{56,57},{64,65... | collective-permute-start | bytes 786440 | tf_op jit(solution)/shard_map/ppermute | solution.py:58
  10.3 15.2 %collective-permute-done.1.rest_4_ = bf16[1,64,1024]{2,1,0:T(8,128)(2,1)S(1)} collective-permute-done((bf16[1,64,1024]{2,1,0:T(8,128)(2,1)S(1)}, bf16[1,64,1024]{2,1,0:T(8,128)(2,1)S(1)}, u32[]{:S(2)}, u32[]{:S(2)}) %collective-permute-start.1) | collective-permute-done | bytes 131104 | tf_op jit(solution)/shard_map/ppermute | solution.py:60
  25.5 0.8 collective-permute-start.3
  26.3 0.0 collective-permute-done.rest_1_
  26.3 2.5 %collective-permute-start.11 = (bf16[1,64,1024]{2,1,0:T(8,128)(2,1)S(1)}, bf16[1,64,1024]{2,1,0:T(8,128)(2,1)S(1)}, u32[]{:S(2)}, u32[]{:S(2)}) collective-permute-start(bf16[1,64,1024]{2,1,0:T(8,128)(2,1)S(1)} %get-tuple-element.23), channel_id=1, source_target_pairs={{0,121},{8,17},{16,9},{24,33},{32,25},{40,49},{48,41},{56,65},{64,... | collective-permute-start | bytes 393224 | tf_op jit(solution)/shard_map/ppermute | solution.py:60
  28.8 0.0 collective-permute-done.6.rest_10_
  28.8 1.7 %collective-permute-start.8 = (bf16[1,64,1024]{2,1,0:T(8,128)(2,1)S(1)}, bf16[1,64,1024]{2,1,0:T(8,128)(2,1)S(1)}, u32[]{:S(2)}, u32[]{:S(2)}) collective-permute-start(bf16[1,64,1024]{2,1,0:T(8,128)(2,1)S(1)} %get-tuple-element.25), channel_id=1, source_target_pairs={{0,120},{8,16},{16,8},{24,32},{32,24},{40,48},{48,40},{56,64},{64,... | collective-permute-start | bytes 393224 | tf_op jit(solution)/shard_map/ppermute | solution.py:59
  30.6 0.0 collective-permute-done.5.rest_7_
  30.6 3.2 %collective-permute-start.2 = (bf16[3,64,1024]{2,1,0:T(8,128)(2,1)S(1)}, bf16[3,64,1024]{2,1,0:T(8,128)(2,1)S(1)}, u32[]{:S(2)}, u32[]{:S(2)}) collective-permute-start(bf16[3,64,1024]{2,1,0:T(8,128)(2,1)S(1)} %pad_maximum_fusion.2), channel_id=1, source_target_pairs={{0,2},{8,10},{16,18},{24,26},{32,34},{40,42},{48,50},{56,58},{64,6... | collective-permute-start | bytes 1179656 | tf_op jit(solution)/shard_map/ppermute | solution.py:61
  33.9 0.0 collective-permute-done.11.rest_4_
  33.9 1.9 %collective-permute-start.7 = (bf16[3,64,1024]{2,1,0:T(8,128)(2,1)S(1)}, bf16[3,64,1024]{2,1,0:T(8,128)(2,1)S(1)}, u32[]{:S(2)}, u32[]{:S(2)}) collective-permute-start(bf16[3,64,1024]{2,1,0:T(8,128)(2,1)S(1)} %pad_maximum_fusion.4), channel_id=1, source_target_pairs={{0,2},{8,10},{16,18},{24,26},{32,34},{40,42},{48,50},{56,58},{64,6... | collective-permute-start | bytes 1179656 | tf_op jit(solution)/shard_map/ppermute | solution.py:61
  35.8 0.0 collective-permute-done.10.rest_1_
  35.9 1.9 %collective-permute-start.12 = (bf16[3,64,1024]{2,1,0:T(8,128)(2,1)S(1)}, bf16[3,64,1024]{2,1,0:T(8,128)(2,1)S(1)}, u32[]{:S(2)}, u32[]{:S(2)}) collective-permute-start(bf16[3,64,1024]{2,1,0:T(8,128)(2,1)S(1)} %pad_maximum_fusion.6), channel_id=1, source_target_pairs={{0,2},{8,10},{16,18},{24,26},{32,34},{40,42},{48,50},{56,58},{64,6... | collective-permute-start | bytes 1179656 | tf_op jit(solution)/shard_map/ppermute | solution.py:61
  37.9 5.8 %collective-permute-done.2.rest_2_ = bf16[3,64,1024]{2,1,0:T(8,128)(2,1)S(1)} collective-permute-done((bf16[3,64,1024]{2,1,0:T(8,128)(2,1)S(1)}, bf16[3,64,1024]{2,1,0:T(8,128)(2,1)S(1)}, u32[]{:S(2)}, u32[]{:S(2)}) %collective-permute-start.2) | collective-permute-done | bytes 393248 | tf_op jit(solution)/shard_map/ppermute | solution.py:61
  43.7 0.1 collective-permute-start.4
  43.8 8.3 %collective-permute-done.7.rest_8_ = bf16[3,64,1024]{2,1,0:T(8,128)(2,1)S(1)} collective-permute-done((bf16[3,64,1024]{2,1,0:T(8,128)(2,1)S(1)}, bf16[3,64,1024]{2,1,0:T(8,128)(2,1)S(1)}, u32[]{:S(2)}, u32[]{:S(2)}) %collective-permute-start.7) | collective-permute-done | bytes 393248 | tf_op jit(solution)/shard_map/ppermute | solution.py:61
  52.1 0.1 collective-permute-start.9
  52.2 6.7 %collective-permute-done.12.rest_2_ = bf16[3,64,1024]{2,1,0:T(8,128)(2,1)S(1)} collective-permute-done((bf16[3,64,1024]{2,1,0:T(8,128)(2,1)S(1)}, bf16[3,64,1024]{2,1,0:T(8,128)(2,1)S(1)}, u32[]{:S(2)}, u32[]{:S(2)}) %collective-permute-start.12) | collective-permute-done | bytes 393248 | tf_op jit(solution)/shard_map/ppermute | solution.py:61
  58.9 0.0 copy-start.3
  59.0 0.1 collective-permute-start.14
  59.1 0.1 pad_add_fusion.here_ref
  59.2 0.7 copy-done.3
  59.9 0.0 collective-permute-done.3.rest_3_
  59.9 1.7 %collective-permute-start.13 = (bf16[1,64,1024]{2,1,0:T(8,128)(2,1)S(1)}, bf16[1,64,1024]{2,1,0:T(8,128)(2,1)S(1)}, u32[]{:S(2)}, u32[]{:S(2)}) collective-permute-start(bf16[1,64,1024]{2,1,0:T(8,128)(2,1)S(1)} %get-tuple-element.23), channel_id=1, source_target_pairs={{0,120},{8,16},{16,8},{24,32},{32,24},{40,48},{48,40},{56,64},{64,... | collective-permute-start | bytes 393224 | tf_op jit(solution)/shard_map/ppermute | solution.py:59
  61.6 0.0 collective-permute-done.8.rest_9_
  61.6 1.8 %collective-permute-start.15 = (bf16[2,64,1024]{2,1,0:T(8,128)(2,1)S(1)}, bf16[2,64,1024]{2,1,0:T(8,128)(2,1)S(1)}, u32[]{:S(2)}, u32[]{:S(2)}) collective-permute-start(bf16[2,64,1024]{2,1,0:T(8,128)(2,1)S(1)} %bitcast.29), channel_id=1, source_target_pairs={{0,1},{8,9},{16,17},{24,25},{32,33},{40,41},{48,49},{56,57},{64,65... | collective-permute-start | bytes 786440 | tf_op jit(solution)/shard_map/ppermute | solution.py:58
  63.5 0.0 collective-permute-done.4.rest_5_
  63.5 0.6 collective-permute-start.16
  64.1 0.0 collective-permute-done.9.rest_11_
  64.1 0.0 copy-done.6
  64.1 3.4 %attend.1 = (bf16[2,64,1024]{2,1,0:T(8,128)(2,1)S(1)}, f32[2,64,128]{2,1,0:T(8,128)S(1)}) custom-call(s32[2]{0:T(128)S(1)} %pad_add_fusion.here_ref, s32[8,32]{1,0:T(8,128)S(1)} %copy-done.6, bf16[2,64,1024]{2,1,0:T(8,128)(2,1)S(1)} %bitcast.30, bf16[2,64,1024]{2,1,0:T(8,128)(2,1)S(1)} %bitcast.34, bf16[2,64,1024]{2,1,0:T(8,128)(2,1)S(1)} %collective-permute-done.rest_1_, ...), custom_call_target="tpu_custom_call" | custom-call | flops 2400000000 | bytes 6000000 | tf_op jit(solution)/shard_map/attend/pallas_call | solution.py:343
  67.5 0.0 collective-permute-done.13.rest_3_
  67.5 0.0 collective-permute-done.14.rest_5_
  67.5 0.0 copy-start.7
  67.5 0.7 copy-done.7
  68.2 2.9 %contrast.1 = (f32[2,64]{1,0:T(2,128)}, bf16[2,64,1152]{2,1,0:T(8,128)(2,1)S(1)}, f32[2,64,128]{2,1,0:T(8,128)S(1)}) custom-call(s32[2]{0:T(128)S(1)} %pad_add_fusion.here_ref, s32[8,32]{1,0:T(8,128)S(1)} %copy-done.6, bf16[2,64,1024]{2,1,0:T(8,128)(2,1)S(1)} %get-tuple-element.11.att_ref, f32[2,64,128]{2,1,0:T(8,128)S(1)} %get-tuple-element.12.stat_ref, ...), custom_call_target="tpu_custom_call" | custom-call | flops 1200000000 | bytes 6000000 | tf_op jit(solution)/shard_map/contrast/pallas_call | solution.py:352
  71.1 2.6 %collective-permute-start.20 = (bf16[2,64,1152]{2,1,0:T(8,128)(2,1)S(1)}, bf16[2,64,1152]{2,1,0:T(8,128)(2,1)S(1)}, u32[]{:S(2)}, u32[]{:S(2)}) collective-permute-start(bf16[2,64,1152]{2,1,0:T(8,128)(2,1)S(1)} %get-tuple-element.14.grad_ref.rest_6_), channel_id=1, source_target_pairs={{0,1},{8,9},{16,17},{24,25},{32,33},{40,41},{48,49},{56,57},{64,65... | collective-permute-start | bytes 884744 | tf_op jit(solution)/shard_map/ppermute | solution.py:58
  73.8 1.5 %collective-permute-start.21 = (bf16[1,64,1152]{2,1,0:T(8,128)(2,1)S(1)}, bf16[1,64,1152]{2,1,0:T(8,128)(2,1)S(1)}, u32[]{:S(2)}, u32[]{:S(2)}) collective-permute-start(bf16[1,64,1152]{2,1,0:T(8,128)(2,1)S(1)} %get-tuple-element.19), channel_id=1, source_target_pairs={{0,121},{8,17},{16,9},{24,33},{32,25},{40,49},{48,41},{56,65},{64,... | collective-permute-start | bytes 442376 | tf_op jit(solution)/shard_map/ppermute | solution.py:60
  75.2 0.0 collective-permute-done.16.rest_4_
  75.2 0.0 collective-permute-done.15.rest_1_
  75.3 3.3 %collective-permute-start.17 = (bf16[3,64,1024]{2,1,0:T(8,128)(2,1)S(1)}, bf16[3,64,1024]{2,1,0:T(8,128)(2,1)S(1)}, u32[]{:S(2)}, u32[]{:S(2)}) collective-permute-start(bf16[3,64,1024]{2,1,0:T(8,128)(2,1)S(1)} %pad_maximum_fusion.8), channel_id=1, source_target_pairs={{0,2},{8,10},{16,18},{24,26},{32,34},{40,42},{48,50},{56,58},{64,6... | collective-permute-start | bytes 1179656 | tf_op jit(solution)/shard_map/ppermute | solution.py:61
  78.5 6.1 %collective-permute-done.21.rest_10_ = bf16[1,64,1152]{2,1,0:T(8,128)(2,1)S(1)} collective-permute-done((bf16[1,64,1152]{2,1,0:T(8,128)(2,1)S(1)}, bf16[1,64,1152]{2,1,0:T(8,128)(2,1)S(1)}, u32[]{:S(2)}, u32[]{:S(2)}) %collective-permute-start.21) | collective-permute-done | bytes 147488 | tf_op jit(solution)/shard_map/ppermute | solution.py:60
  84.6 0.0 collective-permute-done.20.rest_7_
  84.7 2.8 %collective-permute-start.22 = (bf16[3,64,1152]{2,1,0:T(8,128)(2,1)S(1)}, bf16[3,64,1152]{2,1,0:T(8,128)(2,1)S(1)}, u32[]{:S(2)}, u32[]{:S(2)}) collective-permute-start(bf16[3,64,1152]{2,1,0:T(8,128)(2,1)S(1)} %pad_maximum_fusion), channel_id=1, source_target_pairs={{0,2},{8,10},{16,18},{24,26},{32,34},{40,42},{48,50},{56,58},{64,6... | collective-permute-start | bytes 1327112 | tf_op jit(solution)/shard_map/ppermute | solution.py:61
  87.5 0.0 collective-permute-done.17.rest_2_
  87.5 0.0 copy-done
  87.5 0.0 slice-start
  87.5 11.2 %collective-permute-done.22.rest_8_ = bf16[3,64,1152]{2,1,0:T(8,128)(2,1)S(1)} collective-permute-done((bf16[3,64,1152]{2,1,0:T(8,128)(2,1)S(1)}, bf16[3,64,1152]{2,1,0:T(8,128)(2,1)S(1)}, u32[]{:S(2)}, u32[]{:S(2)}) %collective-permute-start.22) | collective-permute-done | bytes 442400 | tf_op jit(solution)/shard_map/ppermute | solution.py:61
  98.8 0.1 pad_maximum_fusion.1
  98.8 0.5 collective-permute-start.24
  99.4 0.2 collective-permute-start.19
  99.6 7.5 %collective-permute-start.18 = (bf16[1,64,1024]{2,1,0:T(8,128)(2,1)S(1)}, bf16[1,64,1024]{2,1,0:T(8,128)(2,1)S(1)}, u32[]{:S(2)}, u32[]{:S(2)}) collective-permute-start(bf16[1,64,1024]{2,1,0:T(8,128)(2,1)S(1)} %get-tuple-element.21), channel_id=1, source_target_pairs={{0,120},{8,16},{16,8},{24,32},{32,24},{40,48},{48,40},{56,64},{64,... | collective-permute-start | bytes 393224 | tf_op jit(solution)/shard_map/ppermute | solution.py:59
  107.1 0.0 collective-permute-start.23
  107.1 4.4 %query_grads.1 = bf16[2,64,1024]{2,1,0:T(8,128)(2,1)} custom-call(s32[2]{0:T(128)S(1)} %pad_add_fusion.here_ref, s32[8,32]{1,0:T(8,128)S(1)} %copy-done.6, bf16[2,64,1024]{2,1,0:T(8,128)(2,1)S(1)} %bitcast.31, bf16[2,64,1152]{2,1,0:T(8,128)(2,1)S(1)} %get-tuple-element.14.grad_ref.rest_6_, f32[2,64,128]{2,1,0:T(8,128)S(1)} %get-tuple-element.15.stats_ref, ...), custom_call_target="tpu_custom_call" | custom-call | flops 3600000000 | bytes 6000000 | tf_op jit(solution)/shard_map/query_grads/pallas_call | solution.py:363
  111.6 0.0 collective-permute-done.18.rest_3_
  111.6 0.0 collective-permute-done.19.rest_5_
  111.6 2.1 %collective-permute-done.23.rest_9_ = bf16[1,64,1152]{2,1,0:T(8,128)(2,1)S(1)} collective-permute-done((bf16[1,64,1152]{2,1,0:T(8,128)(2,1)S(1)}, bf16[1,64,1152]{2,1,0:T(8,128)(2,1)S(1)}, u32[]{:S(2)}, u32[]{:S(2)}) %collective-permute-start.23) | collective-permute-done | bytes 147488 | tf_op jit(solution)/shard_map/ppermute | solution.py:59
  113.7 0.0 collective-permute-done.24.rest_11_
  113.7 4.9 %key_grads.1 = (bf16[2,64,1024]{2,1,0:T(8,128)(2,1)}, bf16[2,64,1024]{2,1,0:T(8,128)(2,1)}) custom-call(s32[2]{0:T(128)S(1)} %pad_add_fusion.here_ref, s32[8,32]{1,0:T(8,128)S(1)} %copy-done.6, bf16[2,64,1024]{2,1,0:T(8,128)(2,1)S(1)} %bitcast.36, bf16[2,64,1024]{2,1,0:T(8,128)(2,1)S(1)} %bitcast.40, bf16[2,64,1024]{2,1,0:T(8,128)(2,1)S(1)} %bitcast.32, ...), custom_call_target="tpu_custom_call" | custom-call | flops 4800000000 | bytes 6000000 | tf_op jit(solution)/shard_map/key_grads/pallas_call | solution.py:372
  (33 shorter events, 0.6 us)
Async XLA Ops:
  0.6 25.7 %collective-permute-start = (bf16[2,64,1024]{2,1,0:T(8,128)(2,1)}, bf16[2,64,1024]{2,1,0:T(8,128)(2,1)S(1)}, u32[]{:S(2)}, u32[]{:S(2)}) collective-permute-start(bf16[2,64,1024]{2,1,0:T(8,128)(2,1)} %bitcast.33), channel_id=1, source_target_pairs={{0,1},{8,9},{16,17},{24,25},{32,33},{40,41},{48,49},{56,57},{64,65... | collective-permute-start | bytes 786440 | tf_op jit(solution)/shard_map/ppermute | solution.py:58
  2.6 2.6 %copy-start.5 = (bf16[1,2,64,1024]{3,2,1,0:T(8,128)(2,1)S(1)}, bf16[1,2,64,1024]{3,2,1,0:T(8,128)(2,1)}, u32[]{:S(2)}) copy-start(bf16[1,2,64,1024]{3,2,1,0:T(8,128)(2,1)} %param.8) | copy-start | bytes 786436
  3.6 21.9 %collective-permute-start.1 = (bf16[1,64,1024]{2,1,0:T(8,128)(2,1)S(1)}, bf16[1,64,1024]{2,1,0:T(8,128)(2,1)S(1)}, u32[]{:S(2)}, u32[]{:S(2)}) collective-permute-start(bf16[1,64,1024]{2,1,0:T(8,128)(2,1)S(1)} %get-tuple-element.27), channel_id=1, source_target_pairs={{0,121},{8,17},{16,9},{24,33},{32,25},{40,49},{48,41},{56,65},{64,... | collective-permute-start | bytes 393224 | tf_op jit(solution)/shard_map/ppermute | solution.py:60
  5.1 3.5 %copy-start.2 = (bf16[1,2,64,1024]{3,2,1,0:T(8,128)(2,1)S(1)}, bf16[1,2,64,1024]{3,2,1,0:T(8,128)(2,1)}, u32[]{:S(2)}) copy-start(bf16[1,2,64,1024]{3,2,1,0:T(8,128)(2,1)} %param.9) | copy-start | bytes 786436
  5.1 25.5 %collective-permute-start.5 = (bf16[2,64,1024]{2,1,0:T(8,128)(2,1)S(1)}, bf16[2,64,1024]{2,1,0:T(8,128)(2,1)S(1)}, u32[]{:S(2)}, u32[]{:S(2)}) collective-permute-start(bf16[2,64,1024]{2,1,0:T(8,128)(2,1)S(1)} %bitcast.37), channel_id=1, source_target_pairs={{0,1},{8,9},{16,17},{24,25},{32,33},{40,41},{48,49},{56,57},{64,65... | collective-permute-start | bytes 786440 | tf_op jit(solution)/shard_map/ppermute | solution.py:58
  8.5 20.3 %collective-permute-start.6 = (bf16[1,64,1024]{2,1,0:T(8,128)(2,1)S(1)}, bf16[1,64,1024]{2,1,0:T(8,128)(2,1)S(1)}, u32[]{:S(2)}, u32[]{:S(2)}) collective-permute-start(bf16[1,64,1024]{2,1,0:T(8,128)(2,1)S(1)} %get-tuple-element.25), channel_id=1, source_target_pairs={{0,121},{8,17},{16,9},{24,33},{32,25},{40,49},{48,41},{56,65},{64,... | collective-permute-start | bytes 393224 | tf_op jit(solution)/shard_map/ppermute | solution.py:60
  8.6 27.2 %collective-permute-start.10 = (bf16[2,64,1024]{2,1,0:T(8,128)(2,1)S(1)}, bf16[2,64,1024]{2,1,0:T(8,128)(2,1)S(1)}, u32[]{:S(2)}, u32[]{:S(2)}) collective-permute-start(bf16[2,64,1024]{2,1,0:T(8,128)(2,1)S(1)} %bitcast.27), channel_id=1, source_target_pairs={{0,1},{8,9},{16,17},{24,25},{32,33},{40,41},{48,49},{56,57},{64,65... | collective-permute-start | bytes 786440 | tf_op jit(solution)/shard_map/ppermute | solution.py:58
  25.5 34.4 %collective-permute-start.3 = (bf16[1,64,1024]{2,1,0:T(8,128)(2,1)S(1)}, bf16[1,64,1024]{2,1,0:T(8,128)(2,1)S(1)}, u32[]{:S(2)}, u32[]{:S(2)}) collective-permute-start(bf16[1,64,1024]{2,1,0:T(8,128)(2,1)S(1)} %get-tuple-element.27), channel_id=1, source_target_pairs={{0,120},{8,16},{16,8},{24,32},{32,24},{40,48},{48,40},{56,64},{64,... | collective-permute-start | bytes 393224 | tf_op jit(solution)/shard_map/ppermute | solution.py:59
  26.3 7.6 %collective-permute-start.11 = (bf16[1,64,1024]{2,1,0:T(8,128)(2,1)S(1)}, bf16[1,64,1024]{2,1,0:T(8,128)(2,1)S(1)}, u32[]{:S(2)}, u32[]{:S(2)}) collective-permute-start(bf16[1,64,1024]{2,1,0:T(8,128)(2,1)S(1)} %get-tuple-element.23), channel_id=1, source_target_pairs={{0,121},{8,17},{16,9},{24,33},{32,25},{40,49},{48,41},{56,65},{64,... | collective-permute-start | bytes 393224 | tf_op jit(solution)/shard_map/ppermute | solution.py:60
  28.8 32.8 %collective-permute-start.8 = (bf16[1,64,1024]{2,1,0:T(8,128)(2,1)S(1)}, bf16[1,64,1024]{2,1,0:T(8,128)(2,1)S(1)}, u32[]{:S(2)}, u32[]{:S(2)}) collective-permute-start(bf16[1,64,1024]{2,1,0:T(8,128)(2,1)S(1)} %get-tuple-element.25), channel_id=1, source_target_pairs={{0,120},{8,16},{16,8},{24,32},{32,24},{40,48},{48,40},{56,64},{64,... | collective-permute-start | bytes 393224 | tf_op jit(solution)/shard_map/ppermute | solution.py:59
  30.6 13.1 %collective-permute-start.2 = (bf16[3,64,1024]{2,1,0:T(8,128)(2,1)S(1)}, bf16[3,64,1024]{2,1,0:T(8,128)(2,1)S(1)}, u32[]{:S(2)}, u32[]{:S(2)}) collective-permute-start(bf16[3,64,1024]{2,1,0:T(8,128)(2,1)S(1)} %pad_maximum_fusion.2), channel_id=1, source_target_pairs={{0,2},{8,10},{16,18},{24,26},{32,34},{40,42},{48,50},{56,58},{64,6... | collective-permute-start | bytes 1179656 | tf_op jit(solution)/shard_map/ppermute | solution.py:61
  33.9 18.2 %collective-permute-start.7 = (bf16[3,64,1024]{2,1,0:T(8,128)(2,1)S(1)}, bf16[3,64,1024]{2,1,0:T(8,128)(2,1)S(1)}, u32[]{:S(2)}, u32[]{:S(2)}) collective-permute-start(bf16[3,64,1024]{2,1,0:T(8,128)(2,1)S(1)} %pad_maximum_fusion.4), channel_id=1, source_target_pairs={{0,2},{8,10},{16,18},{24,26},{32,34},{40,42},{48,50},{56,58},{64,6... | collective-permute-start | bytes 1179656 | tf_op jit(solution)/shard_map/ppermute | solution.py:61
  35.9 23.0 %collective-permute-start.12 = (bf16[3,64,1024]{2,1,0:T(8,128)(2,1)S(1)}, bf16[3,64,1024]{2,1,0:T(8,128)(2,1)S(1)}, u32[]{:S(2)}, u32[]{:S(2)}) collective-permute-start(bf16[3,64,1024]{2,1,0:T(8,128)(2,1)S(1)} %pad_maximum_fusion.6), channel_id=1, source_target_pairs={{0,2},{8,10},{16,18},{24,26},{32,34},{40,42},{48,50},{56,58},{64,6... | collective-permute-start | bytes 1179656 | tf_op jit(solution)/shard_map/ppermute | solution.py:61
  43.7 19.7 %collective-permute-start.4 = (bf16[3,64,1024]{2,1,0:T(8,128)(2,1)S(1)}, bf16[3,64,1024]{2,1,0:T(8,128)(2,1)S(1)}, u32[]{:S(2)}, u32[]{:S(2)}) collective-permute-start(bf16[3,64,1024]{2,1,0:T(8,128)(2,1)S(1)} %pad_maximum_fusion.3), channel_id=1, source_target_pairs={{0,8},{8,0},{16,24},{24,16},{32,40},{40,32},{48,56},{56,48},{64,72... | collective-permute-start | bytes 1179656 | tf_op jit(solution)/shard_map/ppermute | solution.py:63
  52.1 12.0 %collective-permute-start.9 = (bf16[3,64,1024]{2,1,0:T(8,128)(2,1)S(1)}, bf16[3,64,1024]{2,1,0:T(8,128)(2,1)S(1)}, u32[]{:S(2)}, u32[]{:S(2)}) collective-permute-start(bf16[3,64,1024]{2,1,0:T(8,128)(2,1)S(1)} %pad_maximum_fusion.5), channel_id=1, source_target_pairs={{0,8},{8,0},{16,24},{24,16},{32,40},{40,32},{48,56},{56,48},{64,72... | collective-permute-start | bytes 1179656 | tf_op jit(solution)/shard_map/ppermute | solution.py:63
  58.9 1.0 copy-start.3
  59.0 8.5 %collective-permute-start.14 = (bf16[3,64,1024]{2,1,0:T(8,128)(2,1)S(1)}, bf16[3,64,1024]{2,1,0:T(8,128)(2,1)S(1)}, u32[]{:S(2)}, u32[]{:S(2)}) collective-permute-start(bf16[3,64,1024]{2,1,0:T(8,128)(2,1)S(1)} %pad_maximum_fusion.7), channel_id=1, source_target_pairs={{0,8},{8,0},{16,24},{24,16},{32,40},{40,32},{48,56},{56,48},{64,72... | collective-permute-start | bytes 1179656 | tf_op jit(solution)/shard_map/ppermute | solution.py:63
  59.9 4.2 %copy-start.4 = (bf16[1,2,64,1024]{3,2,1,0:T(8,128)(2,1)S(1)}, bf16[1,2,64,1024]{3,2,1,0:T(8,128)(2,1)}, u32[]{:S(2)}) copy-start(bf16[1,2,64,1024]{3,2,1,0:T(8,128)(2,1)} %param.7) | copy-start | bytes 786436
  59.9 4.2 %copy-start.6 = (s32[8,32]{1,0:T(8,128)S(1)}, s32[8,32]{1,0:T(8,128)}, u32[]{:S(2)}) copy-start(s32[8,32]{1,0:T(8,128)} %cloud_ref.7) | copy-start | bytes 3076
  59.9 7.6 %collective-permute-start.13 = (bf16[1,64,1024]{2,1,0:T(8,128)(2,1)S(1)}, bf16[1,64,1024]{2,1,0:T(8,128)(2,1)S(1)}, u32[]{:S(2)}, u32[]{:S(2)}) collective-permute-start(bf16[1,64,1024]{2,1,0:T(8,128)(2,1)S(1)} %get-tuple-element.23), channel_id=1, source_target_pairs={{0,120},{8,16},{16,8},{24,32},{32,24},{40,48},{48,40},{56,64},{64,... | collective-permute-start | bytes 393224 | tf_op jit(solution)/shard_map/ppermute | solution.py:59
  61.6 13.6 %collective-permute-start.15 = (bf16[2,64,1024]{2,1,0:T(8,128)(2,1)S(1)}, bf16[2,64,1024]{2,1,0:T(8,128)(2,1)S(1)}, u32[]{:S(2)}, u32[]{:S(2)}) collective-permute-start(bf16[2,64,1024]{2,1,0:T(8,128)(2,1)S(1)} %bitcast.29), channel_id=1, source_target_pairs={{0,1},{8,9},{16,17},{24,25},{32,33},{40,41},{48,49},{56,57},{64,65... | collective-permute-start | bytes 786440 | tf_op jit(solution)/shard_map/ppermute | solution.py:58
  63.5 11.8 %collective-permute-start.16 = (bf16[1,64,1024]{2,1,0:T(8,128)(2,1)S(1)}, bf16[1,64,1024]{2,1,0:T(8,128)(2,1)S(1)}, u32[]{:S(2)}, u32[]{:S(2)}) collective-permute-start(bf16[1,64,1024]{2,1,0:T(8,128)(2,1)S(1)} %get-tuple-element.21), channel_id=1, source_target_pairs={{0,121},{8,17},{16,9},{24,33},{32,25},{40,49},{48,41},{56,65},{64,... | collective-permute-start | bytes 393224 | tf_op jit(solution)/shard_map/ppermute | solution.py:60
  67.5 0.7 copy-start.7
  71.1 13.5 %collective-permute-start.20 = (bf16[2,64,1152]{2,1,0:T(8,128)(2,1)S(1)}, bf16[2,64,1152]{2,1,0:T(8,128)(2,1)S(1)}, u32[]{:S(2)}, u32[]{:S(2)}) collective-permute-start(bf16[2,64,1152]{2,1,0:T(8,128)(2,1)S(1)} %get-tuple-element.14.grad_ref.rest_6_), channel_id=1, source_target_pairs={{0,1},{8,9},{16,17},{24,25},{32,33},{40,41},{48,49},{56,57},{64,65... | collective-permute-start | bytes 884744 | tf_op jit(solution)/shard_map/ppermute | solution.py:58
  73.8 10.8 %collective-permute-start.21 = (bf16[1,64,1152]{2,1,0:T(8,128)(2,1)S(1)}, bf16[1,64,1152]{2,1,0:T(8,128)(2,1)S(1)}, u32[]{:S(2)}, u32[]{:S(2)}) collective-permute-start(bf16[1,64,1152]{2,1,0:T(8,128)(2,1)S(1)} %get-tuple-element.19), channel_id=1, source_target_pairs={{0,121},{8,17},{16,9},{24,33},{32,25},{40,49},{48,41},{56,65},{64,... | collective-permute-start | bytes 442376 | tf_op jit(solution)/shard_map/ppermute | solution.py:60
  75.3 12.2 %collective-permute-start.17 = (bf16[3,64,1024]{2,1,0:T(8,128)(2,1)S(1)}, bf16[3,64,1024]{2,1,0:T(8,128)(2,1)S(1)}, u32[]{:S(2)}, u32[]{:S(2)}) collective-permute-start(bf16[3,64,1024]{2,1,0:T(8,128)(2,1)S(1)} %pad_maximum_fusion.8), channel_id=1, source_target_pairs={{0,2},{8,10},{16,18},{24,26},{32,34},{40,42},{48,50},{56,58},{64,6... | collective-permute-start | bytes 1179656 | tf_op jit(solution)/shard_map/ppermute | solution.py:61
  84.6 2.9 %copy-start = (bf16[2,64,1152]{2,1,0:T(8,128)(2,1)}, bf16[2,64,1152]{2,1,0:T(8,128)(2,1)S(1)}, u32[]{:S(2)}) copy-start(bf16[2,64,1152]{2,1,0:T(8,128)(2,1)S(1)} %collective-permute-done.20.rest_7_) | copy-start | bytes 884740
  84.7 14.1 %collective-permute-start.22 = (bf16[3,64,1152]{2,1,0:T(8,128)(2,1)S(1)}, bf16[3,64,1152]{2,1,0:T(8,128)(2,1)S(1)}, u32[]{:S(2)}, u32[]{:S(2)}) collective-permute-start(bf16[3,64,1152]{2,1,0:T(8,128)(2,1)S(1)} %pad_maximum_fusion), channel_id=1, source_target_pairs={{0,2},{8,10},{16,18},{24,26},{32,34},{40,42},{48,50},{56,58},{64,6... | collective-permute-start | bytes 1327112 | tf_op jit(solution)/shard_map/ppermute | solution.py:61
  87.5 11.2 %slice-start = ((bf16[2,64,1152]{2,1,0:T(8,128)(2,1)}), bf16[1,64,1152]{2,1,0:T(8,128)(2,1)S(1)}, s32[]{:S(2)}) async-start(bf16[2,64,1152]{2,1,0:T(8,128)(2,1)} %copy-done), calls=%async_computation | async-start | bytes 294912 | tf_op jit(solution)/shard_map/slice | solution.py:361
  98.8 14.9 %collective-permute-start.24 = (bf16[3,64,1152]{2,1,0:T(8,128)(2,1)S(1)}, bf16[3,64,1152]{2,1,0:T(8,128)(2,1)S(1)}, u32[]{:S(2)}, u32[]{:S(2)}) collective-permute-start(bf16[3,64,1152]{2,1,0:T(8,128)(2,1)S(1)} %pad_maximum_fusion.1), channel_id=1, source_target_pairs={{0,8},{8,0},{16,24},{24,16},{32,40},{40,32},{48,56},{56,48},{64,72... | collective-permute-start | bytes 1327112 | tf_op jit(solution)/shard_map/ppermute | solution.py:63
  99.4 12.2 %collective-permute-start.19 = (bf16[3,64,1024]{2,1,0:T(8,128)(2,1)S(1)}, bf16[3,64,1024]{2,1,0:T(8,128)(2,1)S(1)}, u32[]{:S(2)}, u32[]{:S(2)}) collective-permute-start(bf16[3,64,1024]{2,1,0:T(8,128)(2,1)S(1)} %pad_maximum_fusion.9), channel_id=1, source_target_pairs={{0,8},{8,0},{16,24},{24,16},{32,40},{40,32},{48,56},{56,48},{64,72... | collective-permute-start | bytes 1179656 | tf_op jit(solution)/shard_map/ppermute | solution.py:63
  99.6 12.0 %collective-permute-start.18 = (bf16[1,64,1024]{2,1,0:T(8,128)(2,1)S(1)}, bf16[1,64,1024]{2,1,0:T(8,128)(2,1)S(1)}, u32[]{:S(2)}, u32[]{:S(2)}) collective-permute-start(bf16[1,64,1024]{2,1,0:T(8,128)(2,1)S(1)} %get-tuple-element.21), channel_id=1, source_target_pairs={{0,120},{8,16},{16,8},{24,32},{32,24},{40,48},{48,40},{56,64},{64,... | collective-permute-start | bytes 393224 | tf_op jit(solution)/shard_map/ppermute | solution.py:59
  107.1 6.6 %collective-permute-start.23 = (bf16[1,64,1152]{2,1,0:T(8,128)(2,1)S(1)}, bf16[1,64,1152]{2,1,0:T(8,128)(2,1)S(1)}, u32[]{:S(2)}, u32[]{:S(2)}) collective-permute-start(bf16[1,64,1152]{2,1,0:T(8,128)(2,1)S(1)} %get-tuple-element.19), channel_id=1, source_target_pairs={{0,120},{8,16},{16,8},{24,32},{32,24},{40,48},{48,40},{56,64},{64,... | collective-permute-start | bytes 442376 | tf_op jit(solution)/shard_map/ppermute | solution.py:59
  107.1 6.6 %copy-start.1 = (bf16[2,64,1152]{2,1,0:T(8,128)(2,1)S(1)}, bf16[2,64,1152]{2,1,0:T(8,128)(2,1)}, u32[]{:S(2)}) copy-start(bf16[2,64,1152]{2,1,0:T(8,128)(2,1)} %copy-done) | copy-start | bytes 884740

commit v3 on v2

--- a/solution.py
+++ b/solution.py
@@ -45,40 +45,41 @@
     def hop(r):
         return r + 2 if r % 2 == 0 else r - 2
 
+    def past(r):
+        return r - 1 if r % 2 == 0 else r + 1
+
     return dict(
         swap=[(at(r, c), at(r ^ 1, c)) for r, c in cells],
         off=[(at(r, c), at(r, away(c))) for r, c in cells],
         cor=[(at(r, c), at(r ^ 1, away(c))) for r, c in cells],
         far=[(at(r, c), at(hop(r), c)) for r, c in cells if 0 <= hop(r) < rows],
         twin=[(at(r, c), at(r, c ^ 1)) for r, c in cells],
-    )
-
-
-def exchange(own, near, face_of, way):
-    swap = lax.ppermute(own, AXES, way["swap"])
-    off = lax.ppermute(near, AXES, way["off"])
-    cor = lax.ppermute(near, AXES, way["cor"])
-    far = lax.ppermute(jnp.concatenate([swap, cor], axis=0), AXES, way["far"])
-    facing = jnp.concatenate([face_of(own), face_of(swap), face_of(far)], axis=0)
-    twin = lax.ppermute(facing, AXES, way["twin"])
-    return (own, swap, far, off, cor, twin)
-
-
-def region_block(pieces, n, row, col, fs):
-    own, swap, far, off, cor, twin = pieces
-    if col == 0:
-        ref, index = ((off, 0), (cor, 0), (far, 2))[row]
-    elif col == 3:
-        ref, index = twin, row
-    else:
-        ref, index = (own, swap, far)[row], n if col == 1 else 1 - n
-    return ref[index, :, fs]
-
-
-def window(pieces, n, t, fs):
-    return jnp.concatenate(
-        [region_block(pieces, n, row, col + t, fs) for row in range(3) for col in range(3)], axis=0
-    )
+        out=[(at(r, c), at(past(r), c)) for r, c in cells if 0 <= past(r) < rows],
+        edge=[(at(r, c), at(past(r), away(c))) for r, c in cells if 0 <= past(r) < rows],
+    )
+
+
+def after(x, *done):
+    return lax.optimization_barrier((x,) + done)[0]
+
+
+def phase(*values):
+    return lax.optimization_barrier(values)
+
+
+def region(own, swap, far, off, cor, twins, n, side=0, inner=(0, 1, 2), corner=None):
+    far, edge = far if isinstance(far, tuple) else (far, None)
+    corner = side if corner is None else corner
+    return (
+        ((off, side), (own, n), (own, 1 - n), (twins[0], inner[0])),
+        ((cor, corner), (swap, n), (swap, 1 - n), (twins[1], inner[1])),
+        ((far, 2) if edge is None else (edge, corner), (far, n), (far, 1 - n), (twins[2], inner[2])),
+    )
+
+
+def window(table, t, fs, rows=(0, 1, 2)):
+    places = [table[row][col + t] for row in rows for col in range(3)]
+    return jnp.concatenate([ref[index, :, fs] for ref, index in places], axis=0)
 
 
 def spread(x):
@@ -137,10 +138,54 @@
     ]
 
 
+def join_kernel(count, *refs):
+    out = refs[count]
+    at = 0
+    for ref in refs[:count]:
+        size = ref.shape[0]
+        out[at : at + size] = ref[...]
+        at += size
+
+
+def edges_kernel(here_ref, k_ref, v_ref, s_ref, q_ref, cor_ref, qn_ref, off_ref, sems):
+    n = here_ref[1] % 2
+    copies = [
+        pltpu.make_async_copy(ref.at[n], off_ref.at[i], sems.at[i])
+        for i, ref in enumerate((k_ref, v_ref, s_ref, q_ref))
+    ]
+    for c in copies:
+        c.start()
+    for c in copies:
+        c.wait()
+    cor_ref[...] = off_ref[0:3]
+    qn_ref[0] = off_ref[3]
+
+
+def faces_kernel(here_ref, *refs):
+    n = here_ref[1] % 2
+    for i, ref in enumerate(refs[:-1]):
+        refs[-1][i] = ref[1 - n]
+
+
+def grad_pack_kernel(grad_ref, swap_ref, cor_ref, far_ref, face_ref):
+    far_ref[0:2] = swap_ref[...]
+    far_ref[2] = cor_ref[0]
+    face_ref[0] = grad_ref[1]
+    face_ref[1] = swap_ref[1]
+
+
+def key_value_tables(refs, n):
+    k, v, k_swap, v_swap, k_far, v_far, cor, edge, off, twin, k_far_twin, v_far_twin = refs
+    return (
+        region(k, k_swap, (k_far, edge), off, cor, (twin, twin, k_far_twin), n, 0, (0, 4, n)),
+        region(v, v_swap, (v_far, edge), off, cor, (twin, twin, v_far_twin), n, 1, (1, 5, n)),
+    )
+
+
 def attend_kernel(here_ref, cloud_ref, q_ref, *rest):
-    k_pieces, v_pieces = rest[0:6], rest[6:12]
+    n, _, clear = region_flags(here_ref, cloud_ref)
+    k_table, v_table = key_value_tables(rest[0:12], n)
     att_ref, stat_ref = rest[12:]
-    n, _, clear = region_flags(here_ref, cloud_ref)
     for t in range(2):
         qt = n if t == 0 else 1 - n
         stat_ref[t] = jnp.zeros((PP, 128), F32)
@@ -149,14 +194,14 @@
         def step(g, carry):
             fs = group_slice(g)
             q = spread(q_ref[qt, :, fs] * SCALE)
-            kw = window(k_pieces, n, t, fs)
+            kw = window(k_table, t, fs)
             s = dot(q, kw, NT) + mask
             m = jnp.max(s, axis=1, keepdims=True)
             e = jnp.exp(s - m)
             total = jnp.sum(e, axis=1, keepdims=True)
             p = (e * (1.0 / total)).astype(BF)
             lse = m + jnp.log(total)
-            att_ref[t, :, fs] = gather_heads(dot(p, window(v_pieces, n, t, fs), NN)).astype(BF)
+            att_ref[t, :, fs] = gather_heads(dot(p, window(v_table, t, fs), NN)).astype(BF)
             lane = lax.broadcasted_iota(jnp.int32, (PP, 128), 1)
             stat = stat_ref[t]
             for h in range(GROUP):
@@ -168,13 +213,11 @@
 
 
 def contrast_kernel(here_ref, cloud_ref, att_ref, stat_ref, pair_ref, *rest):
-    pieces = rest[0:6]
-    loss_ref, grad_ref, stats_ref = rest[6:]
+    loss_ref, grad_ref, stats_ref = rest[8:]
     n, _, clear = region_flags(here_ref, cloud_ref)
-    whole = slice(0, WIDTH)
-    season = jnp.concatenate(
-        [region_block(pieces, n, row, col, whole) for row in range(3) for col in range(4)], axis=0
-    )
+    s, swap, far, edge, off, cor, twin, far_twin = rest[0:8]
+    table = region(s, swap, (far, edge), off, cor, (twin, twin, far_twin), n, side=2, inner=(2, 6, n))
+    season = jnp.concatenate([ref[index] for line in table for ref, index in line], axis=0)
     att = jnp.concatenate([att_ref[0], att_ref[1]], axis=0)
     side = lax.broadcasted_iota(jnp.int32, (2 * PP, REG), 0) < PP
     sides = []
@@ -233,9 +276,9 @@
 
 
 def query_kernel(here_ref, cloud_ref, q_ref, grad_ref, stats_ref, *rest):
-    k_pieces, v_pieces = rest[0:6], rest[6:12]
+    n, _, clear = region_flags(here_ref, cloud_ref)
+    k_table, v_table = key_value_tables(rest[0:12], n)
     out_ref = rest[12]
-    n, _, clear = region_flags(here_ref, cloud_ref)
     for t in range(2):
         qt = n if t == 0 else 1 - n
         mask = segments(query_flags(clear, t), NEG_FILL)
@@ -246,10 +289,10 @@
             stat = stats_ref[t]
             lse = head_column(stat, g * GROUP)
             delta = head_column(stat, g * GROUP + HEADS)
-            kw = window(k_pieces, n, t, fs)
+            kw = window(k_table, t, fs)
             s = dot(q, kw, NT) + mask
             p = jnp.exp(s - lse)
-            gd = dot(spread(grad_ref[t, :, fs]), window(v_pieces, n, t, fs), NT)
+            gd = dot(spread(grad_ref[t, :, fs]), window(v_table, t, fs), NT)
             ds = (p * (gd - delta)).astype(BF)
             out = gather_heads(dot(ds, kw, NN)) * SCALE
             out_ref[qt, :, fs] = out.astype(BF)
@@ -258,29 +301,27 @@
         lax.fori_loop(0, GROUPS, step, 0, unroll=True)
 
 
-def key_kernel(here_ref, cloud_ref, k_ref, v_ref, *rest):
-    q_pieces, g_pieces = rest[0:6], rest[6:12]
-    kout_ref, vout_ref, rows_ref = rest[12:]
-    n, inside, clear = region_flags(here_ref, cloud_ref)
+def key_terms(flags, rows, k_ref, v_ref, n, q_table, g_table, rows_ref, finish):
+    inside, clear = flags
     for t in range(2):
         kt = n if t == 0 else 1 - n
-        parts = jnp.transpose(window(g_pieces, 0, t, slice(WIDTH, EXT)).astype(F32))
+        parts = jnp.transpose(window(g_table, t, slice(WIDTH, EXT), rows).astype(F32))
         stats = parts[0:32] + parts[32:64] + parts[64:96]
         seen = clear[0][1 + t]
-        flags = [
+        open_to = [
             True if (row, col) == (0, 1) else (seen & inside[2] if row == 2 else seen)
-            for row in range(3)
+            for row in rows
             for col in range(3)
         ]
-        rows_ref[0:HEADS] = stats[0:HEADS] + segments(flags, -NEG_FILL)
+        rows_ref[0:HEADS] = stats[0:HEADS] + segments(open_to, -NEG_FILL)
         rows_ref[HEADS : 2 * HEADS] = stats[HEADS : 2 * HEADS]
 
         def step(g, carry):
             fs = group_slice(g)
             ks = spread(k_ref[kt, :, fs] * SCALE)
             vs = spread(v_ref[kt, :, fs])
-            qw = window(q_pieces, n, t, fs)
-            gw = window(g_pieces, 0, t, fs)
+            qw = window(q_table, t, fs, rows)
+            gw = window(g_table, t, fs, rows)
             s = dot(ks, qw, NT)
             gd = dot(vs, gw, NT)
             ps, dss = [], []
@@ -293,15 +334,43 @@
                 dss.append((p * (gd[part] - delta)).astype(BF))
             p = jnp.concatenate(ps, axis=0)
             ds = jnp.concatenate(dss, axis=0)
-            kout_ref[kt, :, fs] = (gather_heads(dot(ds, qw, NN)) * SCALE).astype(BF)
-            vout_ref[kt, :, fs] = gather_heads(dot(p, gw, NN)).astype(BF)
+            finish(t, kt, fs, gather_heads(dot(ds, qw, NN)), gather_heads(dot(p, gw, NN)))
             return carry
 
         lax.fori_loop(0, GROUPS, step, 0, unroll=True)
+
+
+def inner_key_kernel(here_ref, cloud_ref, k_ref, v_ref, *rest):
+    q, q_swap, q_off, q_cor, own_twin, q_twin, g, g_swap, g_off, g_cor, g_twin = rest[0:11]
+    ksum_ref, vsum_ref, rows_ref = rest[11:]
+    n, inside, clear = region_flags(here_ref, cloud_ref)
+    q_table = region(q, q_swap, None, q_off, q_cor, (own_twin, q_twin, None), n, side=3, inner=(3, n, None), corner=0)
+    g_table = region(g, g_swap, None, g_off, g_cor, (g_twin, g_twin, None), 0, inner=(0, 1, None))
+
+    def finish(t, kt, fs, dk, dv):
+        ksum_ref[t, :, fs] = dk
+        vsum_ref[t, :, fs] = dv
+
+    key_terms((inside, clear), (0, 1), k_ref, v_ref, n, q_table, g_table, rows_ref, finish)
+
+
+def outer_key_kernel(here_ref, cloud_ref, k_ref, v_ref, ksum_ref, vsum_ref, *rest):
+    q_far, q_twin, g_far, g_twin = rest[0:4]
+    kout_ref, vout_ref, rows_ref = rest[4:]
+    n, inside, clear = region_flags(here_ref, cloud_ref)
+    q_table = region(None, None, q_far, None, None, (None, None, q_twin), n, inner=(n, n, n))
+    g_table = region(None, None, g_far, None, None, (None, None, g_twin), 0, inner=(1, 1, 1))
+
+    def finish(t, kt, fs, dk, dv):
+        kout_ref[kt, :, fs] = ((ksum_ref[t, :, fs] + dk) * SCALE).astype(BF)
+        vout_ref[kt, :, fs] = (vsum_ref[t, :, fs] + dv).astype(BF)
+
+    key_terms((inside, clear), (2,), k_ref, v_ref, n, q_table, g_table, rows_ref, finish)
 
 
 SMEM = pl.BlockSpec(memory_space=pltpu.SMEM)
 VMEM = pl.BlockSpec(memory_space=pltpu.VMEM)
+ANY = pl.BlockSpec(memory_space=pl.ANY)
 
 
 def call(kernel, name, in_specs, out_shape, scratch, flops):
@@ -324,21 +393,64 @@
 def body(way, queries, keys, values, season, cloud, pairing):
     lat = lax.axis_index("lat")
     lon = lax.axis_index("lon")
-    odd = lon % 2
     q, k, v, s = (x[0] for x in (queries, keys, values, season))
 
-    def near_of(x):
-        return lax.dynamic_slice_in_dim(x, odd, 1, axis=0)
-
-    def face_of(x):
-        return lax.dynamic_slice_in_dim(x, 1 - odd, 1, axis=0)
-
     here = jnp.stack([lat, lon]).astype(jnp.int32)
 
-    kp = exchange(k, near_of(k), face_of, way)
-    vp = exchange(v, near_of(v), face_of, way)
-    sp = exchange(s, near_of(s), face_of, way)
-    qp = exchange(q, near_of(q), face_of, way)
+    def move(x, kind):
+        return lax.ppermute(x, AXES, way[kind])
+
+    def named(name, x, kind):
+        with jax.named_scope(name + "_" + kind):
+            return move(x, kind)
+
+    def joined(*parts):
+        total = sum(p.shape[0] for p in parts)
+        return call(
+            functools.partial(join_kernel, len(parts)),
+            "join",
+            [VMEM] * len(parts),
+            shape((total,) + parts[0].shape[1:], parts[0].dtype),
+            [],
+            1_000_000,
+        )(*parts)
+
+    k_swap = named("key", k, "swap")
+    v_swap = named("value", v, "swap")
+    cor_near, q_near, nears = call(
+        edges_kernel,
+        "edges",
+        [SMEM] + [ANY] * 4,
+        (shape((3, PP, WIDTH), BF), shape((1, PP, WIDTH), BF), shape((4, PP, WIDTH), BF)),
+        [pltpu.SemaphoreType.DMA((4,))],
+        1_000_000,
+    )(here, k, v, s, q)
+    k_swap, v_swap, s1, cor_near, nears = phase(k_swap, v_swap, s, cor_near, nears)
+    k_far = named("key", k_swap, "far")
+    v_far = named("value", v_swap, "far")
+    s_swap = named("season", s1, "swap")
+    cor = named("kvs", cor_near, "cor")
+    off = named("all", nears, "off")
+    k_far, v_far, s_swap, cor, off, q1, q_near = phase(k_far, v_far, s_swap, cor, off, q, q_near)
+    s_far = named("season", s_swap, "far")
+    edge = named("kvs", cor, "far")
+    q_swap = named("query", q1, "swap")
+    q_cor = named("query", q_near, "cor")
+    faces = call(
+        faces_kernel,
+        "faces",
+        [SMEM] + [VMEM] * 7,
+        shape((7, PP, WIDTH), BF),
+        [],
+        1_000_000,
+    )(here, k, v, s, q, k_swap, v_swap, s_swap)
+    twin = named("inner", faces, "twin")
+    s_far, edge, off, twin, q_swap, q_cor = phase(s_far, edge, off, twin, q_swap, q_cor)
+    k_far_twin = named("key_far", k_far, "twin")
+    v_far_twin = named("value_far", v_far, "twin")
+    s_far_twin = named("season_far", s_far, "twin")
+    q_far = named("query", joined(q_swap, q_cor), "far")
+    kvp = (k, v, k_swap, v_swap, k_far, v_far, cor, edge, off, twin, k_far_twin, v_far_twin)
 
     att, stat = call(
         attend_kernel,
@@ -347,19 +459,21 @@
         (shape((2, PP, WIDTH), BF), shape((2, PP, 128), F32)),
         [],
         2_400_000_000,
-    )(here, cloud, q, *kp, *vp)
+    )(here, cloud, q, *kvp)
 
     loss, grad, stats = call(
         contrast_kernel,
         "contrast",
-        [SMEM, SMEM, VMEM, VMEM, VMEM] + [VMEM] * 6,
+        [SMEM, SMEM, VMEM, VMEM, VMEM] + [VMEM] * 8,
         (shape((2, PP), F32), shape((2, PP, EXT), BF), shape((2, PP, 128), F32)),
         [],
         1_200_000_000,
-    )(here, cloud, att, stat, pairing[0], *sp)
-
-    gp = exchange(grad, grad[0:1], lambda x: x[1:2], way)
-
+    )(here, cloud, att, stat, pairing[0], s, s_swap, s_far, edge, off, cor, twin, s_far_twin)
+
+    g_near = grad[0:1]
+    g_swap = named("grad", grad, "swap")
+    g_cor = named("grad", g_near, "cor")
+    g_off = named("grad", g_near, "off")
     query_grad = call(
         query_kernel,
         "query_grads",
@@ -367,16 +481,46 @@
         shape((2, PP, WIDTH), BF),
         [],
         3_600_000_000,
-    )(here, cloud, q, grad, stats, *kp, *vp)
-
+    )(here, cloud, q, grad, stats, *kvp)
+
+    g_swap, g_cor, g_off, q_far, query_grad, q_swap1 = phase(
+        g_swap, g_cor, g_off, q_far, query_grad, q_swap
+    )
+    q_swap_twin = named("query", q_swap1, "twin")
+    far, faces = call(
+        grad_pack_kernel,
+        "grad_pack",
+        [VMEM] * 3,
+        (shape((3, PP, EXT), BF), shape((2, PP, EXT), BF)),
+        [],
+        1_000_000,
+    )(grad, g_swap, g_cor)
+    g_far = named("grad", far, "far")
+    g_twin = named("grad", faces, "twin")
+    q_far_twin = named("query_far", q_far, "twin")
+
+    key_sum, value_sum = call(
+        inner_key_kernel,
+        "inner_key_grads",
+        [SMEM, SMEM, VMEM, VMEM] + [VMEM] * 11,
+        (shape((2, PP, WIDTH), F32), shape((2, PP, WIDTH), F32)),
+        [pltpu.VMEM((2 * HEADS, 6 * PP), F32)],
+        3_200_000_000,
+    )(
+        here, cloud, k, v, q, q_swap, off, q_cor, twin, q_swap_twin,
+        grad, g_swap, g_off, g_cor, g_twin,
+    )
+
+    g_far, q_far_twin, key_sum, value_sum = phase(g_far, q_far_twin, key_sum, value_sum)
+    g_last = named("grad_last", g_far, "twin")
     key_grad, value_grad = call(
-        key_kernel,
-        "key_grads",
-        [SMEM, SMEM, VMEM, VMEM] + [VMEM] * 12,
+        outer_key_kernel,
+        "outer_key_grads",
+        [SMEM, SMEM, VMEM, VMEM, VMEM, VMEM] + [VMEM] * 4,
         (shape((2, PP, WIDTH), BF), shape((2, PP, WIDTH), BF)),
-        [pltpu.VMEM((2 * HEADS, WIN), F32)],
-        4_800_000_000,
-    )(here, cloud, k, v, *qp, *gp)
+        [pltpu.VMEM((2 * HEADS, 3 * PP), F32)],
+        1_600_000_000,
+    )(here, cloud, k, v, key_sum, value_sum, q_far, q_far_twin, g_far, g_last)
 
     return (loss[None], query_grad[None], key_grad[None], value_grad[None])
 

time: 119 us -> 105 us (0.88)
  the two profiles are of different devices: /device:TPU:75 before, /device:TPU:1 now
where the time goes in v3:
time: 105 us
  starting transfers between devices  42.7 us (41%)
  waiting for transfers between devices  37.4 us (36%)
  Pallas kernels  19.5 us (19%)
  local copies, waits for them, and re-layouts  4.5 us (4%)
    ppermute x24, starting transfers between devices, move(): return lax.ppermute(x, AXES, way[kind])  42.7 us
    ppermute x24, waiting for transfers between devices, move(): return lax.ppermute(x, AXES, way[kind])  37.4 us
    unnamed x20, local copies, waits for them, and re-layouts  4.49 us
    pallas_call x1, Pallas kernels, body(): call(query_kernel, 'query_grads', [SMEM, SMEM, VMEM, VMEM, VMEM] + [VMEM]...  4.45 us
    pallas_call x1, Pallas kernels, body(): call(inner_key_kernel, 'inner_key_grads', [SMEM, SMEM, VMEM, VMEM] + [VME...  3.42 us
    pallas_call x1, Pallas kernels, body(): call(attend_kernel, 'attend', [SMEM, SMEM, VMEM] + [VMEM] * 12, (shape((2...  3.41 us
    pallas_call x1, Pallas kernels, body(): call(outer_key_kernel, 'outer_key_grads', [SMEM, SMEM, VMEM, VMEM, VMEM,...  3.34 us
    pallas_call x1, Pallas kernels, body(): call(contrast_kernel, 'contrast', [SMEM, SMEM, VMEM, VMEM, VMEM] + [VMEM]...  2.91 us
  transfers between devices with their start and end apart: 24, of which 9 were waited for; matrix products, arithmetic and copies ran while one was open for 0% of the time, Pallas kernels for 15%

profile of v3, /device:TPU:1, one launch (start us, length us, event | category | flops | bytes accessed | tf_op | source)
XLA Modules:
  0.0 105.1 jit_solution(10435524531323808496)
XLA Ops:
  0.6 3.7 %collective-permute-start = (bf16[2,64,1024]{2,1,0:T(8,128)(2,1)}, bf16[2,64,1024]{2,1,0:T(8,128)(2,1)S(1)}, u32[]{:S(2)}, u32[]{:S(2)}) collective-permute-start(bf16[2,64,1024]{2,1,0:T(8,128)(2,1)} %bitcast.21), channel_id=1, source_target_pairs={{0,1},{8,9},{16,17},{24,25},{32,33},{40,41},{48,49},{56,57},{64,65... | collective-permute-start | bytes 786440 | tf_op jit(solution)/shard_map/key_swap/ppermute | solution.py:401
  4.3 0.1 collective-permute-start.1
  4.4 0.1 pad_add_fusion.here_ref
  4.5 0.9 copy-done
  5.4 0.9 copy-done.2
  6.4 0.9 copy-done.4
  7.3 0.9 copy-done.6
  8.3 1.3 %edges.1 = (bf16[3,64,1024]{2,1,0:T(8,128)(2,1)S(1)}, bf16[1,64,1024]{2,1,0:T(8,128)(2,1)S(1)}, bf16[4,64,1024]{2,1,0:T(8,128)(2,1)S(1)}) custom-call(s32[2]{0:T(128)S(1)} %pad_add_fusion.here_ref, bf16[2,64,1024]{2,1,0:T(8,128)(2,1)S(1)} %bitcast.22, bf16[2,64,1024]{2,1,0:T(8,128)(2,1)S(1)} %bitcast.29, bf16[2,64,1024]{2,1,0:T(8,128)(2,1)S(1)} %bitcast.11, ...), custom_call_target="tpu_custom_call" | custom-call | flops 1000000 | bytes 6000000 | tf_op jit(solution)/shard_map/edges/pallas_call | solution.py:420
  9.6 0.5 collective-permute-done.refs_4_.rest_2_
  10.1 5.6 %collective-permute-done.1.refs_5_.rest_3_ = bf16[2,64,1024]{2,1,0:T(8,128)(2,1)S(1)} collective-permute-done((bf16[2,64,1024]{2,1,0:T(8,128)(2,1)}, bf16[2,64,1024]{2,1,0:T(8,128)(2,1)S(1)}, u32[]{:S(2)}, u32[]{:S(2)}) %collective-permute-start.1) | collective-permute-done | bytes 262176 | tf_op jit(solution)/shard_map/value_swap/ppermute | solution.py:401
  15.7 3.0 %collective-permute-start.6 = (bf16[4,64,1024]{2,1,0:T(8,128)(2,1)S(1)}, bf16[4,64,1024]{2,1,0:T(8,128)(2,1)S(1)}, u32[]{:S(2)}, u32[]{:S(2)}) collective-permute-start(bf16[4,64,1024]{2,1,0:T(8,128)(2,1)S(1)} %get-tuple-element.52), channel_id=1, source_target_pairs={{0,120},{8,16},{16,8},{24,32},{32,24},{40,48},{48,40},{56,64},{64,... | collective-permute-start | bytes 1572872 | tf_op jit(solution)/shard_map/all_off/ppermute | solution.py:401
  18.7 1.3 %collective-permute-start.5 = (bf16[3,64,1024]{2,1,0:T(8,128)(2,1)S(1)}, bf16[3,64,1024]{2,1,0:T(8,128)(2,1)S(1)}, u32[]{:S(2)}, u32[]{:S(2)}) collective-permute-start(bf16[3,64,1024]{2,1,0:T(8,128)(2,1)S(1)} %get-tuple-element.51), channel_id=1, source_target_pairs={{0,121},{8,17},{16,9},{24,33},{32,25},{40,49},{48,41},{56,65},{64,... | collective-permute-start | bytes 1179656 | tf_op jit(solution)/shard_map/kvs_cor/ppermute | solution.py:401
  20.0 3.5 %collective-permute-start.2 = (bf16[2,64,1024]{2,1,0:T(8,128)(2,1)S(1)}, bf16[2,64,1024]{2,1,0:T(8,128)(2,1)S(1)}, u32[]{:S(2)}, u32[]{:S(2)}) collective-permute-start(bf16[2,64,1024]{2,1,0:T(8,128)(2,1)S(1)} %collective-permute-done.refs_4_.rest_2_), channel_id=1, source_target_pairs={{0,2},{8,10},{16,18},{24,26},{32,34},{40,42},{48,50},{56,58},{64,6... | collective-permute-start | bytes 786440 | tf_op jit(solution)/shard_map/key_far/ppermute | solution.py:401
  23.5 3.5 %collective-permute-start.3 = (bf16[2,64,1024]{2,1,0:T(8,128)(2,1)S(1)}, bf16[2,64,1024]{2,1,0:T(8,128)(2,1)S(1)}, u32[]{:S(2)}, u32[]{:S(2)}) collective-permute-start(bf16[2,64,1024]{2,1,0:T(8,128)(2,1)S(1)} %collective-permute-done.1.refs_5_.rest_3_), channel_id=1, source_target_pairs={{0,2},{8,10},{16,18},{24,26},{32,34},{40,42},{48,50},{56,58},{64,6... | collective-permute-start | bytes 786440 | tf_op jit(solution)/shard_map/value_far/ppermute | solution.py:401
  27.1 0.1 collective-permute-start.4
  27.2 0.0 collective-permute-done.2.rest_4_
  27.2 6.0 %collective-permute-done.3.rest_5_ = bf16[2,64,1024]{2,1,0:T(8,128)(2,1)S(1)} collective-permute-done((bf16[2,64,1024]{2,1,0:T(8,128)(2,1)S(1)}, bf16[2,64,1024]{2,1,0:T(8,128)(2,1)S(1)}, u32[]{:S(2)}, u32[]{:S(2)}) %collective-permute-start.3) | collective-permute-done | bytes 262176 | tf_op jit(solution)/shard_map/value_far/ppermute | solution.py:401
  33.2 4.8 %collective-permute-done.4.refs_6_.rest_1_ = bf16[2,64,1024]{2,1,0:T(8,128)(2,1)S(1)} collective-permute-done((bf16[2,64,1024]{2,1,0:T(8,128)(2,1)S(1)}, bf16[2,64,1024]{2,1,0:T(8,128)(2,1)S(1)}, u32[]{:S(2)}, u32[]{:S(2)}) %collective-permute-start.4) | collective-permute-done | bytes 262176 | tf_op jit(solution)/shard_map/season_swap/ppermute | solution.py:401
  38.0 0.0 collective-permute-done.5.rest_6_.rest_5_
  38.0 0.0 collective-permute-done.6.rest_8_.rest_4_.rest_2_
  38.0 0.6 faces.1
  38.6 0.0 copy-start.3
  38.6 0.0 copy-start.5
  38.6 0.0 copy-start.7
  38.6 2.1 %collective-permute-start.9 = (bf16[7,64,1024]{2,1,0:T(8,128)(2,1)S(1)}, bf16[7,64,1024]{2,1,0:T(8,128)(2,1)S(1)}, u32[]{:S(2)}, u32[]{:S(2)}) collective-permute-start(bf16[7,64,1024]{2,1,0:T(8,128)(2,1)S(1)} %faces.1), channel_id=1, source_target_pairs={{0,8},{8,0},{16,24},{24,16},{32,40},{40,32},{48,56},{56,48},{64,72... | collective-permute-start | bytes 2752520 | tf_op jit(solution)/shard_map/inner_twin/ppermute | solution.py:401
  40.8 0.1 collective-permute-start.10
  40.9 3.6 %collective-permute-start.8 = (bf16[3,64,1024]{2,1,0:T(8,128)(2,1)S(1)}, bf16[3,64,1024]{2,1,0:T(8,128)(2,1)S(1)}, u32[]{:S(2)}, u32[]{:S(2)}) collective-permute-start(bf16[3,64,1024]{2,1,0:T(8,128)(2,1)S(1)} %collective-permute-done.5.rest_6_.rest_5_), channel_id=1, source_target_pairs={{0,2},{8,10},{16,18},{24,26},{32,34},{40,42},{48,50},{56,58},{64,6... | collective-permute-start | bytes 1179656 | tf_op jit(solution)/shard_map/kvs_far/ppermute | solution.py:401
  44.5 0.1 collective-permute-start.11
  44.6 3.8 %collective-permute-start.7 = (bf16[2,64,1024]{2,1,0:T(8,128)(2,1)S(1)}, bf16[2,64,1024]{2,1,0:T(8,128)(2,1)S(1)}, u32[]{:S(2)}, u32[]{:S(2)}) collective-permute-start(bf16[2,64,1024]{2,1,0:T(8,128)(2,1)S(1)} %collective-permute-done.4.refs_6_.rest_1_), channel_id=1, source_target_pairs={{0,2},{8,10},{16,18},{24,26},{32,34},{40,42},{48,50},{56,58},{64,6... | collective-permute-start | bytes 786440 | tf_op jit(solution)/shard_map/season_far/ppermute | solution.py:401
  48.4 5.0 %collective-permute-done.11.refs_1_.rest_3_ = bf16[1,64,1024]{2,1,0:T(8,128)(2,1)S(1)} collective-permute-done((bf16[1,64,1024]{2,1,0:T(8,128)(2,1)S(1)}, bf16[1,64,1024]{2,1,0:T(8,128)(2,1)S(1)}, u32[]{:S(2)}, u32[]{:S(2)}) %collective-permute-start.11) | collective-permute-done | bytes 131104 | tf_op jit(solution)/shard_map/query_cor/ppermute | solution.py:401
  53.4 1.8 %collective-permute-start.12 = (bf16[2,64,1024]{2,1,0:T(8,128)(2,1)S(1)}, bf16[2,64,1024]{2,1,0:T(8,128)(2,1)S(1)}, u32[]{:S(2)}, u32[]{:S(2)}) collective-permute-start(bf16[2,64,1024]{2,1,0:T(8,128)(2,1)S(1)} %collective-permute-done.2.rest_4_), channel_id=1, source_target_pairs={{0,8},{8,0},{16,24},{24,16},{32,40},{40,32},{48,56},{56,48},{64,72... | collective-permute-start | bytes 786440 | tf_op jit(solution)/shard_map/key_far_twin/ppermute | solution.py:401
  55.3 0.0 collective-permute-done.10.refs_0_.rest_1_
  55.3 0.0 collective-permute-start.13
  55.3 2.9 %collective-permute-done.7.rest_2_ = bf16[2,64,1024]{2,1,0:T(8,128)(2,1)S(1)} collective-permute-done((bf16[2,64,1024]{2,1,0:T(8,128)(2,1)S(1)}, bf16[2,64,1024]{2,1,0:T(8,128)(2,1)S(1)}, u32[]{:S(2)}, u32[]{:S(2)}) %collective-permute-start.7) | collective-permute-done | bytes 262176 | tf_op jit(solution)/shard_map/season_far/ppermute | solution.py:401
  58.2 0.0 collective-permute-done.8.rest_7_.rest_3_
  58.2 0.0 collective-permute-done.9.rest_9_.rest_6_.rest_4_
  58.2 1.2 %collective-permute-start.14 = (bf16[2,64,1024]{2,1,0:T(8,128)(2,1)S(1)}, bf16[2,64,1024]{2,1,0:T(8,128)(2,1)S(1)}, u32[]{:S(2)}, u32[]{:S(2)}) collective-permute-start(bf16[2,64,1024]{2,1,0:T(8,128)(2,1)S(1)} %collective-permute-done.7.rest_2_), channel_id=1, source_target_pairs={{0,8},{8,0},{16,24},{24,16},{32,40},{40,32},{48,56},{56,48},{64,72... | collective-permute-start | bytes 786440 | tf_op jit(solution)/shard_map/season_far_twin/ppermute | solution.py:401
  59.4 0.0 copy-start.1
  59.4 4.3 %collective-permute-start.18 = (bf16[3,64,1024]{2,1,0:T(8,128)(2,1)S(1)}, bf16[3,64,1024]{2,1,0:T(8,128)(2,1)S(1)}, u32[]{:S(2)}, u32[]{:S(2)}) collective-permute-start(bf16[3,64,1024]{2,1,0:T(8,128)(2,1)S(1)} %join.1), channel_id=1, source_target_pairs={{0,2},{8,10},{16,18},{24,26},{32,34},{40,42},{48,50},{56,58},{64,6... | collective-permute-start | bytes 1179656 | tf_op jit(solution)/shard_map/query_far/ppermute | solution.py:401
  63.7 0.0 collective-permute-done.12.rest_10_
  63.7 0.0 collective-permute-done.13.rest_11_
  63.8 3.4 %attend.1 = (bf16[2,64,1024]{2,1,0:T(8,128)(2,1)S(1)}, f32[2,64,128]{2,1,0:T(8,128)S(1)}) custom-call(s32[2]{0:T(128)S(1)} %pad_add_fusion.here_ref, s32[8,32]{1,0:T(8,128)S(1)} %copy-done.8, bf16[2,64,1024]{2,1,0:T(8,128)(2,1)S(1)} %bitcast.18, bf16[2,64,1024]{2,1,0:T(8,128)(2,1)S(1)} %bitcast.24, bf16[2,64,1024]{2,1,0:T(8,128)(2,1)S(1)} %bitcast.31, ...), custom_call_target="tpu_custom_call" | custom-call | flops 2400000000 | bytes 6000000 | tf_op jit(solution)/shard_map/attend/pallas_call | solution.py:455
  67.2 0.0 collective-permute-done.14.rest_7_
  67.2 0.0 copy-start.9
  67.2 0.7 copy-done.9
  67.9 2.9 %contrast.1 = (f32[2,64]{1,0:T(2,128)}, bf16[2,64,1152]{2,1,0:T(8,128)(2,1)S(1)}, f32[2,64,128]{2,1,0:T(8,128)S(1)}) custom-call(s32[2]{0:T(128)S(1)} %pad_add_fusion.here_ref, s32[8,32]{1,0:T(8,128)S(1)} %copy-done.8, bf16[2,64,1024]{2,1,0:T(8,128)(2,1)S(1)} %get-tuple-element.64.att_ref, f32[2,64,128]{2,1,0:T(8,128)S(1)} %get-tuple-element.65.stat_ref, ...), custom_call_target="tpu_custom_call" | custom-call | flops 1200000000 | bytes 6000000 | tf_op jit(solution)/shard_map/contrast/pallas_call | solution.py:464
  70.8 0.7 collective-permute-start.15
  71.5 1.9 %collective-permute-start.16 = (bf16[1,64,1152]{2,1,0:T(8,128)(2,1)S(1)}, bf16[1,64,1152]{2,1,0:T(8,128)(2,1)S(1)}, u32[]{:S(2)}, u32[]{:S(2)}) collective-permute-start(bf16[1,64,1152]{2,1,0:T(8,128)(2,1)S(1)} %slice.3), channel_id=1, source_target_pairs={{0,121},{8,17},{16,9},{24,33},{32,25},{40,49},{48,41},{56,65},{64,... | collective-permute-start | bytes 442376 | tf_op jit(solution)/shard_map/grad_cor/ppermute | solution.py:401
  73.4 0.4 collective-permute-start.17
  73.8 4.4 %query_grads.1 = bf16[2,64,1024]{2,1,0:T(8,128)(2,1)} custom-call(s32[2]{0:T(128)S(1)} %pad_add_fusion.here_ref, s32[8,32]{1,0:T(8,128)S(1)} %copy-done.8, bf16[2,64,1024]{2,1,0:T(8,128)(2,1)S(1)} %bitcast.19, bf16[2,64,1152]{2,1,0:T(8,128)(2,1)S(1)} %get-tuple-element.68.grad_ref.rest_6_, f32[2,64,128]{2,1,0:T(8,128)S(1)} %get-tuple-element.71.stats_ref, ...), custom_call_target="tpu_custom_call" | custom-call | flops 3600000000 | bytes 6000000 | tf_op jit(solution)/shard_map/query_grads/pallas_call | solution.py:477
  78.3 6.2 %collective-permute-done.16.cor_ref.rest_9_ = bf16[1,64,1152]{2,1,0:T(8,128)(2,1)S(1)} collective-permute-done((bf16[1,64,1152]{2,1,0:T(8,128)(2,1)S(1)}, bf16[1,64,1152]{2,1,0:T(8,128)(2,1)S(1)}, u32[]{:S(2)}, u32[]{:S(2)}) %collective-permute-start.16) | collective-permute-done | bytes 147488 | tf_op jit(solution)/shard_map/grad_cor/ppermute | solution.py:401
  84.5 0.0 collective-permute-done.15.swap_ref.rest_7_
  84.5 0.1 grad_pack.1
  84.5 2.4 %collective-permute-start.22 = (bf16[2,64,1152]{2,1,0:T(8,128)(2,1)S(1)}, bf16[2,64,1152]{2,1,0:T(8,128)(2,1)S(1)}, u32[]{:S(2)}, u32[]{:S(2)}) collective-permute-start(bf16[2,64,1152]{2,1,0:T(8,128)(2,1)S(1)} %get-tuple-element.79), channel_id=1, source_target_pairs={{0,8},{8,0},{16,24},{24,16},{32,40},{40,32},{48,56},{56,48},{64,72... | collective-permute-start | bytes 884744 | tf_op jit(solution)/shard_map/grad_twin/ppermute | solution.py:401
  87.0 0.1 collective-permute-start.21
  87.1 2.9 %collective-permute-start.19 = (bf16[3,64,1152]{2,1,0:T(8,128)(2,1)S(1)}, bf16[3,64,1152]{2,1,0:T(8,128)(2,1)S(1)}, u32[]{:S(2)}, u32[]{:S(2)}) collective-permute-start(bf16[3,64,1152]{2,1,0:T(8,128)(2,1)S(1)} %get-tuple-element.75), channel_id=1, source_target_pairs={{0,2},{8,10},{16,18},{24,26},{32,34},{40,42},{48,50},{56,58},{64,6... | collective-permute-start | bytes 1327112 | tf_op jit(solution)/shard_map/grad_far/ppermute | solution.py:401
  90.0 0.8 collective-permute-start.20
  90.8 0.0 collective-permute-done.21.rest_5_
  90.8 0.0 collective-permute-done.22.rest_10_
  90.8 3.4 %inner_key_grads.1 = (f32[2,64,1024]{2,1,0:T(8,128)S(1)}, f32[2,64,1024]{2,1,0:T(8,128)S(1)}) custom-call(s32[2]{0:T(128)S(1)} %pad_add_fusion.here_ref, s32[8,32]{1,0:T(8,128)S(1)} %copy-done.8, bf16[2,64,1024]{2,1,0:T(8,128)(2,1)S(1)} %bitcast.26, bf16[2,64,1024]{2,1,0:T(8,128)(2,1)S(1)} %bitcast.33, bf16[2,64,1024]{2,1,0:T(8,128)(2,1)S(1)} %bitcast.20, ...), custom_call_target="tpu_custom_call" | custom-call | flops 3200000000 | bytes 6000000 | tf_op jit(solution)/shard_map/inner_key_grads/pallas_call | solution.py:502
  94.2 4.9 %collective-permute-done.19.rest_2_ = bf16[3,64,1152]{2,1,0:T(8,128)(2,1)S(1)} collective-permute-done((bf16[3,64,1152]{2,1,0:T(8,128)(2,1)S(1)}, bf16[3,64,1152]{2,1,0:T(8,128)(2,1)S(1)}, u32[]{:S(2)}, u32[]{:S(2)}) %collective-permute-start.19) | collective-permute-done | bytes 442400 | tf_op jit(solution)/shard_map/grad_far/ppermute | solution.py:401
  99.1 1.2 %collective-permute-start.23 = (bf16[3,64,1152]{2,1,0:T(8,128)(2,1)S(1)}, bf16[3,64,1152]{2,1,0:T(8,128)(2,1)S(1)}, u32[]{:S(2)}, u32[]{:S(2)}) collective-permute-start(bf16[3,64,1152]{2,1,0:T(8,128)(2,1)S(1)} %collective-permute-done.19.rest_2_), channel_id=1, source_target_pairs={{0,8},{8,0},{16,24},{24,16},{32,40},{40,32},{48,56},{56,48},{64,72... | collective-permute-start | bytes 1327112 | tf_op jit(solution)/shard_map/grad_last_twin/ppermute | solution.py:401
  100.3 1.4 %collective-permute-done.23.rest_3_ = bf16[3,64,1152]{2,1,0:T(8,128)(2,1)S(1)} collective-permute-done((bf16[3,64,1152]{2,1,0:T(8,128)(2,1)S(1)}, bf16[3,64,1152]{2,1,0:T(8,128)(2,1)S(1)}, u32[]{:S(2)}, u32[]{:S(2)}) %collective-permute-start.23) | collective-permute-done | bytes 442400 | tf_op jit(solution)/shard_map/grad_last_twin/ppermute | solution.py:401
  101.8 3.3 %outer_key_grads.1 = (bf16[2,64,1024]{2,1,0:T(8,128)(2,1)}, bf16[2,64,1024]{2,1,0:T(8,128)(2,1)}) custom-call(s32[2]{0:T(128)S(1)} %pad_add_fusion.here_ref, s32[8,32]{1,0:T(8,128)S(1)} %copy-done.8, bf16[2,64,1024]{2,1,0:T(8,128)(2,1)S(1)} %bitcast.27, bf16[2,64,1024]{2,1,0:T(8,128)(2,1)S(1)} %bitcast.34, f32[2,64,1024]{2,1,0:T(8,128)S(1)} %get-tuple-element.82.ksum_ref, ...), custom_call_target="tpu_custom_call" | custom-call | flops 1600000000 | bytes 6000000 | tf_op jit(solution)/shard_map/outer_key_grads/pallas_call | solution.py:516
  (15 shorter events, 0.1 us)
Async XLA Ops:
  0.6 9.4 %collective-permute-start = (bf16[2,64,1024]{2,1,0:T(8,128)(2,1)}, bf16[2,64,1024]{2,1,0:T(8,128)(2,1)S(1)}, u32[]{:S(2)}, u32[]{:S(2)}) collective-permute-start(bf16[2,64,1024]{2,1,0:T(8,128)(2,1)} %bitcast.21), channel_id=1, source_target_pairs={{0,1},{8,9},{16,17},{24,25},{32,33},{40,41},{48,49},{56,57},{64,65... | collective-permute-start | bytes 786440 | tf_op jit(solution)/shard_map/key_swap/ppermute | solution.py:401
  4.3 11.4 %collective-permute-start.1 = (bf16[2,64,1024]{2,1,0:T(8,128)(2,1)}, bf16[2,64,1024]{2,1,0:T(8,128)(2,1)S(1)}, u32[]{:S(2)}, u32[]{:S(2)}) collective-permute-start(bf16[2,64,1024]{2,1,0:T(8,128)(2,1)} %bitcast.28), channel_id=1, source_target_pairs={{0,1},{8,9},{16,17},{24,25},{32,33},{40,41},{48,49},{56,57},{64,65... | collective-permute-start | bytes 786440 | tf_op jit(solution)/shard_map/value_swap/ppermute | solution.py:401
  4.5 0.9 copy-start
  5.4 0.9 copy-start.2
  6.4 0.9 copy-start.4
  7.3 0.9 copy-start.6
  15.7 22.3 %collective-permute-start.6 = (bf16[4,64,1024]{2,1,0:T(8,128)(2,1)S(1)}, bf16[4,64,1024]{2,1,0:T(8,128)(2,1)S(1)}, u32[]{:S(2)}, u32[]{:S(2)}) collective-permute-start(bf16[4,64,1024]{2,1,0:T(8,128)(2,1)S(1)} %get-tuple-element.52), channel_id=1, source_target_pairs={{0,120},{8,16},{16,8},{24,32},{32,24},{40,48},{48,40},{56,64},{64,... | collective-permute-start | bytes 1572872 | tf_op jit(solution)/shard_map/all_off/ppermute | solution.py:401
  18.7 19.3 %collective-permute-start.5 = (bf16[3,64,1024]{2,1,0:T(8,128)(2,1)S(1)}, bf16[3,64,1024]{2,1,0:T(8,128)(2,1)S(1)}, u32[]{:S(2)}, u32[]{:S(2)}) collective-permute-start(bf16[3,64,1024]{2,1,0:T(8,128)(2,1)S(1)} %get-tuple-element.51), channel_id=1, source_target_pairs={{0,121},{8,17},{16,9},{24,33},{32,25},{40,49},{48,41},{56,65},{64,... | collective-permute-start | bytes 1179656 | tf_op jit(solution)/shard_map/kvs_cor/ppermute | solution.py:401
  20.0 7.2 %collective-permute-start.2 = (bf16[2,64,1024]{2,1,0:T(8,128)(2,1)S(1)}, bf16[2,64,1024]{2,1,0:T(8,128)(2,1)S(1)}, u32[]{:S(2)}, u32[]{:S(2)}) collective-permute-start(bf16[2,64,1024]{2,1,0:T(8,128)(2,1)S(1)} %collective-permute-done.refs_4_.rest_2_), channel_id=1, source_target_pairs={{0,2},{8,10},{16,18},{24,26},{32,34},{40,42},{48,50},{56,58},{64,6... | collective-permute-start | bytes 786440 | tf_op jit(solution)/shard_map/key_far/ppermute | solution.py:401
  23.5 9.6 %collective-permute-start.3 = (bf16[2,64,1024]{2,1,0:T(8,128)(2,1)S(1)}, bf16[2,64,1024]{2,1,0:T(8,128)(2,1)S(1)}, u32[]{:S(2)}, u32[]{:S(2)}) collective-permute-start(bf16[2,64,1024]{2,1,0:T(8,128)(2,1)S(1)} %collective-permute-done.1.refs_5_.rest_3_), channel_id=1, source_target_pairs={{0,2},{8,10},{16,18},{24,26},{32,34},{40,42},{48,50},{56,58},{64,6... | collective-permute-start | bytes 786440 | tf_op jit(solution)/shard_map/value_far/ppermute | solution.py:401
  27.1 10.9 %collective-permute-start.4 = (bf16[2,64,1024]{2,1,0:T(8,128)(2,1)S(1)}, bf16[2,64,1024]{2,1,0:T(8,128)(2,1)S(1)}, u32[]{:S(2)}, u32[]{:S(2)}) collective-permute-start(bf16[2,64,1024]{2,1,0:T(8,128)(2,1)S(1)} %bitcast.12), channel_id=1, source_target_pairs={{0,1},{8,9},{16,17},{24,25},{32,33},{40,41},{48,49},{56,57},{64,65... | collective-permute-start | bytes 786440 | tf_op jit(solution)/shard_map/season_swap/ppermute | solution.py:401
  38.0 25.8 %copy-start.8 = (s32[8,32]{1,0:T(8,128)S(1)}, s32[8,32]{1,0:T(8,128)}, u32[]{:S(2)}) copy-start(s32[8,32]{1,0:T(8,128)} %cloud_ref.9) | copy-start | bytes 3076
  38.6 25.1 %copy-start.3 = (bf16[1,2,64,1024]{3,2,1,0:T(8,128)(2,1)S(1)}, bf16[1,2,64,1024]{3,2,1,0:T(8,128)(2,1)}, u32[]{:S(2)}) copy-start(bf16[1,2,64,1024]{3,2,1,0:T(8,128)(2,1)} %param.6) | copy-start | bytes 786436
  38.6 25.1 %copy-start.5 = (bf16[1,2,64,1024]{3,2,1,0:T(8,128)(2,1)S(1)}, bf16[1,2,64,1024]{3,2,1,0:T(8,128)(2,1)}, u32[]{:S(2)}) copy-start(bf16[1,2,64,1024]{3,2,1,0:T(8,128)(2,1)} %param.7) | copy-start | bytes 786436
  38.6 25.1 %copy-start.7 = (bf16[1,2,64,1024]{3,2,1,0:T(8,128)(2,1)S(1)}, bf16[1,2,64,1024]{3,2,1,0:T(8,128)(2,1)}, u32[]{:S(2)}) copy-start(bf16[1,2,64,1024]{3,2,1,0:T(8,128)(2,1)} %param.8) | copy-start | bytes 786436
  38.6 19.6 %collective-permute-start.9 = (bf16[7,64,1024]{2,1,0:T(8,128)(2,1)S(1)}, bf16[7,64,1024]{2,1,0:T(8,128)(2,1)S(1)}, u32[]{:S(2)}, u32[]{:S(2)}) collective-permute-start(bf16[7,64,1024]{2,1,0:T(8,128)(2,1)S(1)} %faces.1), channel_id=1, source_target_pairs={{0,8},{8,0},{16,24},{24,16},{32,40},{40,32},{48,56},{56,48},{64,72... | collective-permute-start | bytes 2752520 | tf_op jit(solution)/shard_map/inner_twin/ppermute | solution.py:401
  40.8 14.5 %collective-permute-start.10 = (bf16[2,64,1024]{2,1,0:T(8,128)(2,1)S(1)}, bf16[2,64,1024]{2,1,0:T(8,128)(2,1)S(1)}, u32[]{:S(2)}, u32[]{:S(2)}) collective-permute-start(bf16[2,64,1024]{2,1,0:T(8,128)(2,1)S(1)} %bitcast.17), channel_id=1, source_target_pairs={{0,1},{8,9},{16,17},{24,25},{32,33},{40,41},{48,49},{56,57},{64,65... | collective-permute-start | bytes 786440 | tf_op jit(solution)/shard_map/query_swap/ppermute | solution.py:401
  40.9 17.3 %collective-permute-start.8 = (bf16[3,64,1024]{2,1,0:T(8,128)(2,1)S(1)}, bf16[3,64,1024]{2,1,0:T(8,128)(2,1)S(1)}, u32[]{:S(2)}, u32[]{:S(2)}) collective-permute-start(bf16[3,64,1024]{2,1,0:T(8,128)(2,1)S(1)} %collective-permute-done.5.rest_6_.rest_5_), channel_id=1, source_target_pairs={{0,2},{8,10},{16,18},{24,26},{32,34},{40,42},{48,50},{56,58},{64,6... | collective-permute-start | bytes 1179656 | tf_op jit(solution)/shard_map/kvs_far/ppermute | solution.py:401
  44.5 8.9 %collective-permute-start.11 = (bf16[1,64,1024]{2,1,0:T(8,128)(2,1)S(1)}, bf16[1,64,1024]{2,1,0:T(8,128)(2,1)S(1)}, u32[]{:S(2)}, u32[]{:S(2)}) collective-permute-start(bf16[1,64,1024]{2,1,0:T(8,128)(2,1)S(1)} %get-tuple-element.60), channel_id=1, source_target_pairs={{0,121},{8,17},{16,9},{24,33},{32,25},{40,49},{48,41},{56,65},{64,... | collective-permute-start | bytes 393224 | tf_op jit(solution)/shard_map/query_cor/ppermute | solution.py:401
  44.6 13.6 %collective-permute-start.7 = (bf16[2,64,1024]{2,1,0:T(8,128)(2,1)S(1)}, bf16[2,64,1024]{2,1,0:T(8,128)(2,1)S(1)}, u32[]{:S(2)}, u32[]{:S(2)}) collective-permute-start(bf16[2,64,1024]{2,1,0:T(8,128)(2,1)S(1)} %collective-permute-done.4.refs_6_.rest_1_), channel_id=1, source_target_pairs={{0,2},{8,10},{16,18},{24,26},{32,34},{40,42},{48,50},{56,58},{64,6... | collective-permute-start | bytes 786440 | tf_op jit(solution)/shard_map/season_far/ppermute | solution.py:401
  53.4 10.3 %collective-permute-start.12 = (bf16[2,64,1024]{2,1,0:T(8,128)(2,1)S(1)}, bf16[2,64,1024]{2,1,0:T(8,128)(2,1)S(1)}, u32[]{:S(2)}, u32[]{:S(2)}) collective-permute-start(bf16[2,64,1024]{2,1,0:T(8,128)(2,1)S(1)} %collective-permute-done.2.rest_4_), channel_id=1, source_target_pairs={{0,8},{8,0},{16,24},{24,16},{32,40},{40,32},{48,56},{56,48},{64,72... | collective-permute-start | bytes 786440 | tf_op jit(solution)/shard_map/key_far_twin/ppermute | solution.py:401
  55.3 8.4 %collective-permute-start.13 = (bf16[2,64,1024]{2,1,0:T(8,128)(2,1)S(1)}, bf16[2,64,1024]{2,1,0:T(8,128)(2,1)S(1)}, u32[]{:S(2)}, u32[]{:S(2)}) collective-permute-start(bf16[2,64,1024]{2,1,0:T(8,128)(2,1)S(1)} %collective-permute-done.3.rest_5_), channel_id=1, source_target_pairs={{0,8},{8,0},{16,24},{24,16},{32,40},{40,32},{48,56},{56,48},{64,72... | collective-permute-start | bytes 786440 | tf_op jit(solution)/shard_map/value_far_twin/ppermute | solution.py:401
  58.2 9.0 %collective-permute-start.14 = (bf16[2,64,1024]{2,1,0:T(8,128)(2,1)S(1)}, bf16[2,64,1024]{2,1,0:T(8,128)(2,1)S(1)}, u32[]{:S(2)}, u32[]{:S(2)}) collective-permute-start(bf16[2,64,1024]{2,1,0:T(8,128)(2,1)S(1)} %collective-permute-done.7.rest_2_), channel_id=1, source_target_pairs={{0,8},{8,0},{16,24},{24,16},{32,40},{40,32},{48,56},{56,48},{64,72... | collective-permute-start | bytes 786440 | tf_op jit(solution)/shard_map/season_far_twin/ppermute | solution.py:401
  59.4 7.8 %copy-start.1 = (bf16[1,2,64,1024]{3,2,1,0:T(8,128)(2,1)S(1)}, bf16[1,2,64,1024]{3,2,1,0:T(8,128)(2,1)}, u32[]{:S(2)}) copy-start(bf16[1,2,64,1024]{3,2,1,0:T(8,128)(2,1)} %param.9) | copy-start | bytes 786436
  59.4 18.8 %collective-permute-start.18 = (bf16[3,64,1024]{2,1,0:T(8,128)(2,1)S(1)}, bf16[3,64,1024]{2,1,0:T(8,128)(2,1)S(1)}, u32[]{:S(2)}, u32[]{:S(2)}) collective-permute-start(bf16[3,64,1024]{2,1,0:T(8,128)(2,1)S(1)} %join.1), channel_id=1, source_target_pairs={{0,2},{8,10},{16,18},{24,26},{32,34},{40,42},{48,50},{56,58},{64,6... | collective-permute-start | bytes 1179656 | tf_op jit(solution)/shard_map/query_far/ppermute | solution.py:401
  67.2 0.7 copy-start.9
  70.8 13.7 %collective-permute-start.15 = (bf16[2,64,1152]{2,1,0:T(8,128)(2,1)S(1)}, bf16[2,64,1152]{2,1,0:T(8,128)(2,1)S(1)}, u32[]{:S(2)}, u32[]{:S(2)}) collective-permute-start(bf16[2,64,1152]{2,1,0:T(8,128)(2,1)S(1)} %get-tuple-element.68.grad_ref.rest_6_), channel_id=1, source_target_pairs={{0,1},{8,9},{16,17},{24,25},{32,33},{40,41},{48,49},{56,57},{64,65... | collective-permute-start | bytes 884744 | tf_op jit(solution)/shard_map/grad_swap/ppermute | solution.py:401
  71.5 12.9 %collective-permute-start.16 = (bf16[1,64,1152]{2,1,0:T(8,128)(2,1)S(1)}, bf16[1,64,1152]{2,1,0:T(8,128)(2,1)S(1)}, u32[]{:S(2)}, u32[]{:S(2)}) collective-permute-start(bf16[1,64,1152]{2,1,0:T(8,128)(2,1)S(1)} %slice.3), channel_id=1, source_target_pairs={{0,121},{8,17},{16,9},{24,33},{32,25},{40,49},{48,41},{56,65},{64,... | collective-permute-start | bytes 442376 | tf_op jit(solution)/shard_map/grad_cor/ppermute | solution.py:401
  73.4 11.1 %collective-permute-start.17 = (bf16[1,64,1152]{2,1,0:T(8,128)(2,1)S(1)}, bf16[1,64,1152]{2,1,0:T(8,128)(2,1)S(1)}, u32[]{:S(2)}, u32[]{:S(2)}) collective-permute-start(bf16[1,64,1152]{2,1,0:T(8,128)(2,1)S(1)} %slice.3), channel_id=1, source_target_pairs={{0,120},{8,16},{16,8},{24,32},{32,24},{40,48},{48,40},{56,64},{64,... | collective-permute-start | bytes 442376 | tf_op jit(solution)/shard_map/grad_off/ppermute | solution.py:401
  84.5 6.2 %collective-permute-start.22 = (bf16[2,64,1152]{2,1,0:T(8,128)(2,1)S(1)}, bf16[2,64,1152]{2,1,0:T(8,128)(2,1)S(1)}, u32[]{:S(2)}, u32[]{:S(2)}) collective-permute-start(bf16[2,64,1152]{2,1,0:T(8,128)(2,1)S(1)} %get-tuple-element.79), channel_id=1, source_target_pairs={{0,8},{8,0},{16,24},{24,16},{32,40},{40,32},{48,56},{56,48},{64,72... | collective-permute-start | bytes 884744 | tf_op jit(solution)/shard_map/grad_twin/ppermute | solution.py:401
  87.0 3.8 %collective-permute-start.21 = (bf16[2,64,1024]{2,1,0:T(8,128)(2,1)S(1)}, bf16[2,64,1024]{2,1,0:T(8,128)(2,1)S(1)}, u32[]{:S(2)}, u32[]{:S(2)}) collective-permute-start(bf16[2,64,1024]{2,1,0:T(8,128)(2,1)S(1)} %collective-permute-done.10.refs_0_.rest_1_), channel_id=1, source_target_pairs={{0,8},{8,0},{16,24},{24,16},{32,40},{40,32},{48,56},{56,48},{64,72... | collective-permute-start | bytes 786440 | tf_op jit(solution)/shard_map/query_twin/ppermute | solution.py:401
  87.1 12.0 %collective-permute-start.19 = (bf16[3,64,1152]{2,1,0:T(8,128)(2,1)S(1)}, bf16[3,64,1152]{2,1,0:T(8,128)(2,1)S(1)}, u32[]{:S(2)}, u32[]{:S(2)}) collective-permute-start(bf16[3,64,1152]{2,1,0:T(8,128)(2,1)S(1)} %get-tuple-element.75), channel_id=1, source_target_pairs={{0,2},{8,10},{16,18},{24,26},{32,34},{40,42},{48,50},{56,58},{64,6... | collective-permute-start | bytes 1327112 | tf_op jit(solution)/shard_map/grad_far/ppermute | solution.py:401
  90.0 4.2 %collective-permute-start.20 = (bf16[3,64,1024]{2,1,0:T(8,128)(2,1)S(1)}, bf16[3,64,1024]{2,1,0:T(8,128)(2,1)S(1)}, u32[]{:S(2)}, u32[]{:S(2)}) collective-permute-start(bf16[3,64,1024]{2,1,0:T(8,128)(2,1)S(1)} %collective-permute-done.18.rest_0_), channel_id=1, source_target_pairs={{0,8},{8,0},{16,24},{24,16},{32,40},{40,32},{48,56},{56,48},{64,72... | collective-permute-start | bytes 1179656 | tf_op jit(solution)/shard_map/query_far_twin/ppermute | solution.py:401
  99.1 2.7 %collective-permute-start.23 = (bf16[3,64,1152]{2,1,0:T(8,128)(2,1)S(1)}, bf16[3,64,1152]{2,1,0:T(8,128)(2,1)S(1)}, u32[]{:S(2)}, u32[]{:S(2)}) collective-permute-start(bf16[3,64,1152]{2,1,0:T(8,128)(2,1)S(1)} %collective-permute-done.19.rest_2_), channel_id=1, source_target_pairs={{0,8},{8,0},{16,24},{24,16},{32,40},{40,32},{48,56},{56,48},{64,72... | collective-permute-start | bytes 1327112 | tf_op jit(solution)/shard_map/grad_last_twin/ppermute | solution.py:401

commit v4 on v3

--- a/solution.py
+++ b/solution.py
@@ -67,13 +67,11 @@
     return lax.optimization_barrier(values)
 
 
-def region(own, swap, far, off, cor, twins, n, side=0, inner=(0, 1, 2), corner=None):
-    far, edge = far if isinstance(far, tuple) else (far, None)
-    corner = side if corner is None else corner
+def region(own, swap, far, off, cor, twins, n, inner):
     return (
-        ((off, side), (own, n), (own, 1 - n), (twins[0], inner[0])),
-        ((cor, corner), (swap, n), (swap, 1 - n), (twins[1], inner[1])),
-        ((far, 2) if edge is None else (edge, corner), (far, n), (far, 1 - n), (twins[2], inner[2])),
+        ((off, 0), (own, n), (own, 1 - n), (twins[0], inner[0])),
+        ((cor, 0), (swap, n), (swap, 1 - n), (twins[1], inner[1])),
+        ((far, 2), (far, n), (far, 1 - n), (twins[2], inner[2])),
     )
 
 
@@ -147,24 +145,28 @@
         at += size
 
 
-def edges_kernel(here_ref, k_ref, v_ref, s_ref, q_ref, cor_ref, qn_ref, off_ref, sems):
+def edges_kernel(here_ref, pair_ref, k_ref, v_ref, s_ref, q_ref, off_ref, qn_ref, pair_out, sems):
     n = here_ref[1] % 2
     copies = [
-        pltpu.make_async_copy(ref.at[n], off_ref.at[i], sems.at[i])
+        pltpu.make_async_copy(
+            ref.at[n], off_ref.at[i] if i < 3 else qn_ref.at[0], sems.at[i]
+        )
         for i, ref in enumerate((k_ref, v_ref, s_ref, q_ref))
     ]
     for c in copies:
         c.start()
+    pair_out[...] = pair_ref[...]
     for c in copies:
         c.wait()
-    cor_ref[...] = off_ref[0:3]
-    qn_ref[0] = off_ref[3]
-
-
-def faces_kernel(here_ref, *refs):
+
+
+def pack_kernel(here_ref, k_ref, v_ref, s_ref, q_ref, ks_ref, vs_ref, ss_ref, kf_ref, vf_ref, cor_ref,
+                far_ref, face_ref):
     n = here_ref[1] % 2
-    for i, ref in enumerate(refs[:-1]):
-        refs[-1][i] = ref[1 - n]
+    far_ref[0:2] = ss_ref[...]
+    far_ref[2:5] = cor_ref[...]
+    for i, ref in enumerate((k_ref, v_ref, s_ref, q_ref, ks_ref, vs_ref, ss_ref, kf_ref, vf_ref)):
+        face_ref[i] = ref[1 - n]
 
 
 def grad_pack_kernel(grad_ref, swap_ref, cor_ref, far_ref, face_ref):
@@ -175,17 +177,21 @@
 
 
 def key_value_tables(refs, n):
-    k, v, k_swap, v_swap, k_far, v_far, cor, edge, off, twin, k_far_twin, v_far_twin = refs
-    return (
-        region(k, k_swap, (k_far, edge), off, cor, (twin, twin, k_far_twin), n, 0, (0, 4, n)),
-        region(v, v_swap, (v_far, edge), off, cor, (twin, twin, v_far_twin), n, 1, (1, 5, n)),
-    )
+    k, v, k_swap, v_swap, k_far, v_far, far, cor, off, twin = refs
+    return [
+        (
+            ((off, i), (own, n), (own, 1 - n), (twin, i)),
+            ((cor, i), (swap, n), (swap, 1 - n), (twin, 4 + i)),
+            ((far, 2 + i), (outer, n), (outer, 1 - n), (twin, 7 + i)),
+        )
+        for i, (own, swap, outer) in enumerate(((k, k_swap, k_far), (v, v_swap, v_far)))
+    ]
 
 
 def attend_kernel(here_ref, cloud_ref, q_ref, *rest):
     n, _, clear = region_flags(here_ref, cloud_ref)
-    k_table, v_table = key_value_tables(rest[0:12], n)
-    att_ref, stat_ref = rest[12:]
+    k_table, v_table = key_value_tables(rest[0:10], n)
+    att_ref, stat_ref = rest[10:]
     for t in range(2):
         qt = n if t == 0 else 1 - n
         stat_ref[t] = jnp.zeros((PP, 128), F32)
@@ -213,10 +219,14 @@
 
 
 def contrast_kernel(here_ref, cloud_ref, att_ref, stat_ref, pair_ref, *rest):
-    loss_ref, grad_ref, stats_ref = rest[8:]
+    loss_ref, grad_ref, stats_ref = rest[7:]
     n, _, clear = region_flags(here_ref, cloud_ref)
-    s, swap, far, edge, off, cor, twin, far_twin = rest[0:8]
-    table = region(s, swap, (far, edge), off, cor, (twin, twin, far_twin), n, side=2, inner=(2, 6, n))
+    s, swap, far, off, cor, twin, far_twin = rest[0:7]
+    table = (
+        ((off, 2), (s, n), (s, 1 - n), (twin, 2)),
+        ((cor, 2), (swap, n), (swap, 1 - n), (twin, 6)),
+        ((far, 4), (far, n), (far, 1 - n), (far_twin, n)),
+    )
     season = jnp.concatenate([ref[index] for line in table for ref, index in line], axis=0)
     att = jnp.concatenate([att_ref[0], att_ref[1]], axis=0)
     side = lax.broadcasted_iota(jnp.int32, (2 * PP, REG), 0) < PP
@@ -277,8 +287,8 @@
 
 def query_kernel(here_ref, cloud_ref, q_ref, grad_ref, stats_ref, *rest):
     n, _, clear = region_flags(here_ref, cloud_ref)
-    k_table, v_table = key_value_tables(rest[0:12], n)
-    out_ref = rest[12]
+    k_table, v_table = key_value_tables(rest[0:10], n)
+    out_ref = rest[10]
     for t in range(2):
         qt = n if t == 0 else 1 - n
         mask = segments(query_flags(clear, t), NEG_FILL)
@@ -301,9 +311,9 @@
         lax.fori_loop(0, GROUPS, step, 0, unroll=True)
 
 
-def key_terms(flags, rows, k_ref, v_ref, n, q_table, g_table, rows_ref, finish):
+def key_terms(flags, rows, k_ref, v_ref, n, q_table, g_table, rows_ref, finish, blocks=(0, 1)):
     inside, clear = flags
-    for t in range(2):
+    for t in blocks:
         kt = n if t == 0 else 1 - n
         parts = jnp.transpose(window(g_table, t, slice(WIDTH, EXT), rows).astype(F32))
         stats = parts[0:32] + parts[32:64] + parts[64:96]
@@ -344,8 +354,8 @@
     q, q_swap, q_off, q_cor, own_twin, q_twin, g, g_swap, g_off, g_cor, g_twin = rest[0:11]
     ksum_ref, vsum_ref, rows_ref = rest[11:]
     n, inside, clear = region_flags(here_ref, cloud_ref)
-    q_table = region(q, q_swap, None, q_off, q_cor, (own_twin, q_twin, None), n, side=3, inner=(3, n, None), corner=0)
-    g_table = region(g, g_swap, None, g_off, g_cor, (g_twin, g_twin, None), 0, inner=(0, 1, None))
+    q_table = region(q, q_swap, None, q_off, q_cor, (own_twin, q_twin, None), n, (3, n, None))
+    g_table = region(g, g_swap, None, g_off, g_cor, (g_twin, g_twin, None), 0, (0, 1, None))
 
     def finish(t, kt, fs, dk, dv):
         ksum_ref[t, :, fs] = dk
@@ -354,18 +364,32 @@
     key_terms((inside, clear), (0, 1), k_ref, v_ref, n, q_table, g_table, rows_ref, finish)
 
 
-def outer_key_kernel(here_ref, cloud_ref, k_ref, v_ref, ksum_ref, vsum_ref, *rest):
-    q_far, q_twin, g_far, g_twin = rest[0:4]
-    kout_ref, vout_ref, rows_ref = rest[4:]
+def outer_near_kernel(here_ref, cloud_ref, k_ref, v_ref, ksum_ref, vsum_ref, *rest):
+    q_far, g_far, kout_ref, vout_ref, rows_ref = rest
     n, inside, clear = region_flags(here_ref, cloud_ref)
-    q_table = region(None, None, q_far, None, None, (None, None, q_twin), n, inner=(n, n, n))
-    g_table = region(None, None, g_far, None, None, (None, None, g_twin), 0, inner=(1, 1, 1))
+    q_table = region(None, None, q_far, None, None, (None,) * 3, n, (None,) * 3)
+    g_table = region(None, None, g_far, None, None, (None,) * 3, 0, (None,) * 3)
+
+    def finish(t, kt, fs, dk, dv):
+        kout_ref[:, fs] = ((ksum_ref[t, :, fs] + dk) * SCALE).astype(BF)
+        vout_ref[:, fs] = (vsum_ref[t, :, fs] + dv).astype(BF)
+
+    key_terms((inside, clear), (2,), k_ref, v_ref, n, q_table, g_table, rows_ref, finish, (0,))
+
+
+def outer_face_kernel(here_ref, cloud_ref, k_ref, v_ref, ksum_ref, vsum_ref, *rest):
+    q_far, q_twin, g_far, g_twin, k_near_ref, v_near_ref, kout_ref, vout_ref, rows_ref = rest
+    n, inside, clear = region_flags(here_ref, cloud_ref)
+    kout_ref[n] = k_near_ref[...]
+    vout_ref[n] = v_near_ref[...]
+    q_table = region(None, None, q_far, None, None, (None, None, q_twin), n, (n, n, n))
+    g_table = region(None, None, g_far, None, None, (None, None, g_twin), 0, (1, 1, 1))
 
     def finish(t, kt, fs, dk, dv):
         kout_ref[kt, :, fs] = ((ksum_ref[t, :, fs] + dk) * SCALE).astype(BF)
         vout_ref[kt, :, fs] = (vsum_ref[t, :, fs] + dv).astype(BF)
 
-    key_terms((inside, clear), (2,), k_ref, v_ref, n, q_table, g_table, rows_ref, finish)
+    key_terms((inside, clear), (2,), k_ref, v_ref, n, q_table, g_table, rows_ref, finish, (1,))
 
 
 SMEM = pl.BlockSpec(memory_space=pltpu.SMEM)
@@ -373,7 +397,7 @@
 ANY = pl.BlockSpec(memory_space=pl.ANY)
 
 
-def call(kernel, name, in_specs, out_shape, scratch, flops):
+def call(kernel, name, in_specs, out_shape, scratch):
     return pl.pallas_call(
         kernel,
         name=name,
@@ -382,7 +406,7 @@
         out_specs=jax.tree.map(lambda _: VMEM, out_shape),
         scratch_shapes=scratch,
         compiler_params=pltpu.CompilerParams(vmem_limit_bytes=VMEM_LIMIT),
-        cost_estimate=pl.CostEstimate(flops=flops, bytes_accessed=6_000_000, transcendentals=0),
+        cost_estimate=pl.CostEstimate(flops=1000, bytes_accessed=1000, transcendentals=0),
     )
 
 
@@ -412,63 +436,59 @@
             [VMEM] * len(parts),
             shape((total,) + parts[0].shape[1:], parts[0].dtype),
             [],
-            1_000_000,
         )(*parts)
 
     k_swap = named("key", k, "swap")
     v_swap = named("value", v, "swap")
-    cor_near, q_near, nears = call(
+    edge, q_near, pair = call(
         edges_kernel,
         "edges",
-        [SMEM] + [ANY] * 4,
-        (shape((3, PP, WIDTH), BF), shape((1, PP, WIDTH), BF), shape((4, PP, WIDTH), BF)),
+        [SMEM, VMEM] + [ANY] * 4,
+        (
+            shape((3, PP, WIDTH), BF),
+            shape((1, PP, WIDTH), BF),
+            shape((2, PP), jnp.int32),
+        ),
         [pltpu.SemaphoreType.DMA((4,))],
-        1_000_000,
-    )(here, k, v, s, q)
-    k_swap, v_swap, s1, cor_near, nears = phase(k_swap, v_swap, s, cor_near, nears)
+    )(here, pairing[0], k, v, s, q)
+    k_swap, v_swap, s1, edge = phase(k_swap, v_swap, s, edge)
+    cor = named("kvs", edge, "cor")
     k_far = named("key", k_swap, "far")
     v_far = named("value", v_swap, "far")
     s_swap = named("season", s1, "swap")
-    cor = named("kvs", cor_near, "cor")
-    off = named("all", nears, "off")
-    k_far, v_far, s_swap, cor, off, q1, q_near = phase(k_far, v_far, s_swap, cor, off, q, q_near)
-    s_far = named("season", s_swap, "far")
-    edge = named("kvs", cor, "far")
+    k_far, v_far, cor, s_swap, edge, q1, q_near = phase(k_far, v_far, cor, s_swap, edge, q, q_near)
+    far_stack, faces = call(
+        pack_kernel,
+        "pack",
+        [SMEM] + [VMEM] * 10,
+        (shape((5, PP, WIDTH), BF), shape((9, PP, WIDTH), BF)),
+        [],
+    )(here, k, v, s, q, k_swap, v_swap, s_swap, k_far, v_far, cor)
+    far = named("season", far_stack, "far")
+    off = named("kvs", edge, "off")
     q_swap = named("query", q1, "swap")
     q_cor = named("query", q_near, "cor")
-    faces = call(
-        faces_kernel,
-        "faces",
-        [SMEM] + [VMEM] * 7,
-        shape((7, PP, WIDTH), BF),
-        [],
-        1_000_000,
-    )(here, k, v, s, q, k_swap, v_swap, s_swap)
-    twin = named("inner", faces, "twin")
-    s_far, edge, off, twin, q_swap, q_cor = phase(s_far, edge, off, twin, q_swap, q_cor)
-    k_far_twin = named("key_far", k_far, "twin")
-    v_far_twin = named("value_far", v_far, "twin")
-    s_far_twin = named("season_far", s_far, "twin")
+    twin = named("faces", faces, "twin")
+    twin, q_cor, off, q_swap, far = phase(twin, q_cor, off, q_swap, far)
+    far_twin = named("season_far", far, "twin")
     q_far = named("query", joined(q_swap, q_cor), "far")
-    kvp = (k, v, k_swap, v_swap, k_far, v_far, cor, edge, off, twin, k_far_twin, v_far_twin)
+    kvp = (k, v, k_swap, v_swap, k_far, v_far, far, cor, off, twin)
 
     att, stat = call(
         attend_kernel,
         "attend",
-        [SMEM, SMEM, VMEM] + [VMEM] * 12,
+        [SMEM, SMEM, VMEM] + [VMEM] * 10,
         (shape((2, PP, WIDTH), BF), shape((2, PP, 128), F32)),
         [],
-        2_400_000_000,
     )(here, cloud, q, *kvp)
 
     loss, grad, stats = call(
         contrast_kernel,
         "contrast",
-        [SMEM, SMEM, VMEM, VMEM, VMEM] + [VMEM] * 8,
+        [SMEM, SMEM, VMEM, VMEM, VMEM] + [VMEM] * 7,
         (shape((2, PP), F32), shape((2, PP, EXT), BF), shape((2, PP, 128), F32)),
         [],
-        1_200_000_000,
-    )(here, cloud, att, stat, pairing[0], s, s_swap, s_far, edge, off, cor, twin, s_far_twin)
+    )(here, cloud, att, stat, pair, s, s_swap, far, off, cor, twin, far_twin)
 
     g_near = grad[0:1]
     g_swap = named("grad", grad, "swap")
@@ -477,25 +497,24 @@
     query_grad = call(
         query_kernel,
         "query_grads",
-        [SMEM, SMEM, VMEM, VMEM, VMEM] + [VMEM] * 12,
+        [SMEM, SMEM, VMEM, VMEM, VMEM] + [VMEM] * 10,
         shape((2, PP, WIDTH), BF),
         [],
-        3_600_000_000,
     )(here, cloud, q, grad, stats, *kvp)
 
-    g_swap, g_cor, g_off, q_far, query_grad, q_swap1 = phase(
-        g_swap, g_cor, g_off, q_far, query_grad, q_swap
+    q_off = named("query", after(q_near, grad), "off")
+    g_swap, g_cor, g_off, q_off, q_far, query_grad, q_swap1 = phase(
+        g_swap, g_cor, g_off, q_off, q_far, query_grad, q_swap
     )
     q_swap_twin = named("query", q_swap1, "twin")
-    far, faces = call(
+    far_stack, faces = call(
         grad_pack_kernel,
         "grad_pack",
         [VMEM] * 3,
         (shape((3, PP, EXT), BF), shape((2, PP, EXT), BF)),
         [],
-        1_000_000,
     )(grad, g_swap, g_cor)
-    g_far = named("grad", far, "far")
+    g_far = named("grad", far_stack, "far")
     g_twin = named("grad", faces, "twin")
     q_far_twin = named("query_far", q_far, "twin")
 
@@ -505,22 +524,30 @@
         [SMEM, SMEM, VMEM, VMEM] + [VMEM] * 11,
         (shape((2, PP, WIDTH), F32), shape((2, PP, WIDTH), F32)),
         [pltpu.VMEM((2 * HEADS, 6 * PP), F32)],
-        3_200_000_000,
     )(
-        here, cloud, k, v, q, q_swap, off, q_cor, twin, q_swap_twin,
+        here, cloud, k, v, q, q_swap, q_off, q_cor, twin, q_swap_twin,
         grad, g_swap, g_off, g_cor, g_twin,
     )
 
     g_far, q_far_twin, key_sum, value_sum = phase(g_far, q_far_twin, key_sum, value_sum)
     g_last = named("grad_last", g_far, "twin")
+    k_near_grad, v_near_grad = call(
+        outer_near_kernel,
+        "outer_near_key_grads",
+        [SMEM, SMEM] + [VMEM] * 6,
+        (shape((PP, WIDTH), BF), shape((PP, WIDTH), BF)),
+        [pltpu.VMEM((2 * HEADS, 3 * PP), F32)],
+    )(here, cloud, k, v, key_sum, value_sum, q_far, g_far)
     key_grad, value_grad = call(
-        outer_key_kernel,
-        "outer_key_grads",
-        [SMEM, SMEM, VMEM, VMEM, VMEM, VMEM] + [VMEM] * 4,
+        outer_face_kernel,
+        "outer_face_key_grads",
+        [SMEM, SMEM] + [VMEM] * 10,
         (shape((2, PP, WIDTH), BF), shape((2, PP, WIDTH), BF)),
         [pltpu.VMEM((2 * HEADS, 3 * PP), F32)],
-        1_600_000_000,
-    )(here, cloud, k, v, key_sum, value_sum, q_far, q_far_twin, g_far, g_last)
+    )(
+        here, cloud, k, v, key_sum, value_sum, q_far, q_far_twin, g_far, g_last,
+        k_near_grad, v_near_grad,
+    )
 
     return (loss[None], query_grad[None], key_grad[None], value_grad[None])
 

time: 105 us -> 102 us (0.971)
  waiting for transfers between devices: 37.4 us -> 30.3 us
  starting transfers between devices: 42.7 us -> 45.9 us
    ppermute x24 -> x22, waiting for transfers between devices: 37.4 us -> 30.3 us  [move(): return lax.ppermute(x, AXES, way[kind])]
    ppermute x24 -> x22, starting transfers between devices: 42.7 us -> 45.9 us  [move(): return lax.ppermute(x, AXES, way[kind])]
    pallas_call x4 -> x5, Pallas kernels: 8.66 us -> 9.44 us  [the longest x1 3.38 us: body(): call(attend_kernel, 'attend', [SMEM, SMEM, VMEM] + [VMEM] * 10, (shape((2...]
  transfers between devices with their start and end apart: 24 -> 22, of which waited for: 9 -> 9; matrix products, arithmetic and copies ran while one was open for 0% -> 0% of each run, Pallas kernels for 15% -> 17%
where the time goes in v4:
time: 102 us
  starting transfers between devices  45.9 us (45%)
  waiting for transfers between devices  30.3 us (30%)
  Pallas kernels  20.3 us (20%)
  local copies, waits for them, and re-layouts  4.51 us (4%)
    ppermute x22, starting transfers between devices, move(): return lax.ppermute(x, AXES, way[kind])  45.9 us
    ppermute x22, waiting for transfers between devices, move(): return lax.ppermute(x, AXES, way[kind])  30.3 us
    unnamed x20, local copies, waits for them, and re-layouts  4.5 us
    pallas_call x1, Pallas kernels, body(): call(query_kernel, 'query_grads', [SMEM, SMEM, VMEM, VMEM, VMEM] + [VMEM]...  4.43 us
    pallas_call x1, Pallas kernels, body(): call(inner_key_kernel, 'inner_key_grads', [SMEM, SMEM, VMEM, VMEM] + [VME...  3.41 us
    pallas_call x1, Pallas kernels, body(): call(attend_kernel, 'attend', [SMEM, SMEM, VMEM] + [VMEM] * 10, (shape((2...  3.38 us
    pallas_call x1, Pallas kernels, body(): call(contrast_kernel, 'contrast', [SMEM, SMEM, VMEM, VMEM, VMEM] + [VMEM]...  2.92 us
    pallas_call x1, Pallas kernels, body(): call(outer_face_kernel, 'outer_face_key_grads', [SMEM, SMEM] + [VMEM] * 1...  2.46 us
  transfers between devices with their start and end apart: 22, of which 9 were waited for; matrix products, arithmetic and copies ran while one was open for 0% of the time, Pallas kernels for 17%

profile of v4, /device:TPU:1, one launch (start us, length us, event | category | flops | bytes accessed | tf_op | source)
XLA Modules:
  0.0 101.8 jit_solution(6717812478044357101)
XLA Ops:
  0.6 3.7 %collective-permute-start = (bf16[2,64,1024]{2,1,0:T(8,128)(2,1)}, bf16[2,64,1024]{2,1,0:T(8,128)(2,1)S(1)}, u32[]{:S(2)}, u32[]{:S(2)}) collective-permute-start(bf16[2,64,1024]{2,1,0:T(8,128)(2,1)} %bitcast.11), channel_id=1, source_target_pairs={{0,1},{8,9},{16,17},{24,25},{32,33},{40,41},{48,49},{56,57},{64,65... | collective-permute-start | bytes 786440 | tf_op jit(solution)/shard_map/key_swap/ppermute | solution.py:425
  4.3 0.1 collective-permute-start.1
  4.4 0.1 pad_add_fusion.here_ref
  4.5 0.9 copy-done
  5.4 0.9 copy-done.2
  6.4 0.9 copy-done.4
  7.3 0.9 copy-done.6
  8.3 0.7 copy-done.9
  8.9 1.3 %edges.1 = (bf16[3,64,1024]{2,1,0:T(8,128)(2,1)S(1)}, bf16[1,64,1024]{2,1,0:T(8,128)(2,1)S(1)}, s32[2,64]{1,0:T(2,128)S(1)}) custom-call(s32[2]{0:T(128)S(1)} %pad_add_fusion.here_ref, s32[2,64]{1,0:T(2,128)S(1)} %bitcast.37, bf16[2,64,1024]{2,1,0:T(8,128)(2,1)S(1)} %bitcast.12, bf16[2,64,1024]{2,1,0:T(8,128)(2,1)S(1)} %bitcast.20, ...), custom_call_target="tpu_custom_call" | custom-call | flops 1000 | bytes 1000 | tf_op jit(solution)/shard_map/edges/pallas_call | solution.py:443
  10.2 0.0 collective-permute-done.ks_ref.rest_2_
  10.2 5.4 %collective-permute-done.1.vs_ref.rest_3_ = bf16[2,64,1024]{2,1,0:T(8,128)(2,1)S(1)} collective-permute-done((bf16[2,64,1024]{2,1,0:T(8,128)(2,1)}, bf16[2,64,1024]{2,1,0:T(8,128)(2,1)S(1)}, u32[]{:S(2)}, u32[]{:S(2)}) %collective-permute-start.1) | collective-permute-done | bytes 262176 | tf_op jit(solution)/shard_map/value_swap/ppermute | solution.py:425
  15.7 4.3 %collective-permute-start.4 = (bf16[3,64,1024]{2,1,0:T(8,128)(2,1)S(1)}, bf16[3,64,1024]{2,1,0:T(8,128)(2,1)S(1)}, u32[]{:S(2)}, u32[]{:S(2)}) collective-permute-start(bf16[3,64,1024]{2,1,0:T(8,128)(2,1)S(1)} %get-tuple-element.62), channel_id=1, source_target_pairs={{0,121},{8,17},{16,9},{24,33},{32,25},{40,49},{48,41},{56,65},{64,... | collective-permute-start | bytes 1179656 | tf_op jit(solution)/shard_map/kvs_cor/ppermute | solution.py:425
  20.0 3.5 %collective-permute-start.2 = (bf16[2,64,1024]{2,1,0:T(8,128)(2,1)S(1)}, bf16[2,64,1024]{2,1,0:T(8,128)(2,1)S(1)}, u32[]{:S(2)}, u32[]{:S(2)}) collective-permute-start(bf16[2,64,1024]{2,1,0:T(8,128)(2,1)S(1)} %collective-permute-done.ks_ref.rest_2_), channel_id=1, source_target_pairs={{0,2},{8,10},{16,18},{24,26},{32,34},{40,42},{48,50},{56,58},{64,6... | collective-permute-start | bytes 786440 | tf_op jit(solution)/shard_map/key_far/ppermute | solution.py:425
  23.5 3.5 %collective-permute-start.3 = (bf16[2,64,1024]{2,1,0:T(8,128)(2,1)S(1)}, bf16[2,64,1024]{2,1,0:T(8,128)(2,1)S(1)}, u32[]{:S(2)}, u32[]{:S(2)}) collective-permute-start(bf16[2,64,1024]{2,1,0:T(8,128)(2,1)S(1)} %collective-permute-done.1.vs_ref.rest_3_), channel_id=1, source_target_pairs={{0,2},{8,10},{16,18},{24,26},{32,34},{40,42},{48,50},{56,58},{64,6... | collective-permute-start | bytes 786440 | tf_op jit(solution)/shard_map/value_far/ppermute | solution.py:425
  27.1 0.1 collective-permute-start.5
  27.2 0.5 collective-permute-done.2.kf_ref.rest_4_
  27.7 5.6 %collective-permute-done.3.vf_ref.rest_5_ = bf16[2,64,1024]{2,1,0:T(8,128)(2,1)S(1)} collective-permute-done((bf16[2,64,1024]{2,1,0:T(8,128)(2,1)S(1)}, bf16[2,64,1024]{2,1,0:T(8,128)(2,1)S(1)}, u32[]{:S(2)}, u32[]{:S(2)}) %collective-permute-start.3) | collective-permute-done | bytes 262176 | tf_op jit(solution)/shard_map/value_far/ppermute | solution.py:425
  33.3 1.2 %collective-permute-done.5.ss_ref.rest_1_ = bf16[2,64,1024]{2,1,0:T(8,128)(2,1)S(1)} collective-permute-done((bf16[2,64,1024]{2,1,0:T(8,128)(2,1)S(1)}, bf16[2,64,1024]{2,1,0:T(8,128)(2,1)S(1)}, u32[]{:S(2)}, u32[]{:S(2)}) %collective-permute-start.5) | collective-permute-done | bytes 262176 | tf_op jit(solution)/shard_map/season_swap/ppermute | solution.py:425
  34.5 0.0 collective-permute-done.4.cor_ref.rest_7_.rest_4_
  34.5 0.0 copy-done.1
  34.5 0.0 copy-done.3
  34.5 0.0 copy-done.5
  34.5 0.0 copy-start.8
  34.5 0.7 pack.1
  35.2 3.0 %collective-permute-start.6 = (bf16[9,64,1024]{2,1,0:T(8,128)(2,1)S(1)}, bf16[9,64,1024]{2,1,0:T(8,128)(2,1)S(1)}, u32[]{:S(2)}, u32[]{:S(2)}) collective-permute-start(bf16[9,64,1024]{2,1,0:T(8,128)(2,1)S(1)} %get-tuple-element.60), channel_id=1, source_target_pairs={{0,8},{8,0},{16,24},{24,16},{32,40},{40,32},{48,56},{56,48},{64,72... | collective-permute-start | bytes 3538952 | tf_op jit(solution)/shard_map/faces_twin/ppermute | solution.py:425
  38.2 3.3 %collective-permute-start.10 = (bf16[5,64,1024]{2,1,0:T(8,128)(2,1)S(1)}, bf16[5,64,1024]{2,1,0:T(8,128)(2,1)S(1)}, u32[]{:S(2)}, u32[]{:S(2)}) collective-permute-start(bf16[5,64,1024]{2,1,0:T(8,128)(2,1)S(1)} %get-tuple-element.64), channel_id=1, source_target_pairs={{0,2},{8,10},{16,18},{24,26},{32,34},{40,42},{48,50},{56,58},{64,6... | collective-permute-start | bytes 1966088 | tf_op jit(solution)/shard_map/season_far/ppermute | solution.py:425
  41.4 0.1 collective-permute-start.8
  41.5 0.1 collective-permute-start.9
  41.6 4.3 %collective-permute-start.7 = (bf16[1,64,1024]{2,1,0:T(8,128)(2,1)S(1)}, bf16[1,64,1024]{2,1,0:T(8,128)(2,1)S(1)}, u32[]{:S(2)}, u32[]{:S(2)}) collective-permute-start(bf16[1,64,1024]{2,1,0:T(8,128)(2,1)S(1)} %get-tuple-element.73), channel_id=1, source_target_pairs={{0,121},{8,17},{16,9},{24,33},{32,25},{40,49},{48,41},{56,65},{64,... | collective-permute-start | bytes 393224 | tf_op jit(solution)/shard_map/query_cor/ppermute | solution.py:425
  45.9 6.2 %collective-permute-done.7.refs_1_.rest_3_ = bf16[1,64,1024]{2,1,0:T(8,128)(2,1)S(1)} collective-permute-done((bf16[1,64,1024]{2,1,0:T(8,128)(2,1)S(1)}, bf16[1,64,1024]{2,1,0:T(8,128)(2,1)S(1)}, u32[]{:S(2)}, u32[]{:S(2)}) %collective-permute-start.7) | collective-permute-done | bytes 131104 | tf_op jit(solution)/shard_map/query_cor/ppermute | solution.py:425
  52.1 1.3 %collective-permute-done.9.refs_0_.rest_1_ = bf16[2,64,1024]{2,1,0:T(8,128)(2,1)S(1)} collective-permute-done((bf16[2,64,1024]{2,1,0:T(8,128)(2,1)S(1)}, bf16[2,64,1024]{2,1,0:T(8,128)(2,1)S(1)}, u32[]{:S(2)}, u32[]{:S(2)}) %collective-permute-start.9) | collective-permute-done | bytes 262176 | tf_op jit(solution)/shard_map/query_swap/ppermute | solution.py:425
  53.4 0.0 collective-permute-done.8.rest_8_.rest_3_
  53.4 2.1 %collective-permute-done.10.rest_6_.rest_2_ = bf16[5,64,1024]{2,1,0:T(8,128)(2,1)S(1)} collective-permute-done((bf16[5,64,1024]{2,1,0:T(8,128)(2,1)S(1)}, bf16[5,64,1024]{2,1,0:T(8,128)(2,1)S(1)}, u32[]{:S(2)}, u32[]{:S(2)}) %collective-permute-start.10) | collective-permute-done | bytes 655392 | tf_op jit(solution)/shard_map/season_far/ppermute | solution.py:425
  55.5 0.0 collective-permute-done.6.rest_9_.rest_5_.rest_4_
  55.5 1.0 %collective-permute-start.11 = (bf16[5,64,1024]{2,1,0:T(8,128)(2,1)S(1)}, bf16[5,64,1024]{2,1,0:T(8,128)(2,1)S(1)}, u32[]{:S(2)}, u32[]{:S(2)}) collective-permute-start(bf16[5,64,1024]{2,1,0:T(8,128)(2,1)S(1)} %collective-permute-done.10.rest_6_.rest_2_), channel_id=1, source_target_pairs={{0,8},{8,0},{16,24},{24,16},{32,40},{40,32},{48,56},{56,48},{64,72... | collective-permute-start | bytes 1966088 | tf_op jit(solution)/shard_map/season_far_twin/ppermute | solution.py:425
  56.6 0.0 copy-start.7
  56.6 4.4 %collective-permute-start.16 = (bf16[3,64,1024]{2,1,0:T(8,128)(2,1)S(1)}, bf16[3,64,1024]{2,1,0:T(8,128)(2,1)S(1)}, u32[]{:S(2)}, u32[]{:S(2)}) collective-permute-start(bf16[3,64,1024]{2,1,0:T(8,128)(2,1)S(1)} %join.1), channel_id=1, source_target_pairs={{0,2},{8,10},{16,18},{24,26},{32,34},{40,42},{48,50},{56,58},{64,6... | collective-permute-start | bytes 1179656 | tf_op jit(solution)/shard_map/query_far/ppermute | solution.py:425
  61.1 3.4 %attend.1 = (bf16[2,64,1024]{2,1,0:T(8,128)(2,1)S(1)}, f32[2,64,128]{2,1,0:T(8,128)S(1)}) custom-call(s32[2]{0:T(128)S(1)} %pad_add_fusion.here_ref, s32[8,32]{1,0:T(8,128)S(1)} %copy-done.8, bf16[2,64,1024]{2,1,0:T(8,128)(2,1)S(1)} %bitcast.30, bf16[2,64,1024]{2,1,0:T(8,128)(2,1)S(1)} %bitcast.14, bf16[2,64,1024]{2,1,0:T(8,128)(2,1)S(1)} %bitcast.22, ...), custom_call_target="tpu_custom_call" | custom-call | flops 1000 | bytes 1000 | tf_op jit(solution)/shard_map/attend/pallas_call | solution.py:477
  64.4 0.0 collective-permute-done.11.rest_6_
  64.5 2.9 %contrast.1 = (f32[2,64]{1,0:T(2,128)}, bf16[2,64,1152]{2,1,0:T(8,128)(2,1)S(1)}, f32[2,64,128]{2,1,0:T(8,128)S(1)}) custom-call(s32[2]{0:T(128)S(1)} %pad_add_fusion.here_ref, s32[8,32]{1,0:T(8,128)S(1)} %copy-done.8, bf16[2,64,1024]{2,1,0:T(8,128)(2,1)S(1)} %get-tuple-element.68.att_ref, f32[2,64,128]{2,1,0:T(8,128)S(1)} %get-tuple-element.69.stat_ref, ...), custom_call_target="tpu_custom_call" | custom-call | flops 1000 | bytes 1000 | tf_op jit(solution)/shard_map/contrast/pallas_call | solution.py:485
  67.4 0.7 collective-permute-start.12
  68.1 2.7 %collective-permute-start.13 = (bf16[1,64,1152]{2,1,0:T(8,128)(2,1)S(1)}, bf16[1,64,1152]{2,1,0:T(8,128)(2,1)S(1)}, u32[]{:S(2)}, u32[]{:S(2)}) collective-permute-start(bf16[1,64,1152]{2,1,0:T(8,128)(2,1)S(1)} %slice.3), channel_id=1, source_target_pairs={{0,121},{8,17},{16,9},{24,33},{32,25},{40,49},{48,41},{56,65},{64,... | collective-permute-start | bytes 442376 | tf_op jit(solution)/shard_map/grad_cor/ppermute | solution.py:425
  70.8 0.0 collective-permute-start.14
  70.8 1.7 %collective-permute-start.15 = (bf16[1,64,1024]{2,1,0:T(8,128)(2,1)S(1)}, bf16[1,64,1024]{2,1,0:T(8,128)(2,1)S(1)}, u32[]{:S(2)}, u32[]{:S(2)}) collective-permute-start(bf16[1,64,1024]{2,1,0:T(8,128)(2,1)S(1)} %get-tuple-element.73), channel_id=1, source_target_pairs={{0,120},{8,16},{16,8},{24,32},{32,24},{40,48},{48,40},{56,64},{64,... | collective-permute-start | bytes 393224 | tf_op jit(solution)/shard_map/query_off/ppermute | solution.py:425
  72.6 4.4 %query_grads.1 = bf16[2,64,1024]{2,1,0:T(8,128)(2,1)} custom-call(s32[2]{0:T(128)S(1)} %pad_add_fusion.here_ref, s32[8,32]{1,0:T(8,128)S(1)} %copy-done.8, bf16[2,64,1024]{2,1,0:T(8,128)(2,1)S(1)} %bitcast.31, bf16[2,64,1152]{2,1,0:T(8,128)(2,1)S(1)} %get-tuple-element.72.grad_ref.rest_6_, f32[2,64,128]{2,1,0:T(8,128)S(1)} %get-tuple-element.76.stats_ref, ...), custom_call_target="tpu_custom_call" | custom-call | flops 1000 | bytes 1000 | tf_op jit(solution)/shard_map/query_grads/pallas_call | solution.py:497
  77.0 0.0 collective-permute-done.16.rest_0_
  77.0 6.3 %collective-permute-done.15.rest_2_ = bf16[1,64,1024]{2,1,0:T(8,128)(2,1)S(1)} collective-permute-done((bf16[1,64,1024]{2,1,0:T(8,128)(2,1)S(1)}, bf16[1,64,1024]{2,1,0:T(8,128)(2,1)S(1)}, u32[]{:S(2)}, u32[]{:S(2)}) %collective-permute-start.15) | collective-permute-done | bytes 131104 | tf_op jit(solution)/shard_map/query_off/ppermute | solution.py:425
  83.3 0.0 collective-permute-done.13.cor_ref.rest_9_
  83.3 0.0 collective-permute-done.14.rest_8_
  83.3 0.0 collective-permute-done.12.swap_ref.rest_7_
  83.3 0.1 grad_pack.1
  83.3 4.0 %collective-permute-start.17 = (bf16[3,64,1152]{2,1,0:T(8,128)(2,1)S(1)}, bf16[3,64,1152]{2,1,0:T(8,128)(2,1)S(1)}, u32[]{:S(2)}, u32[]{:S(2)}) collective-permute-start(bf16[3,64,1152]{2,1,0:T(8,128)(2,1)S(1)} %get-tuple-element.80), channel_id=1, source_target_pairs={{0,2},{8,10},{16,18},{24,26},{32,34},{40,42},{48,50},{56,58},{64,6... | collective-permute-start | bytes 1327112 | tf_op jit(solution)/shard_map/grad_far/ppermute | solution.py:425
  87.4 2.2 %collective-permute-start.18 = (bf16[3,64,1024]{2,1,0:T(8,128)(2,1)S(1)}, bf16[3,64,1024]{2,1,0:T(8,128)(2,1)S(1)}, u32[]{:S(2)}, u32[]{:S(2)}) collective-permute-start(bf16[3,64,1024]{2,1,0:T(8,128)(2,1)S(1)} %collective-permute-done.16.rest_0_), channel_id=1, source_target_pairs={{0,8},{8,0},{16,24},{24,16},{32,40},{40,32},{48,56},{56,48},{64,72... | collective-permute-start | bytes 1179656 | tf_op jit(solution)/shard_map/query_far_twin/ppermute | solution.py:425
  89.5 0.3 collective-permute-start.20
  89.8 0.2 collective-permute-start.19
  90.0 1.6 %collective-permute-done.19.rest_5_ = bf16[2,64,1024]{2,1,0:T(8,128)(2,1)S(1)} collective-permute-done((bf16[2,64,1024]{2,1,0:T(8,128)(2,1)S(1)}, bf16[2,64,1024]{2,1,0:T(8,128)(2,1)S(1)}, u32[]{:S(2)}, u32[]{:S(2)}) %collective-permute-start.19) | collective-permute-done | bytes 262176 | tf_op jit(solution)/shard_map/query_twin/ppermute | solution.py:425
  91.7 0.0 collective-permute-done.20.rest_10_
  91.7 3.4 %inner_key_grads.1 = (f32[2,64,1024]{2,1,0:T(8,128)S(1)}, f32[2,64,1024]{2,1,0:T(8,128)S(1)}) custom-call(s32[2]{0:T(128)S(1)} %pad_add_fusion.here_ref, s32[8,32]{1,0:T(8,128)S(1)} %copy-done.8, bf16[2,64,1024]{2,1,0:T(8,128)(2,1)S(1)} %bitcast.16, bf16[2,64,1024]{2,1,0:T(8,128)(2,1)S(1)} %bitcast.24, bf16[2,64,1024]{2,1,0:T(8,128)(2,1)S(1)} %bitcast.32, ...), custom_call_target="tpu_custom_call" | custom-call | flops 1000 | bytes 1000 | tf_op jit(solution)/shard_map/inner_key_grads/pallas_call | solution.py:521
  95.1 0.0 collective-permute-done.18.rest_1_
  95.1 0.0 collective-permute-done.17.rest_1_.rest_2_
  95.1 2.6 %collective-permute-start.21 = (bf16[3,64,1152]{2,1,0:T(8,128)(2,1)S(1)}, bf16[3,64,1152]{2,1,0:T(8,128)(2,1)S(1)}, u32[]{:S(2)}, u32[]{:S(2)}) collective-permute-start(bf16[3,64,1152]{2,1,0:T(8,128)(2,1)S(1)} %collective-permute-done.17.rest_1_.rest_2_), channel_id=1, source_target_pairs={{0,8},{8,0},{16,24},{24,16},{32,40},{40,32},{48,56},{56,48},{64,72... | collective-permute-start | bytes 1327112 | tf_op jit(solution)/shard_map/grad_last_twin/ppermute | solution.py:425
  97.7 1.7 %outer_near_key_grads.1 = (bf16[64,1024]{1,0:T(8,128)(2,1)S(1)}, bf16[64,1024]{1,0:T(8,128)(2,1)S(1)}) custom-call(s32[2]{0:T(128)S(1)} %pad_add_fusion.here_ref, s32[8,32]{1,0:T(8,128)S(1)} %copy-done.8, bf16[2,64,1024]{2,1,0:T(8,128)(2,1)S(1)} %bitcast.17, bf16[2,64,1024]{2,1,0:T(8,128)(2,1)S(1)} %bitcast.25, ...), custom_call_target="tpu_custom_call" | custom-call | flops 1000 | bytes 1000 | tf_op jit(solution)/shard_map/outer_near_key_grads/pallas_call | solution.py:534
  99.4 0.0 collective-permute-done.21.rest_3_
  99.4 2.5 %outer_face_key_grads.1 = (bf16[2,64,1024]{2,1,0:T(8,128)(2,1)}, bf16[2,64,1024]{2,1,0:T(8,128)(2,1)}) custom-call(s32[2]{0:T(128)S(1)} %pad_add_fusion.here_ref, s32[8,32]{1,0:T(8,128)S(1)} %copy-done.8, bf16[2,64,1024]{2,1,0:T(8,128)(2,1)S(1)} %bitcast.18, bf16[2,64,1024]{2,1,0:T(8,128)(2,1)S(1)} %bitcast.26, ...), custom_call_target="tpu_custom_call" | custom-call | flops 1000 | bytes 1000 | tf_op jit(solution)/shard_map/outer_face_key_grads/pallas_call | solution.py:541
  (12 shorter events, 0.1 us)
Async XLA Ops:
  0.6 9.6 %collective-permute-start = (bf16[2,64,1024]{2,1,0:T(8,128)(2,1)}, bf16[2,64,1024]{2,1,0:T(8,128)(2,1)S(1)}, u32[]{:S(2)}, u32[]{:S(2)}) collective-permute-start(bf16[2,64,1024]{2,1,0:T(8,128)(2,1)} %bitcast.11), channel_id=1, source_target_pairs={{0,1},{8,9},{16,17},{24,25},{32,33},{40,41},{48,49},{56,57},{64,65... | collective-permute-start | bytes 786440 | tf_op jit(solution)/shard_map/key_swap/ppermute | solution.py:425
  4.3 11.4 %collective-permute-start.1 = (bf16[2,64,1024]{2,1,0:T(8,128)(2,1)}, bf16[2,64,1024]{2,1,0:T(8,128)(2,1)S(1)}, u32[]{:S(2)}, u32[]{:S(2)}) collective-permute-start(bf16[2,64,1024]{2,1,0:T(8,128)(2,1)} %bitcast.19), channel_id=1, source_target_pairs={{0,1},{8,9},{16,17},{24,25},{32,33},{40,41},{48,49},{56,57},{64,65... | collective-permute-start | bytes 786440 | tf_op jit(solution)/shard_map/value_swap/ppermute | solution.py:425
  4.5 0.9 copy-start
  5.4 0.9 copy-start.2
  6.4 0.9 copy-start.4
  7.3 0.9 copy-start.6
  8.3 0.7 copy-start.9
  8.9 25.5 %copy-start.1 = (bf16[1,2,64,1024]{3,2,1,0:T(8,128)(2,1)S(1)}, bf16[1,2,64,1024]{3,2,1,0:T(8,128)(2,1)}, u32[]{:S(2)}) copy-start(bf16[1,2,64,1024]{3,2,1,0:T(8,128)(2,1)} %param.7) | copy-start | bytes 786436
  8.9 25.5 %copy-start.3 = (bf16[1,2,64,1024]{3,2,1,0:T(8,128)(2,1)S(1)}, bf16[1,2,64,1024]{3,2,1,0:T(8,128)(2,1)}, u32[]{:S(2)}) copy-start(bf16[1,2,64,1024]{3,2,1,0:T(8,128)(2,1)} %param.8) | copy-start | bytes 786436
  8.9 25.5 %copy-start.5 = (bf16[1,2,64,1024]{3,2,1,0:T(8,128)(2,1)S(1)}, bf16[1,2,64,1024]{3,2,1,0:T(8,128)(2,1)}, u32[]{:S(2)}) copy-start(bf16[1,2,64,1024]{3,2,1,0:T(8,128)(2,1)} %param.6) | copy-start | bytes 786436
  15.7 18.8 %collective-permute-start.4 = (bf16[3,64,1024]{2,1,0:T(8,128)(2,1)S(1)}, bf16[3,64,1024]{2,1,0:T(8,128)(2,1)S(1)}, u32[]{:S(2)}, u32[]{:S(2)}) collective-permute-start(bf16[3,64,1024]{2,1,0:T(8,128)(2,1)S(1)} %get-tuple-element.62), channel_id=1, source_target_pairs={{0,121},{8,17},{16,9},{24,33},{32,25},{40,49},{48,41},{56,65},{64,... | collective-permute-start | bytes 1179656 | tf_op jit(solution)/shard_map/kvs_cor/ppermute | solution.py:425
  20.0 7.7 %collective-permute-start.2 = (bf16[2,64,1024]{2,1,0:T(8,128)(2,1)S(1)}, bf16[2,64,1024]{2,1,0:T(8,128)(2,1)S(1)}, u32[]{:S(2)}, u32[]{:S(2)}) collective-permute-start(bf16[2,64,1024]{2,1,0:T(8,128)(2,1)S(1)} %collective-permute-done.ks_ref.rest_2_), channel_id=1, source_target_pairs={{0,2},{8,10},{16,18},{24,26},{32,34},{40,42},{48,50},{56,58},{64,6... | collective-permute-start | bytes 786440 | tf_op jit(solution)/shard_map/key_far/ppermute | solution.py:425
  23.5 9.8 %collective-permute-start.3 = (bf16[2,64,1024]{2,1,0:T(8,128)(2,1)S(1)}, bf16[2,64,1024]{2,1,0:T(8,128)(2,1)S(1)}, u32[]{:S(2)}, u32[]{:S(2)}) collective-permute-start(bf16[2,64,1024]{2,1,0:T(8,128)(2,1)S(1)} %collective-permute-done.1.vs_ref.rest_3_), channel_id=1, source_target_pairs={{0,2},{8,10},{16,18},{24,26},{32,34},{40,42},{48,50},{56,58},{64,6... | collective-permute-start | bytes 786440 | tf_op jit(solution)/shard_map/value_far/ppermute | solution.py:425
  27.1 7.4 %collective-permute-start.5 = (bf16[2,64,1024]{2,1,0:T(8,128)(2,1)S(1)}, bf16[2,64,1024]{2,1,0:T(8,128)(2,1)S(1)}, u32[]{:S(2)}, u32[]{:S(2)}) collective-permute-start(bf16[2,64,1024]{2,1,0:T(8,128)(2,1)S(1)} %bitcast.34), channel_id=1, source_target_pairs={{0,1},{8,9},{16,17},{24,25},{32,33},{40,41},{48,49},{56,57},{64,65... | collective-permute-start | bytes 786440 | tf_op jit(solution)/shard_map/season_swap/ppermute | solution.py:425
  34.5 26.6 %copy-start.8 = (s32[8,32]{1,0:T(8,128)S(1)}, s32[8,32]{1,0:T(8,128)}, u32[]{:S(2)}) copy-start(s32[8,32]{1,0:T(8,128)} %cloud_ref.11) | copy-start | bytes 3076
  35.2 20.3 %collective-permute-start.6 = (bf16[9,64,1024]{2,1,0:T(8,128)(2,1)S(1)}, bf16[9,64,1024]{2,1,0:T(8,128)(2,1)S(1)}, u32[]{:S(2)}, u32[]{:S(2)}) collective-permute-start(bf16[9,64,1024]{2,1,0:T(8,128)(2,1)S(1)} %get-tuple-element.60), channel_id=1, source_target_pairs={{0,8},{8,0},{16,24},{24,16},{32,40},{40,32},{48,56},{56,48},{64,72... | collective-permute-start | bytes 3538952 | tf_op jit(solution)/shard_map/faces_twin/ppermute | solution.py:425
  38.2 17.4 %collective-permute-start.10 = (bf16[5,64,1024]{2,1,0:T(8,128)(2,1)S(1)}, bf16[5,64,1024]{2,1,0:T(8,128)(2,1)S(1)}, u32[]{:S(2)}, u32[]{:S(2)}) collective-permute-start(bf16[5,64,1024]{2,1,0:T(8,128)(2,1)S(1)} %get-tuple-element.64), channel_id=1, source_target_pairs={{0,2},{8,10},{16,18},{24,26},{32,34},{40,42},{48,50},{56,58},{64,6... | collective-permute-start | bytes 1966088 | tf_op jit(solution)/shard_map/season_far/ppermute | solution.py:425
  41.4 12.0 %collective-permute-start.8 = (bf16[3,64,1024]{2,1,0:T(8,128)(2,1)S(1)}, bf16[3,64,1024]{2,1,0:T(8,128)(2,1)S(1)}, u32[]{:S(2)}, u32[]{:S(2)}) collective-permute-start(bf16[3,64,1024]{2,1,0:T(8,128)(2,1)S(1)} %get-tuple-element.62), channel_id=1, source_target_pairs={{0,120},{8,16},{16,8},{24,32},{32,24},{40,48},{48,40},{56,64},{64,... | collective-permute-start | bytes 1179656 | tf_op jit(solution)/shard_map/kvs_off/ppermute | solution.py:425
  41.5 11.9 %collective-permute-start.9 = (bf16[2,64,1024]{2,1,0:T(8,128)(2,1)S(1)}, bf16[2,64,1024]{2,1,0:T(8,128)(2,1)S(1)}, u32[]{:S(2)}, u32[]{:S(2)}) collective-permute-start(bf16[2,64,1024]{2,1,0:T(8,128)(2,1)S(1)} %bitcast.29), channel_id=1, source_target_pairs={{0,1},{8,9},{16,17},{24,25},{32,33},{40,41},{48,49},{56,57},{64,65... | collective-permute-start | bytes 786440 | tf_op jit(solution)/shard_map/query_swap/ppermute | solution.py:425
  41.6 10.5 %collective-permute-start.7 = (bf16[1,64,1024]{2,1,0:T(8,128)(2,1)S(1)}, bf16[1,64,1024]{2,1,0:T(8,128)(2,1)S(1)}, u32[]{:S(2)}, u32[]{:S(2)}) collective-permute-start(bf16[1,64,1024]{2,1,0:T(8,128)(2,1)S(1)} %get-tuple-element.73), channel_id=1, source_target_pairs={{0,121},{8,17},{16,9},{24,33},{32,25},{40,49},{48,41},{56,65},{64,... | collective-permute-start | bytes 393224 | tf_op jit(solution)/shard_map/query_cor/ppermute | solution.py:425
  55.5 8.9 %collective-permute-start.11 = (bf16[5,64,1024]{2,1,0:T(8,128)(2,1)S(1)}, bf16[5,64,1024]{2,1,0:T(8,128)(2,1)S(1)}, u32[]{:S(2)}, u32[]{:S(2)}) collective-permute-start(bf16[5,64,1024]{2,1,0:T(8,128)(2,1)S(1)} %collective-permute-done.10.rest_6_.rest_2_), channel_id=1, source_target_pairs={{0,8},{8,0},{16,24},{24,16},{32,40},{40,32},{48,56},{56,48},{64,72... | collective-permute-start | bytes 1966088 | tf_op jit(solution)/shard_map/season_far_twin/ppermute | solution.py:425
  56.6 7.9 %copy-start.7 = (bf16[1,2,64,1024]{3,2,1,0:T(8,128)(2,1)S(1)}, bf16[1,2,64,1024]{3,2,1,0:T(8,128)(2,1)}, u32[]{:S(2)}) copy-start(bf16[1,2,64,1024]{3,2,1,0:T(8,128)(2,1)} %param.9) | copy-start | bytes 786436
  56.6 20.4 %collective-permute-start.16 = (bf16[3,64,1024]{2,1,0:T(8,128)(2,1)S(1)}, bf16[3,64,1024]{2,1,0:T(8,128)(2,1)S(1)}, u32[]{:S(2)}, u32[]{:S(2)}) collective-permute-start(bf16[3,64,1024]{2,1,0:T(8,128)(2,1)S(1)} %join.1), channel_id=1, source_target_pairs={{0,2},{8,10},{16,18},{24,26},{32,34},{40,42},{48,50},{56,58},{64,6... | collective-permute-start | bytes 1179656 | tf_op jit(solution)/shard_map/query_far/ppermute | solution.py:425
  67.4 15.9 %collective-permute-start.12 = (bf16[2,64,1152]{2,1,0:T(8,128)(2,1)S(1)}, bf16[2,64,1152]{2,1,0:T(8,128)(2,1)S(1)}, u32[]{:S(2)}, u32[]{:S(2)}) collective-permute-start(bf16[2,64,1152]{2,1,0:T(8,128)(2,1)S(1)} %get-tuple-element.72.grad_ref.rest_6_), channel_id=1, source_target_pairs={{0,1},{8,9},{16,17},{24,25},{32,33},{40,41},{48,49},{56,57},{64,65... | collective-permute-start | bytes 884744 | tf_op jit(solution)/shard_map/grad_swap/ppermute | solution.py:425
  68.1 15.2 %collective-permute-start.13 = (bf16[1,64,1152]{2,1,0:T(8,128)(2,1)S(1)}, bf16[1,64,1152]{2,1,0:T(8,128)(2,1)S(1)}, u32[]{:S(2)}, u32[]{:S(2)}) collective-permute-start(bf16[1,64,1152]{2,1,0:T(8,128)(2,1)S(1)} %slice.3), channel_id=1, source_target_pairs={{0,121},{8,17},{16,9},{24,33},{32,25},{40,49},{48,41},{56,65},{64,... | collective-permute-start | bytes 442376 | tf_op jit(solution)/shard_map/grad_cor/ppermute | solution.py:425
  70.8 12.4 %collective-permute-start.14 = (bf16[1,64,1152]{2,1,0:T(8,128)(2,1)S(1)}, bf16[1,64,1152]{2,1,0:T(8,128)(2,1)S(1)}, u32[]{:S(2)}, u32[]{:S(2)}) collective-permute-start(bf16[1,64,1152]{2,1,0:T(8,128)(2,1)S(1)} %slice.3), channel_id=1, source_target_pairs={{0,120},{8,16},{16,8},{24,32},{32,24},{40,48},{48,40},{56,64},{64,... | collective-permute-start | bytes 442376 | tf_op jit(solution)/shard_map/grad_off/ppermute | solution.py:425
  70.8 12.4 %collective-permute-start.15 = (bf16[1,64,1024]{2,1,0:T(8,128)(2,1)S(1)}, bf16[1,64,1024]{2,1,0:T(8,128)(2,1)S(1)}, u32[]{:S(2)}, u32[]{:S(2)}) collective-permute-start(bf16[1,64,1024]{2,1,0:T(8,128)(2,1)S(1)} %get-tuple-element.73), channel_id=1, source_target_pairs={{0,120},{8,16},{16,8},{24,32},{32,24},{40,48},{48,40},{56,64},{64,... | collective-permute-start | bytes 393224 | tf_op jit(solution)/shard_map/query_off/ppermute | solution.py:425
  83.3 11.8 %collective-permute-start.17 = (bf16[3,64,1152]{2,1,0:T(8,128)(2,1)S(1)}, bf16[3,64,1152]{2,1,0:T(8,128)(2,1)S(1)}, u32[]{:S(2)}, u32[]{:S(2)}) collective-permute-start(bf16[3,64,1152]{2,1,0:T(8,128)(2,1)S(1)} %get-tuple-element.80), channel_id=1, source_target_pairs={{0,2},{8,10},{16,18},{24,26},{32,34},{40,42},{48,50},{56,58},{64,6... | collective-permute-start | bytes 1327112 | tf_op jit(solution)/shard_map/grad_far/ppermute | solution.py:425
  87.4 7.7 %collective-permute-start.18 = (bf16[3,64,1024]{2,1,0:T(8,128)(2,1)S(1)}, bf16[3,64,1024]{2,1,0:T(8,128)(2,1)S(1)}, u32[]{:S(2)}, u32[]{:S(2)}) collective-permute-start(bf16[3,64,1024]{2,1,0:T(8,128)(2,1)S(1)} %collective-permute-done.16.rest_0_), channel_id=1, source_target_pairs={{0,8},{8,0},{16,24},{24,16},{32,40},{40,32},{48,56},{56,48},{64,72... | collective-permute-start | bytes 1179656 | tf_op jit(solution)/shard_map/query_far_twin/ppermute | solution.py:425
  89.5 2.1 %collective-permute-start.20 = (bf16[2,64,1152]{2,1,0:T(8,128)(2,1)S(1)}, bf16[2,64,1152]{2,1,0:T(8,128)(2,1)S(1)}, u32[]{:S(2)}, u32[]{:S(2)}) collective-permute-start(bf16[2,64,1152]{2,1,0:T(8,128)(2,1)S(1)} %get-tuple-element.85), channel_id=1, source_target_pairs={{0,8},{8,0},{16,24},{24,16},{32,40},{40,32},{48,56},{56,48},{64,72... | collective-permute-start | bytes 884744 | tf_op jit(solution)/shard_map/grad_twin/ppermute | solution.py:425
  89.8 1.9 %collective-permute-start.19 = (bf16[2,64,1024]{2,1,0:T(8,128)(2,1)S(1)}, bf16[2,64,1024]{2,1,0:T(8,128)(2,1)S(1)}, u32[]{:S(2)}, u32[]{:S(2)}) collective-permute-start(bf16[2,64,1024]{2,1,0:T(8,128)(2,1)S(1)} %collective-permute-done.9.refs_0_.rest_1_), channel_id=1, source_target_pairs={{0,8},{8,0},{16,24},{24,16},{32,40},{40,32},{48,56},{56,48},{64,72... | collective-permute-start | bytes 786440 | tf_op jit(solution)/shard_map/query_twin/ppermute | solution.py:425
  95.1 4.3 %collective-permute-start.21 = (bf16[3,64,1152]{2,1,0:T(8,128)(2,1)S(1)}, bf16[3,64,1152]{2,1,0:T(8,128)(2,1)S(1)}, u32[]{:S(2)}, u32[]{:S(2)}) collective-permute-start(bf16[3,64,1152]{2,1,0:T(8,128)(2,1)S(1)} %collective-permute-done.17.rest_1_.rest_2_), channel_id=1, source_target_pairs={{0,8},{8,0},{16,24},{24,16},{32,40},{40,32},{48,56},{56,48},{64,72... | collective-permute-start | bytes 1327112 | tf_op jit(solution)/shard_map/grad_last_twin/ppermute | solution.py:425

commit v5 on v4

--- a/solution.py
+++ b/solution.py
@@ -451,11 +451,11 @@
         ),
         [pltpu.SemaphoreType.DMA((4,))],
     )(here, pairing[0], k, v, s, q)
-    k_swap, v_swap, s1, edge = phase(k_swap, v_swap, s, edge)
+    k_swap, edge, s1 = phase(k_swap, edge, s)
     cor = named("kvs", edge, "cor")
     k_far = named("key", k_swap, "far")
+    s_swap = named("season", s1, "swap")
     v_far = named("value", v_swap, "far")
-    s_swap = named("season", s1, "swap")
     k_far, v_far, cor, s_swap, edge, q1, q_near = phase(k_far, v_far, cor, s_swap, edge, q, q_near)
     far_stack, faces = call(
         pack_kernel,

time: 102 us -> 98.1 us (0.962)
  waiting for transfers between devices: 30.3 us -> 25.4 us
    ppermute x22, waiting for transfers between devices: 30.3 us -> 25.4 us  [move(): return lax.ppermute(x, AXES, way[kind])]
  transfers between devices with their start and end apart: 22 -> 22, of which waited for: 9 -> 10; matrix products, arithmetic and copies ran while one was open for 0% -> 0% of each run, Pallas kernels for 17% -> 18%
where the time goes in v5:
time: 98.1 us; the launch traced here: 97.5 us
  starting transfers between devices  46.4 us (47%)
  waiting for transfers between devices  25.4 us (26%)
  Pallas kernels  20.3 us (21%)
  local copies, waits for them, and re-layouts  4.51 us (5%)
    ppermute x22, starting transfers between devices, move(): return lax.ppermute(x, AXES, way[kind])  46.4 us
    ppermute x22, waiting for transfers between devices, move(): return lax.ppermute(x, AXES, way[kind])  25.4 us
    unnamed x20, local copies, waits for them, and re-layouts  4.5 us
    pallas_call x1, Pallas kernels, body(): call(query_kernel, 'query_grads', [SMEM, SMEM, VMEM, VMEM, VMEM] + [VMEM]...  4.43 us
    pallas_call x1, Pallas kernels, body(): call(inner_key_kernel, 'inner_key_grads', [SMEM, SMEM, VMEM, VMEM] + [VME...  3.41 us
    pallas_call x1, Pallas kernels, body(): call(attend_kernel, 'attend', [SMEM, SMEM, VMEM] + [VMEM] * 10, (shape((2...  3.38 us
    pallas_call x1, Pallas kernels, body(): call(contrast_kernel, 'contrast', [SMEM, SMEM, VMEM, VMEM, VMEM] + [VMEM]...  2.92 us
    pallas_call x1, Pallas kernels, body(): call(outer_face_kernel, 'outer_face_key_grads', [SMEM, SMEM] + [VMEM] * 1...  2.46 us
  transfers between devices with their start and end apart: 22, of which 10 were waited for; matrix products, arithmetic and copies ran while one was open for 0% of the time, Pallas kernels for 18%

profile of v5, /device:TPU:1, one launch (start us, length us, event | category | flops | bytes accessed | tf_op | source)
XLA Modules:
  0.0 97.5 jit_solution(13930801487757003390)
XLA Ops:
  0.6 3.7 %collective-permute-start = (bf16[2,64,1024]{2,1,0:T(8,128)(2,1)}, bf16[2,64,1024]{2,1,0:T(8,128)(2,1)S(1)}, u32[]{:S(2)}, u32[]{:S(2)}) collective-permute-start(bf16[2,64,1024]{2,1,0:T(8,128)(2,1)} %bitcast.11), channel_id=1, source_target_pairs={{0,1},{8,9},{16,17},{24,25},{32,33},{40,41},{48,49},{56,57},{64,65... | collective-permute-start | bytes 786440 | tf_op jit(solution)/shard_map/key_swap/ppermute | solution.py:425
  4.3 0.1 collective-permute-start.1
  4.4 0.1 pad_add_fusion.here_ref
  4.5 0.9 copy-done
  5.4 0.9 copy-done.2
  6.4 0.9 copy-done.4
  7.3 0.9 copy-done.6
  8.3 0.7 copy-done.9
  8.9 1.3 %edges.1 = (bf16[3,64,1024]{2,1,0:T(8,128)(2,1)S(1)}, bf16[1,64,1024]{2,1,0:T(8,128)(2,1)S(1)}, s32[2,64]{1,0:T(2,128)S(1)}) custom-call(s32[2]{0:T(128)S(1)} %pad_add_fusion.here_ref, s32[2,64]{1,0:T(2,128)S(1)} %bitcast.37, bf16[2,64,1024]{2,1,0:T(8,128)(2,1)S(1)} %bitcast.12, bf16[2,64,1024]{2,1,0:T(8,128)(2,1)S(1)} %bitcast.20, ...), custom_call_target="tpu_custom_call" | custom-call | flops 1000 | bytes 1000 | tf_op jit(solution)/shard_map/edges/pallas_call | solution.py:443
  10.2 0.0 collective-permute-done.ks_ref.rest_2_
  10.2 5.3 %collective-permute-start.4 = (bf16[3,64,1024]{2,1,0:T(8,128)(2,1)S(1)}, bf16[3,64,1024]{2,1,0:T(8,128)(2,1)S(1)}, u32[]{:S(2)}, u32[]{:S(2)}) collective-permute-start(bf16[3,64,1024]{2,1,0:T(8,128)(2,1)S(1)} %get-tuple-element.60), channel_id=1, source_target_pairs={{0,121},{8,17},{16,9},{24,33},{32,25},{40,49},{48,41},{56,65},{64,... | collective-permute-start | bytes 1179656 | tf_op jit(solution)/shard_map/kvs_cor/ppermute | solution.py:425
  15.5 3.5 %collective-permute-start.2 = (bf16[2,64,1024]{2,1,0:T(8,128)(2,1)S(1)}, bf16[2,64,1024]{2,1,0:T(8,128)(2,1)S(1)}, u32[]{:S(2)}, u32[]{:S(2)}) collective-permute-start(bf16[2,64,1024]{2,1,0:T(8,128)(2,1)S(1)} %collective-permute-done.ks_ref.rest_2_), channel_id=1, source_target_pairs={{0,2},{8,10},{16,18},{24,26},{32,34},{40,42},{48,50},{56,58},{64,6... | collective-permute-start | bytes 786440 | tf_op jit(solution)/shard_map/key_far/ppermute | solution.py:425
  19.0 0.1 collective-permute-start.5
  19.1 0.0 collective-permute-done.1.vs_ref.rest_3_
  19.1 3.5 %collective-permute-start.3 = (bf16[2,64,1024]{2,1,0:T(8,128)(2,1)S(1)}, bf16[2,64,1024]{2,1,0:T(8,128)(2,1)S(1)}, u32[]{:S(2)}, u32[]{:S(2)}) collective-permute-start(bf16[2,64,1024]{2,1,0:T(8,128)(2,1)S(1)} %collective-permute-done.1.vs_ref.rest_3_), channel_id=1, source_target_pairs={{0,2},{8,10},{16,18},{24,26},{32,34},{40,42},{48,50},{56,58},{64,6... | collective-permute-start | bytes 786440 | tf_op jit(solution)/shard_map/value_far/ppermute | solution.py:425
  22.7 1.7 %collective-permute-done.2.kf_ref.rest_4_ = bf16[2,64,1024]{2,1,0:T(8,128)(2,1)S(1)} collective-permute-done((bf16[2,64,1024]{2,1,0:T(8,128)(2,1)S(1)}, bf16[2,64,1024]{2,1,0:T(8,128)(2,1)S(1)}, u32[]{:S(2)}, u32[]{:S(2)}) %collective-permute-start.2) | collective-permute-done | bytes 262176 | tf_op jit(solution)/shard_map/key_far/ppermute | solution.py:425
  24.4 3.6 %collective-permute-done.5.ss_ref.rest_1_ = bf16[2,64,1024]{2,1,0:T(8,128)(2,1)S(1)} collective-permute-done((bf16[2,64,1024]{2,1,0:T(8,128)(2,1)S(1)}, bf16[2,64,1024]{2,1,0:T(8,128)(2,1)S(1)}, u32[]{:S(2)}, u32[]{:S(2)}) %collective-permute-start.5) | collective-permute-done | bytes 262176 | tf_op jit(solution)/shard_map/season_swap/ppermute | solution.py:425
  28.0 2.0 %collective-permute-done.3.vf_ref.rest_5_ = bf16[2,64,1024]{2,1,0:T(8,128)(2,1)S(1)} collective-permute-done((bf16[2,64,1024]{2,1,0:T(8,128)(2,1)S(1)}, bf16[2,64,1024]{2,1,0:T(8,128)(2,1)S(1)}, u32[]{:S(2)}, u32[]{:S(2)}) %collective-permute-start.3) | collective-permute-done | bytes 262176 | tf_op jit(solution)/shard_map/value_far/ppermute | solution.py:425
  30.1 0.1 collective-permute-done.4.cor_ref.rest_7_.rest_4_
  30.2 0.0 copy-done.1
  30.2 0.0 copy-done.3
  30.2 0.0 copy-done.5
  30.2 0.0 copy-start.8
  30.2 0.7 pack.1
  30.9 3.9 %collective-permute-start.6 = (bf16[9,64,1024]{2,1,0:T(8,128)(2,1)S(1)}, bf16[9,64,1024]{2,1,0:T(8,128)(2,1)S(1)}, u32[]{:S(2)}, u32[]{:S(2)}) collective-permute-start(bf16[9,64,1024]{2,1,0:T(8,128)(2,1)S(1)} %get-tuple-element.58), channel_id=1, source_target_pairs={{0,8},{8,0},{16,24},{24,16},{32,40},{40,32},{48,56},{56,48},{64,72... | collective-permute-start | bytes 3538952 | tf_op jit(solution)/shard_map/faces_twin/ppermute | solution.py:425
  34.8 3.6 %collective-permute-start.10 = (bf16[5,64,1024]{2,1,0:T(8,128)(2,1)S(1)}, bf16[5,64,1024]{2,1,0:T(8,128)(2,1)S(1)}, u32[]{:S(2)}, u32[]{:S(2)}) collective-permute-start(bf16[5,64,1024]{2,1,0:T(8,128)(2,1)S(1)} %get-tuple-element.62), channel_id=1, source_target_pairs={{0,2},{8,10},{16,18},{24,26},{32,34},{40,42},{48,50},{56,58},{64,6... | collective-permute-start | bytes 1966088 | tf_op jit(solution)/shard_map/season_far/ppermute | solution.py:425
  38.4 0.1 collective-permute-start.8
  38.5 0.6 collective-permute-start.9
  39.1 3.8 %collective-permute-start.7 = (bf16[1,64,1024]{2,1,0:T(8,128)(2,1)S(1)}, bf16[1,64,1024]{2,1,0:T(8,128)(2,1)S(1)}, u32[]{:S(2)}, u32[]{:S(2)}) collective-permute-start(bf16[1,64,1024]{2,1,0:T(8,128)(2,1)S(1)} %get-tuple-element.71), channel_id=1, source_target_pairs={{0,121},{8,17},{16,9},{24,33},{32,25},{40,49},{48,41},{56,65},{64,... | collective-permute-start | bytes 393224 | tf_op jit(solution)/shard_map/query_cor/ppermute | solution.py:425
  42.9 3.0 %collective-permute-done.7.refs_1_.rest_3_ = bf16[1,64,1024]{2,1,0:T(8,128)(2,1)S(1)} collective-permute-done((bf16[1,64,1024]{2,1,0:T(8,128)(2,1)S(1)}, bf16[1,64,1024]{2,1,0:T(8,128)(2,1)S(1)}, u32[]{:S(2)}, u32[]{:S(2)}) %collective-permute-start.7) | collective-permute-done | bytes 131104 | tf_op jit(solution)/shard_map/query_cor/ppermute | solution.py:425
  45.9 6.8 %collective-permute-done.9.refs_0_.rest_1_ = bf16[2,64,1024]{2,1,0:T(8,128)(2,1)S(1)} collective-permute-done((bf16[2,64,1024]{2,1,0:T(8,128)(2,1)S(1)}, bf16[2,64,1024]{2,1,0:T(8,128)(2,1)S(1)}, u32[]{:S(2)}, u32[]{:S(2)}) %collective-permute-start.9) | collective-permute-done | bytes 262176 | tf_op jit(solution)/shard_map/query_swap/ppermute | solution.py:425
  52.7 0.0 collective-permute-done.8.rest_8_.rest_3_
  52.7 0.0 collective-permute-done.10.rest_6_.rest_2_
  52.7 0.0 collective-permute-done.6.rest_9_.rest_5_.rest_4_
  52.7 2.0 %collective-permute-start.11 = (bf16[5,64,1024]{2,1,0:T(8,128)(2,1)S(1)}, bf16[5,64,1024]{2,1,0:T(8,128)(2,1)S(1)}, u32[]{:S(2)}, u32[]{:S(2)}) collective-permute-start(bf16[5,64,1024]{2,1,0:T(8,128)(2,1)S(1)} %collective-permute-done.10.rest_6_.rest_2_), channel_id=1, source_target_pairs={{0,8},{8,0},{16,24},{24,16},{32,40},{40,32},{48,56},{56,48},{64,72... | collective-permute-start | bytes 1966088 | tf_op jit(solution)/shard_map/season_far_twin/ppermute | solution.py:425
  54.8 0.0 copy-start.7
  54.8 4.3 %collective-permute-start.16 = (bf16[3,64,1024]{2,1,0:T(8,128)(2,1)S(1)}, bf16[3,64,1024]{2,1,0:T(8,128)(2,1)S(1)}, u32[]{:S(2)}, u32[]{:S(2)}) collective-permute-start(bf16[3,64,1024]{2,1,0:T(8,128)(2,1)S(1)} %join.1), channel_id=1, source_target_pairs={{0,2},{8,10},{16,18},{24,26},{32,34},{40,42},{48,50},{56,58},{64,6... | collective-permute-start | bytes 1179656 | tf_op jit(solution)/shard_map/query_far/ppermute | solution.py:425
  59.1 3.4 %attend.1 = (bf16[2,64,1024]{2,1,0:T(8,128)(2,1)S(1)}, f32[2,64,128]{2,1,0:T(8,128)S(1)}) custom-call(s32[2]{0:T(128)S(1)} %pad_add_fusion.here_ref, s32[8,32]{1,0:T(8,128)S(1)} %copy-done.8, bf16[2,64,1024]{2,1,0:T(8,128)(2,1)S(1)} %bitcast.30, bf16[2,64,1024]{2,1,0:T(8,128)(2,1)S(1)} %bitcast.14, bf16[2,64,1024]{2,1,0:T(8,128)(2,1)S(1)} %bitcast.22, ...), custom_call_target="tpu_custom_call" | custom-call | flops 1000 | bytes 1000 | tf_op jit(solution)/shard_map/attend/pallas_call | solution.py:477
  62.5 0.0 collective-permute-done.11.rest_6_
  62.5 2.9 %contrast.1 = (f32[2,64]{1,0:T(2,128)}, bf16[2,64,1152]{2,1,0:T(8,128)(2,1)S(1)}, f32[2,64,128]{2,1,0:T(8,128)S(1)}) custom-call(s32[2]{0:T(128)S(1)} %pad_add_fusion.here_ref, s32[8,32]{1,0:T(8,128)S(1)} %copy-done.8, bf16[2,64,1024]{2,1,0:T(8,128)(2,1)S(1)} %get-tuple-element.66.att_ref, f32[2,64,128]{2,1,0:T(8,128)S(1)} %get-tuple-element.67.stat_ref, ...), custom_call_target="tpu_custom_call" | custom-call | flops 1000 | bytes 1000 | tf_op jit(solution)/shard_map/contrast/pallas_call | solution.py:485
  65.5 0.0 collective-permute-start.12
  65.5 2.4 %collective-permute-start.13 = (bf16[1,64,1152]{2,1,0:T(8,128)(2,1)S(1)}, bf16[1,64,1152]{2,1,0:T(8,128)(2,1)S(1)}, u32[]{:S(2)}, u32[]{:S(2)}) collective-permute-start(bf16[1,64,1152]{2,1,0:T(8,128)(2,1)S(1)} %slice.3), channel_id=1, source_target_pairs={{0,121},{8,17},{16,9},{24,33},{32,25},{40,49},{48,41},{56,65},{64,... | collective-permute-start | bytes 442376 | tf_op jit(solution)/shard_map/grad_cor/ppermute | solution.py:425
  67.9 0.6 collective-permute-start.14
  68.5 1.1 %collective-permute-start.15 = (bf16[1,64,1024]{2,1,0:T(8,128)(2,1)S(1)}, bf16[1,64,1024]{2,1,0:T(8,128)(2,1)S(1)}, u32[]{:S(2)}, u32[]{:S(2)}) collective-permute-start(bf16[1,64,1024]{2,1,0:T(8,128)(2,1)S(1)} %get-tuple-element.71), channel_id=1, source_target_pairs={{0,120},{8,16},{16,8},{24,32},{32,24},{40,48},{48,40},{56,64},{64,... | collective-permute-start | bytes 393224 | tf_op jit(solution)/shard_map/query_off/ppermute | solution.py:425
  69.6 4.4 %query_grads.1 = bf16[2,64,1024]{2,1,0:T(8,128)(2,1)} custom-call(s32[2]{0:T(128)S(1)} %pad_add_fusion.here_ref, s32[8,32]{1,0:T(8,128)S(1)} %copy-done.8, bf16[2,64,1024]{2,1,0:T(8,128)(2,1)S(1)} %bitcast.31, bf16[2,64,1152]{2,1,0:T(8,128)(2,1)S(1)} %get-tuple-element.70.grad_ref.rest_6_, f32[2,64,128]{2,1,0:T(8,128)S(1)} %get-tuple-element.74.stats_ref, ...), custom_call_target="tpu_custom_call" | custom-call | flops 1000 | bytes 1000 | tf_op jit(solution)/shard_map/query_grads/pallas_call | solution.py:497
  74.0 0.0 collective-permute-done.16.rest_0_
  74.0 4.7 %collective-permute-done.15.rest_2_ = bf16[1,64,1024]{2,1,0:T(8,128)(2,1)S(1)} collective-permute-done((bf16[1,64,1024]{2,1,0:T(8,128)(2,1)S(1)}, bf16[1,64,1024]{2,1,0:T(8,128)(2,1)S(1)}, u32[]{:S(2)}, u32[]{:S(2)}) %collective-permute-start.15) | collective-permute-done | bytes 131104 | tf_op jit(solution)/shard_map/query_off/ppermute | solution.py:425
  78.8 0.4 collective-permute-done.13.cor_ref.rest_9_
  79.2 0.0 collective-permute-done.14.rest_8_
  79.2 0.0 collective-permute-done.12.swap_ref.rest_7_
  79.2 0.1 grad_pack.1
  79.2 3.8 %collective-permute-start.17 = (bf16[3,64,1152]{2,1,0:T(8,128)(2,1)S(1)}, bf16[3,64,1152]{2,1,0:T(8,128)(2,1)S(1)}, u32[]{:S(2)}, u32[]{:S(2)}) collective-permute-start(bf16[3,64,1152]{2,1,0:T(8,128)(2,1)S(1)} %get-tuple-element.78), channel_id=1, source_target_pairs={{0,2},{8,10},{16,18},{24,26},{32,34},{40,42},{48,50},{56,58},{64,6... | collective-permute-start | bytes 1327112 | tf_op jit(solution)/shard_map/grad_far/ppermute | solution.py:425
  83.0 1.5 %collective-permute-start.18 = (bf16[3,64,1024]{2,1,0:T(8,128)(2,1)S(1)}, bf16[3,64,1024]{2,1,0:T(8,128)(2,1)S(1)}, u32[]{:S(2)}, u32[]{:S(2)}) collective-permute-start(bf16[3,64,1024]{2,1,0:T(8,128)(2,1)S(1)} %collective-permute-done.16.rest_0_), channel_id=1, source_target_pairs={{0,8},{8,0},{16,24},{24,16},{32,40},{40,32},{48,56},{56,48},{64,72... | collective-permute-start | bytes 1179656 | tf_op jit(solution)/shard_map/query_far_twin/ppermute | solution.py:425
  84.5 0.3 collective-permute-start.20
  84.7 0.2 collective-permute-start.19
  85.0 1.6 %collective-permute-done.19.rest_5_ = bf16[2,64,1024]{2,1,0:T(8,128)(2,1)S(1)} collective-permute-done((bf16[2,64,1024]{2,1,0:T(8,128)(2,1)S(1)}, bf16[2,64,1024]{2,1,0:T(8,128)(2,1)S(1)}, u32[]{:S(2)}, u32[]{:S(2)}) %collective-permute-start.19) | collective-permute-done | bytes 262176 | tf_op jit(solution)/shard_map/query_twin/ppermute | solution.py:425
  86.6 0.0 collective-permute-done.20.rest_10_
  86.6 3.4 %inner_key_grads.1 = (f32[2,64,1024]{2,1,0:T(8,128)S(1)}, f32[2,64,1024]{2,1,0:T(8,128)S(1)}) custom-call(s32[2]{0:T(128)S(1)} %pad_add_fusion.here_ref, s32[8,32]{1,0:T(8,128)S(1)} %copy-done.8, bf16[2,64,1024]{2,1,0:T(8,128)(2,1)S(1)} %bitcast.16, bf16[2,64,1024]{2,1,0:T(8,128)(2,1)S(1)} %bitcast.24, bf16[2,64,1024]{2,1,0:T(8,128)(2,1)S(1)} %bitcast.32, ...), custom_call_target="tpu_custom_call" | custom-call | flops 1000 | bytes 1000 | tf_op jit(solution)/shard_map/inner_key_grads/pallas_call | solution.py:521
  90.0 0.0 collective-permute-done.18.rest_1_
  90.0 1.3 %collective-permute-done.17.rest_1_.rest_2_ = bf16[3,64,1152]{2,1,0:T(8,128)(2,1)S(1)} collective-permute-done((bf16[3,64,1152]{2,1,0:T(8,128)(2,1)S(1)}, bf16[3,64,1152]{2,1,0:T(8,128)(2,1)S(1)}, u32[]{:S(2)}, u32[]{:S(2)}) %collective-permute-start.17) | collective-permute-done | bytes 442400 | tf_op jit(solution)/shard_map/grad_far/ppermute | solution.py:425
  91.3 2.0 %collective-permute-start.21 = (bf16[3,64,1152]{2,1,0:T(8,128)(2,1)S(1)}, bf16[3,64,1152]{2,1,0:T(8,128)(2,1)S(1)}, u32[]{:S(2)}, u32[]{:S(2)}) collective-permute-start(bf16[3,64,1152]{2,1,0:T(8,128)(2,1)S(1)} %collective-permute-done.17.rest_1_.rest_2_), channel_id=1, source_target_pairs={{0,8},{8,0},{16,24},{24,16},{32,40},{40,32},{48,56},{56,48},{64,72... | collective-permute-start | bytes 1327112 | tf_op jit(solution)/shard_map/grad_last_twin/ppermute | solution.py:425
  93.3 1.7 %outer_near_key_grads.1 = (bf16[64,1024]{1,0:T(8,128)(2,1)S(1)}, bf16[64,1024]{1,0:T(8,128)(2,1)S(1)}) custom-call(s32[2]{0:T(128)S(1)} %pad_add_fusion.here_ref, s32[8,32]{1,0:T(8,128)S(1)} %copy-done.8, bf16[2,64,1024]{2,1,0:T(8,128)(2,1)S(1)} %bitcast.17, bf16[2,64,1024]{2,1,0:T(8,128)(2,1)S(1)} %bitcast.25, ...), custom_call_target="tpu_custom_call" | custom-call | flops 1000 | bytes 1000 | tf_op jit(solution)/shard_map/outer_near_key_grads/pallas_call | solution.py:534
  95.0 0.0 collective-permute-done.21.rest_3_
  95.0 2.5 %outer_face_key_grads.1 = (bf16[2,64,1024]{2,1,0:T(8,128)(2,1)}, bf16[2,64,1024]{2,1,0:T(8,128)(2,1)}) custom-call(s32[2]{0:T(128)S(1)} %pad_add_fusion.here_ref, s32[8,32]{1,0:T(8,128)S(1)} %copy-done.8, bf16[2,64,1024]{2,1,0:T(8,128)(2,1)S(1)} %bitcast.18, bf16[2,64,1024]{2,1,0:T(8,128)(2,1)S(1)} %bitcast.26, ...), custom_call_target="tpu_custom_call" | custom-call | flops 1000 | bytes 1000 | tf_op jit(solution)/shard_map/outer_face_key_grads/pallas_call | solution.py:541
  (12 shorter events, 0.1 us)
Async XLA Ops:
  0.6 9.6 %collective-permute-start = (bf16[2,64,1024]{2,1,0:T(8,128)(2,1)}, bf16[2,64,1024]{2,1,0:T(8,128)(2,1)S(1)}, u32[]{:S(2)}, u32[]{:S(2)}) collective-permute-start(bf16[2,64,1024]{2,1,0:T(8,128)(2,1)} %bitcast.11), channel_id=1, source_target_pairs={{0,1},{8,9},{16,17},{24,25},{32,33},{40,41},{48,49},{56,57},{64,65... | collective-permute-start | bytes 786440 | tf_op jit(solution)/shard_map/key_swap/ppermute | solution.py:425
  4.3 14.9 %collective-permute-start.1 = (bf16[2,64,1024]{2,1,0:T(8,128)(2,1)}, bf16[2,64,1024]{2,1,0:T(8,128)(2,1)S(1)}, u32[]{:S(2)}, u32[]{:S(2)}) collective-permute-start(bf16[2,64,1024]{2,1,0:T(8,128)(2,1)} %bitcast.19), channel_id=1, source_target_pairs={{0,1},{8,9},{16,17},{24,25},{32,33},{40,41},{48,49},{56,57},{64,65... | collective-permute-start | bytes 786440 | tf_op jit(solution)/shard_map/value_swap/ppermute | solution.py:425
  4.5 0.9 copy-start
  5.4 0.9 copy-start.2
  6.4 0.9 copy-start.4
  7.3 0.9 copy-start.6
  8.3 0.7 copy-start.9
  8.9 21.2 %copy-start.1 = (bf16[1,2,64,1024]{3,2,1,0:T(8,128)(2,1)S(1)}, bf16[1,2,64,1024]{3,2,1,0:T(8,128)(2,1)}, u32[]{:S(2)}) copy-start(bf16[1,2,64,1024]{3,2,1,0:T(8,128)(2,1)} %param.7) | copy-start | bytes 786436
  8.9 21.2 %copy-start.3 = (bf16[1,2,64,1024]{3,2,1,0:T(8,128)(2,1)S(1)}, bf16[1,2,64,1024]{3,2,1,0:T(8,128)(2,1)}, u32[]{:S(2)}) copy-start(bf16[1,2,64,1024]{3,2,1,0:T(8,128)(2,1)} %param.8) | copy-start | bytes 786436
  8.9 21.2 %copy-start.5 = (bf16[1,2,64,1024]{3,2,1,0:T(8,128)(2,1)S(1)}, bf16[1,2,64,1024]{3,2,1,0:T(8,128)(2,1)}, u32[]{:S(2)}) copy-start(bf16[1,2,64,1024]{3,2,1,0:T(8,128)(2,1)} %param.6) | copy-start | bytes 786436
  10.2 19.9 %collective-permute-start.4 = (bf16[3,64,1024]{2,1,0:T(8,128)(2,1)S(1)}, bf16[3,64,1024]{2,1,0:T(8,128)(2,1)S(1)}, u32[]{:S(2)}, u32[]{:S(2)}) collective-permute-start(bf16[3,64,1024]{2,1,0:T(8,128)(2,1)S(1)} %get-tuple-element.60), channel_id=1, source_target_pairs={{0,121},{8,17},{16,9},{24,33},{32,25},{40,49},{48,41},{56,65},{64,... | collective-permute-start | bytes 1179656 | tf_op jit(solution)/shard_map/kvs_cor/ppermute | solution.py:425
  15.5 8.9 %collective-permute-start.2 = (bf16[2,64,1024]{2,1,0:T(8,128)(2,1)S(1)}, bf16[2,64,1024]{2,1,0:T(8,128)(2,1)S(1)}, u32[]{:S(2)}, u32[]{:S(2)}) collective-permute-start(bf16[2,64,1024]{2,1,0:T(8,128)(2,1)S(1)} %collective-permute-done.ks_ref.rest_2_), channel_id=1, source_target_pairs={{0,2},{8,10},{16,18},{24,26},{32,34},{40,42},{48,50},{56,58},{64,6... | collective-permute-start | bytes 786440 | tf_op jit(solution)/shard_map/key_far/ppermute | solution.py:425
  19.0 9.0 %collective-permute-start.5 = (bf16[2,64,1024]{2,1,0:T(8,128)(2,1)S(1)}, bf16[2,64,1024]{2,1,0:T(8,128)(2,1)S(1)}, u32[]{:S(2)}, u32[]{:S(2)}) collective-permute-start(bf16[2,64,1024]{2,1,0:T(8,128)(2,1)S(1)} %bitcast.34), channel_id=1, source_target_pairs={{0,1},{8,9},{16,17},{24,25},{32,33},{40,41},{48,49},{56,57},{64,65... | collective-permute-start | bytes 786440 | tf_op jit(solution)/shard_map/season_swap/ppermute | solution.py:425
  19.1 10.9 %collective-permute-start.3 = (bf16[2,64,1024]{2,1,0:T(8,128)(2,1)S(1)}, bf16[2,64,1024]{2,1,0:T(8,128)(2,1)S(1)}, u32[]{:S(2)}, u32[]{:S(2)}) collective-permute-start(bf16[2,64,1024]{2,1,0:T(8,128)(2,1)S(1)} %collective-permute-done.1.vs_ref.rest_3_), channel_id=1, source_target_pairs={{0,2},{8,10},{16,18},{24,26},{32,34},{40,42},{48,50},{56,58},{64,6... | collective-permute-start | bytes 786440 | tf_op jit(solution)/shard_map/value_far/ppermute | solution.py:425
  30.2 28.9 %copy-start.8 = (s32[8,32]{1,0:T(8,128)S(1)}, s32[8,32]{1,0:T(8,128)}, u32[]{:S(2)}) copy-start(s32[8,32]{1,0:T(8,128)} %cloud_ref.11) | copy-start | bytes 3076
  30.9 21.9 %collective-permute-start.6 = (bf16[9,64,1024]{2,1,0:T(8,128)(2,1)S(1)}, bf16[9,64,1024]{2,1,0:T(8,128)(2,1)S(1)}, u32[]{:S(2)}, u32[]{:S(2)}) collective-permute-start(bf16[9,64,1024]{2,1,0:T(8,128)(2,1)S(1)} %get-tuple-element.58), channel_id=1, source_target_pairs={{0,8},{8,0},{16,24},{24,16},{32,40},{40,32},{48,56},{56,48},{64,72... | collective-permute-start | bytes 3538952 | tf_op jit(solution)/shard_map/faces_twin/ppermute | solution.py:425
  34.8 17.9 %collective-permute-start.10 = (bf16[5,64,1024]{2,1,0:T(8,128)(2,1)S(1)}, bf16[5,64,1024]{2,1,0:T(8,128)(2,1)S(1)}, u32[]{:S(2)}, u32[]{:S(2)}) collective-permute-start(bf16[5,64,1024]{2,1,0:T(8,128)(2,1)S(1)} %get-tuple-element.62), channel_id=1, source_target_pairs={{0,2},{8,10},{16,18},{24,26},{32,34},{40,42},{48,50},{56,58},{64,6... | collective-permute-start | bytes 1966088 | tf_op jit(solution)/shard_map/season_far/ppermute | solution.py:425
  38.4 14.3 %collective-permute-start.8 = (bf16[3,64,1024]{2,1,0:T(8,128)(2,1)S(1)}, bf16[3,64,1024]{2,1,0:T(8,128)(2,1)S(1)}, u32[]{:S(2)}, u32[]{:S(2)}) collective-permute-start(bf16[3,64,1024]{2,1,0:T(8,128)(2,1)S(1)} %get-tuple-element.60), channel_id=1, source_target_pairs={{0,120},{8,16},{16,8},{24,32},{32,24},{40,48},{48,40},{56,64},{64,... | collective-permute-start | bytes 1179656 | tf_op jit(solution)/shard_map/kvs_off/ppermute | solution.py:425
  38.5 14.2 %collective-permute-start.9 = (bf16[2,64,1024]{2,1,0:T(8,128)(2,1)S(1)}, bf16[2,64,1024]{2,1,0:T(8,128)(2,1)S(1)}, u32[]{:S(2)}, u32[]{:S(2)}) collective-permute-start(bf16[2,64,1024]{2,1,0:T(8,128)(2,1)S(1)} %bitcast.29), channel_id=1, source_target_pairs={{0,1},{8,9},{16,17},{24,25},{32,33},{40,41},{48,49},{56,57},{64,65... | collective-permute-start | bytes 786440 | tf_op jit(solution)/shard_map/query_swap/ppermute | solution.py:425
  39.1 6.8 %collective-permute-start.7 = (bf16[1,64,1024]{2,1,0:T(8,128)(2,1)S(1)}, bf16[1,64,1024]{2,1,0:T(8,128)(2,1)S(1)}, u32[]{:S(2)}, u32[]{:S(2)}) collective-permute-start(bf16[1,64,1024]{2,1,0:T(8,128)(2,1)S(1)} %get-tuple-element.71), channel_id=1, source_target_pairs={{0,121},{8,17},{16,9},{24,33},{32,25},{40,49},{48,41},{56,65},{64,... | collective-permute-start | bytes 393224 | tf_op jit(solution)/shard_map/query_cor/ppermute | solution.py:425
  52.7 9.8 %collective-permute-start.11 = (bf16[5,64,1024]{2,1,0:T(8,128)(2,1)S(1)}, bf16[5,64,1024]{2,1,0:T(8,128)(2,1)S(1)}, u32[]{:S(2)}, u32[]{:S(2)}) collective-permute-start(bf16[5,64,1024]{2,1,0:T(8,128)(2,1)S(1)} %collective-permute-done.10.rest_6_.rest_2_), channel_id=1, source_target_pairs={{0,8},{8,0},{16,24},{24,16},{32,40},{40,32},{48,56},{56,48},{64,72... | collective-permute-start | bytes 1966088 | tf_op jit(solution)/shard_map/season_far_twin/ppermute | solution.py:425
  54.8 7.8 %copy-start.7 = (bf16[1,2,64,1024]{3,2,1,0:T(8,128)(2,1)S(1)}, bf16[1,2,64,1024]{3,2,1,0:T(8,128)(2,1)}, u32[]{:S(2)}) copy-start(bf16[1,2,64,1024]{3,2,1,0:T(8,128)(2,1)} %param.9) | copy-start | bytes 786436
  54.8 19.2 %collective-permute-start.16 = (bf16[3,64,1024]{2,1,0:T(8,128)(2,1)S(1)}, bf16[3,64,1024]{2,1,0:T(8,128)(2,1)S(1)}, u32[]{:S(2)}, u32[]{:S(2)}) collective-permute-start(bf16[3,64,1024]{2,1,0:T(8,128)(2,1)S(1)} %join.1), channel_id=1, source_target_pairs={{0,2},{8,10},{16,18},{24,26},{32,34},{40,42},{48,50},{56,58},{64,6... | collective-permute-start | bytes 1179656 | tf_op jit(solution)/shard_map/query_far/ppermute | solution.py:425
  65.5 13.7 %collective-permute-start.12 = (bf16[2,64,1152]{2,1,0:T(8,128)(2,1)S(1)}, bf16[2,64,1152]{2,1,0:T(8,128)(2,1)S(1)}, u32[]{:S(2)}, u32[]{:S(2)}) collective-permute-start(bf16[2,64,1152]{2,1,0:T(8,128)(2,1)S(1)} %get-tuple-element.70.grad_ref.rest_6_), channel_id=1, source_target_pairs={{0,1},{8,9},{16,17},{24,25},{32,33},{40,41},{48,49},{56,57},{64,65... | collective-permute-start | bytes 884744 | tf_op jit(solution)/shard_map/grad_swap/ppermute | solution.py:425
  65.5 13.7 %collective-permute-start.13 = (bf16[1,64,1152]{2,1,0:T(8,128)(2,1)S(1)}, bf16[1,64,1152]{2,1,0:T(8,128)(2,1)S(1)}, u32[]{:S(2)}, u32[]{:S(2)}) collective-permute-start(bf16[1,64,1152]{2,1,0:T(8,128)(2,1)S(1)} %slice.3), channel_id=1, source_target_pairs={{0,121},{8,17},{16,9},{24,33},{32,25},{40,49},{48,41},{56,65},{64,... | collective-permute-start | bytes 442376 | tf_op jit(solution)/shard_map/grad_cor/ppermute | solution.py:425
  67.9 11.3 %collective-permute-start.14 = (bf16[1,64,1152]{2,1,0:T(8,128)(2,1)S(1)}, bf16[1,64,1152]{2,1,0:T(8,128)(2,1)S(1)}, u32[]{:S(2)}, u32[]{:S(2)}) collective-permute-start(bf16[1,64,1152]{2,1,0:T(8,128)(2,1)S(1)} %slice.3), channel_id=1, source_target_pairs={{0,120},{8,16},{16,8},{24,32},{32,24},{40,48},{48,40},{56,64},{64,... | collective-permute-start | bytes 442376 | tf_op jit(solution)/shard_map/grad_off/ppermute | solution.py:425
  68.5 10.3 %collective-permute-start.15 = (bf16[1,64,1024]{2,1,0:T(8,128)(2,1)S(1)}, bf16[1,64,1024]{2,1,0:T(8,128)(2,1)S(1)}, u32[]{:S(2)}, u32[]{:S(2)}) collective-permute-start(bf16[1,64,1024]{2,1,0:T(8,128)(2,1)S(1)} %get-tuple-element.71), channel_id=1, source_target_pairs={{0,120},{8,16},{16,8},{24,32},{32,24},{40,48},{48,40},{56,64},{64,... | collective-permute-start | bytes 393224 | tf_op jit(solution)/shard_map/query_off/ppermute | solution.py:425
  79.2 12.1 %collective-permute-start.17 = (bf16[3,64,1152]{2,1,0:T(8,128)(2,1)S(1)}, bf16[3,64,1152]{2,1,0:T(8,128)(2,1)S(1)}, u32[]{:S(2)}, u32[]{:S(2)}) collective-permute-start(bf16[3,64,1152]{2,1,0:T(8,128)(2,1)S(1)} %get-tuple-element.78), channel_id=1, source_target_pairs={{0,2},{8,10},{16,18},{24,26},{32,34},{40,42},{48,50},{56,58},{64,6... | collective-permute-start | bytes 1327112 | tf_op jit(solution)/shard_map/grad_far/ppermute | solution.py:425
  83.0 7.0 %collective-permute-start.18 = (bf16[3,64,1024]{2,1,0:T(8,128)(2,1)S(1)}, bf16[3,64,1024]{2,1,0:T(8,128)(2,1)S(1)}, u32[]{:S(2)}, u32[]{:S(2)}) collective-permute-start(bf16[3,64,1024]{2,1,0:T(8,128)(2,1)S(1)} %collective-permute-done.16.rest_0_), channel_id=1, source_target_pairs={{0,8},{8,0},{16,24},{24,16},{32,40},{40,32},{48,56},{56,48},{64,72... | collective-permute-start | bytes 1179656 | tf_op jit(solution)/shard_map/query_far_twin/ppermute | solution.py:425
  84.5 2.1 %collective-permute-start.20 = (bf16[2,64,1152]{2,1,0:T(8,128)(2,1)S(1)}, bf16[2,64,1152]{2,1,0:T(8,128)(2,1)S(1)}, u32[]{:S(2)}, u32[]{:S(2)}) collective-permute-start(bf16[2,64,1152]{2,1,0:T(8,128)(2,1)S(1)} %get-tuple-element.83), channel_id=1, source_target_pairs={{0,8},{8,0},{16,24},{24,16},{32,40},{40,32},{48,56},{56,48},{64,72... | collective-permute-start | bytes 884744 | tf_op jit(solution)/shard_map/grad_twin/ppermute | solution.py:425
  84.7 1.9 %collective-permute-start.19 = (bf16[2,64,1024]{2,1,0:T(8,128)(2,1)S(1)}, bf16[2,64,1024]{2,1,0:T(8,128)(2,1)S(1)}, u32[]{:S(2)}, u32[]{:S(2)}) collective-permute-start(bf16[2,64,1024]{2,1,0:T(8,128)(2,1)S(1)} %collective-permute-done.9.refs_0_.rest_1_), channel_id=1, source_target_pairs={{0,8},{8,0},{16,24},{24,16},{32,40},{40,32},{48,56},{56,48},{64,72... | collective-permute-start | bytes 786440 | tf_op jit(solution)/shard_map/query_twin/ppermute | solution.py:425
  91.3 3.7 %collective-permute-start.21 = (bf16[3,64,1152]{2,1,0:T(8,128)(2,1)S(1)}, bf16[3,64,1152]{2,1,0:T(8,128)(2,1)S(1)}, u32[]{:S(2)}, u32[]{:S(2)}) collective-permute-start(bf16[3,64,1152]{2,1,0:T(8,128)(2,1)S(1)} %collective-permute-done.17.rest_1_.rest_2_), channel_id=1, source_target_pairs={{0,8},{8,0},{16,24},{24,16},{32,40},{40,32},{48,56},{56,48},{64,72... | collective-permute-start | bytes 1327112 | tf_op jit(solution)/shard_map/grad_last_twin/ppermute | solution.py:425

commit v6 on v5

--- a/solution.py
+++ b/solution.py
@@ -469,9 +469,10 @@
     q_swap = named("query", q1, "swap")
     q_cor = named("query", q_near, "cor")
     twin = named("faces", faces, "twin")
-    twin, q_cor, off, q_swap, far = phase(twin, q_cor, off, q_swap, far)
+    q_stack = joined(q_swap, q_cor)
+    twin, q_cor, off, q_swap, q_stack, far = phase(twin, q_cor, off, q_swap, q_stack, far)
     far_twin = named("season_far", far, "twin")
-    q_far = named("query", joined(q_swap, q_cor), "far")
+    q_far = named("query", q_stack, "far")
     kvp = (k, v, k_swap, v_swap, k_far, v_far, far, cor, off, twin)
 
     att, stat = call(

time: 98.1 us -> 98.5 us (level)
  starting transfers between devices: 46.4 us -> 47.8 us
    ppermute x22, starting transfers between devices: 46.4 us -> 47.8 us  [move(): return lax.ppermute(x, AXES, way[kind])]
  transfers between devices with their start and end apart: 22 -> 22, of which waited for: 10 -> 10; matrix products, arithmetic and copies ran while one was open for 0% -> 0% of each run, Pallas kernels for 18% -> 17%
where the time goes in v6:
time: 98.5 us; the launch traced here: 98.1 us
  starting transfers between devices  47.8 us (49%)
  waiting for transfers between devices  24.6 us (25%)
  Pallas kernels  20.3 us (21%)
  local copies, waits for them, and re-layouts  4.51 us (5%)
    ppermute x22, starting transfers between devices, move(): return lax.ppermute(x, AXES, way[kind])  47.8 us
    ppermute x22, waiting for transfers between devices, move(): return lax.ppermute(x, AXES, way[kind])  24.6 us
    unnamed x20, local copies, waits for them, and re-layouts  4.5 us
    pallas_call x1, Pallas kernels, body(): call(query_kernel, 'query_grads', [SMEM, SMEM, VMEM, VMEM, VMEM] + [VMEM]...  4.44 us
    pallas_call x1, Pallas kernels, body(): call(inner_key_kernel, 'inner_key_grads', [SMEM, SMEM, VMEM, VMEM] + [VME...  3.42 us
    pallas_call x1, Pallas kernels, body(): call(attend_kernel, 'attend', [SMEM, SMEM, VMEM] + [VMEM] * 10, (shape((2...  3.39 us
    pallas_call x1, Pallas kernels, body(): call(contrast_kernel, 'contrast', [SMEM, SMEM, VMEM, VMEM, VMEM] + [VMEM]...  2.92 us
    pallas_call x1, Pallas kernels, body(): call(outer_face_kernel, 'outer_face_key_grads', [SMEM, SMEM] + [VMEM] * 1...  2.46 us
  transfers between devices with their start and end apart: 22, of which 10 were waited for; matrix products, arithmetic and copies ran while one was open for 0% of the time, Pallas kernels for 17%

profile of v6, /device:TPU:1, one launch (start us, length us, event | category | flops | bytes accessed | tf_op | source)
XLA Modules:
  0.0 98.1 jit_solution(18135088976856646350)
XLA Ops:
  0.6 3.7 %collective-permute-start = (bf16[2,64,1024]{2,1,0:T(8,128)(2,1)}, bf16[2,64,1024]{2,1,0:T(8,128)(2,1)S(1)}, u32[]{:S(2)}, u32[]{:S(2)}) collective-permute-start(bf16[2,64,1024]{2,1,0:T(8,128)(2,1)} %bitcast.11), channel_id=1, source_target_pairs={{0,1},{8,9},{16,17},{24,25},{32,33},{40,41},{48,49},{56,57},{64,65... | collective-permute-start | bytes 786440 | tf_op jit(solution)/shard_map/key_swap/ppermute | solution.py:425
  4.3 0.1 collective-permute-start.1
  4.4 0.1 pad_add_fusion.here_ref
  4.5 0.9 copy-done
  5.4 0.9 copy-done.2
  6.4 0.9 copy-done.4
  7.3 0.9 copy-done.6
  8.3 0.7 copy-done.9
  8.9 1.3 %edges.1 = (bf16[3,64,1024]{2,1,0:T(8,128)(2,1)S(1)}, bf16[1,64,1024]{2,1,0:T(8,128)(2,1)S(1)}, s32[2,64]{1,0:T(2,128)S(1)}) custom-call(s32[2]{0:T(128)S(1)} %pad_add_fusion.here_ref, s32[2,64]{1,0:T(2,128)S(1)} %bitcast.37, bf16[2,64,1024]{2,1,0:T(8,128)(2,1)S(1)} %bitcast.12, bf16[2,64,1024]{2,1,0:T(8,128)(2,1)S(1)} %bitcast.20, ...), custom_call_target="tpu_custom_call" | custom-call | flops 1000 | bytes 1000 | tf_op jit(solution)/shard_map/edges/pallas_call | solution.py:443
  10.2 0.0 collective-permute-done.ks_ref.rest_2_
  10.2 5.3 %collective-permute-start.4 = (bf16[3,64,1024]{2,1,0:T(8,128)(2,1)S(1)}, bf16[3,64,1024]{2,1,0:T(8,128)(2,1)S(1)}, u32[]{:S(2)}, u32[]{:S(2)}) collective-permute-start(bf16[3,64,1024]{2,1,0:T(8,128)(2,1)S(1)} %get-tuple-element.61), channel_id=1, source_target_pairs={{0,121},{8,17},{16,9},{24,33},{32,25},{40,49},{48,41},{56,65},{64,... | collective-permute-start | bytes 1179656 | tf_op jit(solution)/shard_map/kvs_cor/ppermute | solution.py:425
  15.5 0.5 collective-permute-start.5
  16.0 0.0 collective-permute-done.1.vs_ref.rest_3_
  16.0 3.6 %collective-permute-start.3 = (bf16[2,64,1024]{2,1,0:T(8,128)(2,1)S(1)}, bf16[2,64,1024]{2,1,0:T(8,128)(2,1)S(1)}, u32[]{:S(2)}, u32[]{:S(2)}) collective-permute-start(bf16[2,64,1024]{2,1,0:T(8,128)(2,1)S(1)} %collective-permute-done.1.vs_ref.rest_3_), channel_id=1, source_target_pairs={{0,2},{8,10},{16,18},{24,26},{32,34},{40,42},{48,50},{56,58},{64,6... | collective-permute-start | bytes 786440 | tf_op jit(solution)/shard_map/value_far/ppermute | solution.py:425
  19.6 3.5 %collective-permute-start.2 = (bf16[2,64,1024]{2,1,0:T(8,128)(2,1)S(1)}, bf16[2,64,1024]{2,1,0:T(8,128)(2,1)S(1)}, u32[]{:S(2)}, u32[]{:S(2)}) collective-permute-start(bf16[2,64,1024]{2,1,0:T(8,128)(2,1)S(1)} %collective-permute-done.ks_ref.rest_2_), channel_id=1, source_target_pairs={{0,2},{8,10},{16,18},{24,26},{32,34},{40,42},{48,50},{56,58},{64,6... | collective-permute-start | bytes 786440 | tf_op jit(solution)/shard_map/key_far/ppermute | solution.py:425
  23.2 0.4 collective-permute-done.3.vf_ref.rest_5_
  23.6 1.1 %collective-permute-done.5.ss_ref.rest_1_ = bf16[2,64,1024]{2,1,0:T(8,128)(2,1)S(1)} collective-permute-done((bf16[2,64,1024]{2,1,0:T(8,128)(2,1)S(1)}, bf16[2,64,1024]{2,1,0:T(8,128)(2,1)S(1)}, u32[]{:S(2)}, u32[]{:S(2)}) %collective-permute-start.5) | collective-permute-done | bytes 262176 | tf_op jit(solution)/shard_map/season_swap/ppermute | solution.py:425
  24.7 4.6 %collective-permute-done.2.kf_ref.rest_4_ = bf16[2,64,1024]{2,1,0:T(8,128)(2,1)S(1)} collective-permute-done((bf16[2,64,1024]{2,1,0:T(8,128)(2,1)S(1)}, bf16[2,64,1024]{2,1,0:T(8,128)(2,1)S(1)}, u32[]{:S(2)}, u32[]{:S(2)}) %collective-permute-start.2) | collective-permute-done | bytes 262176 | tf_op jit(solution)/shard_map/key_far/ppermute | solution.py:425
  29.3 0.9 collective-permute-done.4.cor_ref.rest_7_.rest_4_
  30.2 0.0 copy-done.1
  30.2 0.0 copy-done.3
  30.2 0.0 copy-start.8
  30.2 0.7 pack.1
  30.9 3.9 %collective-permute-start.6 = (bf16[9,64,1024]{2,1,0:T(8,128)(2,1)S(1)}, bf16[9,64,1024]{2,1,0:T(8,128)(2,1)S(1)}, u32[]{:S(2)}, u32[]{:S(2)}) collective-permute-start(bf16[9,64,1024]{2,1,0:T(8,128)(2,1)S(1)} %get-tuple-element.59), channel_id=1, source_target_pairs={{0,8},{8,0},{16,24},{24,16},{32,40},{40,32},{48,56},{56,48},{64,72... | collective-permute-start | bytes 3538952 | tf_op jit(solution)/shard_map/faces_twin/ppermute | solution.py:425
  34.8 3.6 %collective-permute-start.10 = (bf16[5,64,1024]{2,1,0:T(8,128)(2,1)S(1)}, bf16[5,64,1024]{2,1,0:T(8,128)(2,1)S(1)}, u32[]{:S(2)}, u32[]{:S(2)}) collective-permute-start(bf16[5,64,1024]{2,1,0:T(8,128)(2,1)S(1)} %get-tuple-element.63), channel_id=1, source_target_pairs={{0,2},{8,10},{16,18},{24,26},{32,34},{40,42},{48,50},{56,58},{64,6... | collective-permute-start | bytes 1966088 | tf_op jit(solution)/shard_map/season_far/ppermute | solution.py:425
  38.4 0.1 collective-permute-start.8
  38.5 0.6 collective-permute-start.9
  39.1 3.8 %collective-permute-start.7 = (bf16[1,64,1024]{2,1,0:T(8,128)(2,1)S(1)}, bf16[1,64,1024]{2,1,0:T(8,128)(2,1)S(1)}, u32[]{:S(2)}, u32[]{:S(2)}) collective-permute-start(bf16[1,64,1024]{2,1,0:T(8,128)(2,1)S(1)} %get-tuple-element.72), channel_id=1, source_target_pairs={{0,121},{8,17},{16,9},{24,33},{32,25},{40,49},{48,41},{56,65},{64,... | collective-permute-start | bytes 393224 | tf_op jit(solution)/shard_map/query_cor/ppermute | solution.py:425
  42.9 4.4 %collective-permute-done.7.refs_1_.rest_3_ = bf16[1,64,1024]{2,1,0:T(8,128)(2,1)S(1)} collective-permute-done((bf16[1,64,1024]{2,1,0:T(8,128)(2,1)S(1)}, bf16[1,64,1024]{2,1,0:T(8,128)(2,1)S(1)}, u32[]{:S(2)}, u32[]{:S(2)}) %collective-permute-start.7) | collective-permute-done | bytes 131104 | tf_op jit(solution)/shard_map/query_cor/ppermute | solution.py:425
  47.3 4.6 %collective-permute-done.9.refs_0_.rest_1_ = bf16[2,64,1024]{2,1,0:T(8,128)(2,1)S(1)} collective-permute-done((bf16[2,64,1024]{2,1,0:T(8,128)(2,1)S(1)}, bf16[2,64,1024]{2,1,0:T(8,128)(2,1)S(1)}, u32[]{:S(2)}, u32[]{:S(2)}) %collective-permute-start.9) | collective-permute-done | bytes 262176 | tf_op jit(solution)/shard_map/query_swap/ppermute | solution.py:425
  51.9 0.0 copy-start.7
  51.9 0.0 collective-permute-done.8.rest_8_.rest_3_
  51.9 0.5 collective-permute-done.10.rest_6_.rest_2_
  52.5 0.0 collective-permute-done.6.rest_9_.rest_5_.rest_4_
  52.5 2.3 %collective-permute-start.11 = (bf16[5,64,1024]{2,1,0:T(8,128)(2,1)S(1)}, bf16[5,64,1024]{2,1,0:T(8,128)(2,1)S(1)}, u32[]{:S(2)}, u32[]{:S(2)}) collective-permute-start(bf16[5,64,1024]{2,1,0:T(8,128)(2,1)S(1)} %collective-permute-done.10.rest_6_.rest_2_), channel_id=1, source_target_pairs={{0,8},{8,0},{16,24},{24,16},{32,40},{40,32},{48,56},{56,48},{64,72... | collective-permute-start | bytes 1966088 | tf_op jit(solution)/shard_map/season_far_twin/ppermute | solution.py:425
  54.8 4.2 %collective-permute-start.16 = (bf16[3,64,1024]{2,1,0:T(8,128)(2,1)S(1)}, bf16[3,64,1024]{2,1,0:T(8,128)(2,1)S(1)}, u32[]{:S(2)}, u32[]{:S(2)}) collective-permute-start(bf16[3,64,1024]{2,1,0:T(8,128)(2,1)S(1)} %join.1), channel_id=1, source_target_pairs={{0,2},{8,10},{16,18},{24,26},{32,34},{40,42},{48,50},{56,58},{64,6... | collective-permute-start | bytes 1179656 | tf_op jit(solution)/shard_map/query_far/ppermute | solution.py:425
  59.0 0.0 copy-done.8
  59.0 3.4 %attend.1 = (bf16[2,64,1024]{2,1,0:T(8,128)(2,1)S(1)}, f32[2,64,128]{2,1,0:T(8,128)S(1)}) custom-call(s32[2]{0:T(128)S(1)} %pad_add_fusion.here_ref, s32[8,32]{1,0:T(8,128)S(1)} %copy-done.8, bf16[2,64,1024]{2,1,0:T(8,128)(2,1)S(1)} %bitcast.30, bf16[2,64,1024]{2,1,0:T(8,128)(2,1)S(1)} %bitcast.14, bf16[2,64,1024]{2,1,0:T(8,128)(2,1)S(1)} %bitcast.22, ...), custom_call_target="tpu_custom_call" | custom-call | flops 1000 | bytes 1000 | tf_op jit(solution)/shard_map/attend/pallas_call | solution.py:478
  62.4 0.0 collective-permute-done.11.rest_6_
  62.4 2.9 %contrast.1 = (f32[2,64]{1,0:T(2,128)}, bf16[2,64,1152]{2,1,0:T(8,128)(2,1)S(1)}, f32[2,64,128]{2,1,0:T(8,128)S(1)}) custom-call(s32[2]{0:T(128)S(1)} %pad_add_fusion.here_ref, s32[8,32]{1,0:T(8,128)S(1)} %copy-done.8, bf16[2,64,1024]{2,1,0:T(8,128)(2,1)S(1)} %get-tuple-element.67.att_ref, f32[2,64,128]{2,1,0:T(8,128)S(1)} %get-tuple-element.68.stat_ref, ...), custom_call_target="tpu_custom_call" | custom-call | flops 1000 | bytes 1000 | tf_op jit(solution)/shard_map/contrast/pallas_call | solution.py:486
  65.4 0.0 collective-permute-start.12
  65.4 0.7 collective-permute-start.14
  66.1 2.9 %collective-permute-start.13 = (bf16[1,64,1152]{2,1,0:T(8,128)(2,1)S(1)}, bf16[1,64,1152]{2,1,0:T(8,128)(2,1)S(1)}, u32[]{:S(2)}, u32[]{:S(2)}) collective-permute-start(bf16[1,64,1152]{2,1,0:T(8,128)(2,1)S(1)} %slice.3), channel_id=1, source_target_pairs={{0,121},{8,17},{16,9},{24,33},{32,25},{40,49},{48,41},{56,65},{64,... | collective-permute-start | bytes 442376 | tf_op jit(solution)/shard_map/grad_cor/ppermute | solution.py:425
  69.0 0.7 collective-permute-start.15
  69.7 4.4 %query_grads.1 = bf16[2,64,1024]{2,1,0:T(8,128)(2,1)} custom-call(s32[2]{0:T(128)S(1)} %pad_add_fusion.here_ref, s32[8,32]{1,0:T(8,128)S(1)} %copy-done.8, bf16[2,64,1024]{2,1,0:T(8,128)(2,1)S(1)} %bitcast.31, bf16[2,64,1152]{2,1,0:T(8,128)(2,1)S(1)} %get-tuple-element.71.grad_ref.rest_6_, f32[2,64,128]{2,1,0:T(8,128)S(1)} %get-tuple-element.74.stats_ref, ...), custom_call_target="tpu_custom_call" | custom-call | flops 1000 | bytes 1000 | tf_op jit(solution)/shard_map/query_grads/pallas_call | solution.py:498
  74.2 0.0 collective-permute-done.16.rest_0_
  74.2 5.2 %collective-permute-done.15.rest_2_ = bf16[1,64,1024]{2,1,0:T(8,128)(2,1)S(1)} collective-permute-done((bf16[1,64,1024]{2,1,0:T(8,128)(2,1)S(1)}, bf16[1,64,1024]{2,1,0:T(8,128)(2,1)S(1)}, u32[]{:S(2)}, u32[]{:S(2)}) %collective-permute-start.15) | collective-permute-done | bytes 131104 | tf_op jit(solution)/shard_map/query_off/ppermute | solution.py:425
  79.4 0.0 collective-permute-done.14.rest_8_
  79.4 0.0 collective-permute-done.13.cor_ref.rest_9_
  79.4 0.0 collective-permute-done.12.swap_ref.rest_7_
  79.4 0.1 grad_pack.1
  79.5 4.2 %collective-permute-start.17 = (bf16[3,64,1152]{2,1,0:T(8,128)(2,1)S(1)}, bf16[3,64,1152]{2,1,0:T(8,128)(2,1)S(1)}, u32[]{:S(2)}, u32[]{:S(2)}) collective-permute-start(bf16[3,64,1152]{2,1,0:T(8,128)(2,1)S(1)} %get-tuple-element.79), channel_id=1, source_target_pairs={{0,2},{8,10},{16,18},{24,26},{32,34},{40,42},{48,50},{56,58},{64,6... | collective-permute-start | bytes 1327112 | tf_op jit(solution)/shard_map/grad_far/ppermute | solution.py:425
  83.6 1.5 %collective-permute-start.18 = (bf16[3,64,1024]{2,1,0:T(8,128)(2,1)S(1)}, bf16[3,64,1024]{2,1,0:T(8,128)(2,1)S(1)}, u32[]{:S(2)}, u32[]{:S(2)}) collective-permute-start(bf16[3,64,1024]{2,1,0:T(8,128)(2,1)S(1)} %collective-permute-done.16.rest_0_), channel_id=1, source_target_pairs={{0,8},{8,0},{16,24},{24,16},{32,40},{40,32},{48,56},{56,48},{64,72... | collective-permute-start | bytes 1179656 | tf_op jit(solution)/shard_map/query_far_twin/ppermute | solution.py:425
  85.2 0.3 collective-permute-start.20
  85.4 0.2 collective-permute-start.19
  85.7 1.6 %collective-permute-done.19.rest_5_ = bf16[2,64,1024]{2,1,0:T(8,128)(2,1)S(1)} collective-permute-done((bf16[2,64,1024]{2,1,0:T(8,128)(2,1)S(1)}, bf16[2,64,1024]{2,1,0:T(8,128)(2,1)S(1)}, u32[]{:S(2)}, u32[]{:S(2)}) %collective-permute-start.19) | collective-permute-done | bytes 262176 | tf_op jit(solution)/shard_map/query_twin/ppermute | solution.py:425
  87.3 0.0 collective-permute-done.20.rest_10_
  87.3 3.4 %inner_key_grads.1 = (f32[2,64,1024]{2,1,0:T(8,128)S(1)}, f32[2,64,1024]{2,1,0:T(8,128)S(1)}) custom-call(s32[2]{0:T(128)S(1)} %pad_add_fusion.here_ref, s32[8,32]{1,0:T(8,128)S(1)} %copy-done.8, bf16[2,64,1024]{2,1,0:T(8,128)(2,1)S(1)} %bitcast.16, bf16[2,64,1024]{2,1,0:T(8,128)(2,1)S(1)} %bitcast.24, bf16[2,64,1024]{2,1,0:T(8,128)(2,1)S(1)} %bitcast.32, ...), custom_call_target="tpu_custom_call" | custom-call | flops 1000 | bytes 1000 | tf_op jit(solution)/shard_map/inner_key_grads/pallas_call | solution.py:522
  90.7 0.0 collective-permute-done.18.rest_1_
  90.7 1.2 %collective-permute-done.17.rest_1_.rest_2_ = bf16[3,64,1152]{2,1,0:T(8,128)(2,1)S(1)} collective-permute-done((bf16[3,64,1152]{2,1,0:T(8,128)(2,1)S(1)}, bf16[3,64,1152]{2,1,0:T(8,128)(2,1)S(1)}, u32[]{:S(2)}, u32[]{:S(2)}) %collective-permute-start.17) | collective-permute-done | bytes 442400 | tf_op jit(solution)/shard_map/grad_far/ppermute | solution.py:425
  91.9 2.1 %collective-permute-start.21 = (bf16[3,64,1152]{2,1,0:T(8,128)(2,1)S(1)}, bf16[3,64,1152]{2,1,0:T(8,128)(2,1)S(1)}, u32[]{:S(2)}, u32[]{:S(2)}) collective-permute-start(bf16[3,64,1152]{2,1,0:T(8,128)(2,1)S(1)} %collective-permute-done.17.rest_1_.rest_2_), channel_id=1, source_target_pairs={{0,8},{8,0},{16,24},{24,16},{32,40},{40,32},{48,56},{56,48},{64,72... | collective-permute-start | bytes 1327112 | tf_op jit(solution)/shard_map/grad_last_twin/ppermute | solution.py:425
  94.0 1.7 %outer_near_key_grads.1 = (bf16[64,1024]{1,0:T(8,128)(2,1)S(1)}, bf16[64,1024]{1,0:T(8,128)(2,1)S(1)}) custom-call(s32[2]{0:T(128)S(1)} %pad_add_fusion.here_ref, s32[8,32]{1,0:T(8,128)S(1)} %copy-done.8, bf16[2,64,1024]{2,1,0:T(8,128)(2,1)S(1)} %bitcast.17, bf16[2,64,1024]{2,1,0:T(8,128)(2,1)S(1)} %bitcast.25, ...), custom_call_target="tpu_custom_call" | custom-call | flops 1000 | bytes 1000 | tf_op jit(solution)/shard_map/outer_near_key_grads/pallas_call | solution.py:535
  95.7 0.0 collective-permute-done.21.rest_3_
  95.7 2.5 %outer_face_key_grads.1 = (bf16[2,64,1024]{2,1,0:T(8,128)(2,1)}, bf16[2,64,1024]{2,1,0:T(8,128)(2,1)}) custom-call(s32[2]{0:T(128)S(1)} %pad_add_fusion.here_ref, s32[8,32]{1,0:T(8,128)S(1)} %copy-done.8, bf16[2,64,1024]{2,1,0:T(8,128)(2,1)S(1)} %bitcast.18, bf16[2,64,1024]{2,1,0:T(8,128)(2,1)S(1)} %bitcast.26, ...), custom_call_target="tpu_custom_call" | custom-call | flops 1000 | bytes 1000 | tf_op jit(solution)/shard_map/outer_face_key_grads/pallas_call | solution.py:542
  (12 shorter events, 0.1 us)
Async XLA Ops:
  0.6 9.6 %collective-permute-start = (bf16[2,64,1024]{2,1,0:T(8,128)(2,1)}, bf16[2,64,1024]{2,1,0:T(8,128)(2,1)S(1)}, u32[]{:S(2)}, u32[]{:S(2)}) collective-permute-start(bf16[2,64,1024]{2,1,0:T(8,128)(2,1)} %bitcast.11), channel_id=1, source_target_pairs={{0,1},{8,9},{16,17},{24,25},{32,33},{40,41},{48,49},{56,57},{64,65... | collective-permute-start | bytes 786440 | tf_op jit(solution)/shard_map/key_swap/ppermute | solution.py:425
  4.3 11.7 %collective-permute-start.1 = (bf16[2,64,1024]{2,1,0:T(8,128)(2,1)}, bf16[2,64,1024]{2,1,0:T(8,128)(2,1)S(1)}, u32[]{:S(2)}, u32[]{:S(2)}) collective-permute-start(bf16[2,64,1024]{2,1,0:T(8,128)(2,1)} %bitcast.19), channel_id=1, source_target_pairs={{0,1},{8,9},{16,17},{24,25},{32,33},{40,41},{48,49},{56,57},{64,65... | collective-permute-start | bytes 786440 | tf_op jit(solution)/shard_map/value_swap/ppermute | solution.py:425
  4.5 0.9 copy-start
  5.4 0.9 copy-start.2
  6.4 0.9 copy-start.4
  7.3 0.9 copy-start.6
  8.3 0.7 copy-start.9
  8.9 21.2 %copy-start.1 = (bf16[1,2,64,1024]{3,2,1,0:T(8,128)(2,1)S(1)}, bf16[1,2,64,1024]{3,2,1,0:T(8,128)(2,1)}, u32[]{:S(2)}) copy-start(bf16[1,2,64,1024]{3,2,1,0:T(8,128)(2,1)} %param.7) | copy-start | bytes 786436
  8.9 21.2 %copy-start.3 = (bf16[1,2,64,1024]{3,2,1,0:T(8,128)(2,1)S(1)}, bf16[1,2,64,1024]{3,2,1,0:T(8,128)(2,1)}, u32[]{:S(2)}) copy-start(bf16[1,2,64,1024]{3,2,1,0:T(8,128)(2,1)} %param.8) | copy-start | bytes 786436
  8.9 21.2 %copy-start.5 = (bf16[1,2,64,1024]{3,2,1,0:T(8,128)(2,1)S(1)}, bf16[1,2,64,1024]{3,2,1,0:T(8,128)(2,1)}, u32[]{:S(2)}) copy-start(bf16[1,2,64,1024]{3,2,1,0:T(8,128)(2,1)} %param.6) | copy-start | bytes 786436
  10.2 19.9 %collective-permute-start.4 = (bf16[3,64,1024]{2,1,0:T(8,128)(2,1)S(1)}, bf16[3,64,1024]{2,1,0:T(8,128)(2,1)S(1)}, u32[]{:S(2)}, u32[]{:S(2)}) collective-permute-start(bf16[3,64,1024]{2,1,0:T(8,128)(2,1)S(1)} %get-tuple-element.61), channel_id=1, source_target_pairs={{0,121},{8,17},{16,9},{24,33},{32,25},{40,49},{48,41},{56,65},{64,... | collective-permute-start | bytes 1179656 | tf_op jit(solution)/shard_map/kvs_cor/ppermute | solution.py:425
  15.5 9.2 %collective-permute-start.5 = (bf16[2,64,1024]{2,1,0:T(8,128)(2,1)S(1)}, bf16[2,64,1024]{2,1,0:T(8,128)(2,1)S(1)}, u32[]{:S(2)}, u32[]{:S(2)}) collective-permute-start(bf16[2,64,1024]{2,1,0:T(8,128)(2,1)S(1)} %bitcast.34), channel_id=1, source_target_pairs={{0,1},{8,9},{16,17},{24,25},{32,33},{40,41},{48,49},{56,57},{64,65... | collective-permute-start | bytes 786440 | tf_op jit(solution)/shard_map/season_swap/ppermute | solution.py:425
  16.0 7.6 %collective-permute-start.3 = (bf16[2,64,1024]{2,1,0:T(8,128)(2,1)S(1)}, bf16[2,64,1024]{2,1,0:T(8,128)(2,1)S(1)}, u32[]{:S(2)}, u32[]{:S(2)}) collective-permute-start(bf16[2,64,1024]{2,1,0:T(8,128)(2,1)S(1)} %collective-permute-done.1.vs_ref.rest_3_), channel_id=1, source_target_pairs={{0,2},{8,10},{16,18},{24,26},{32,34},{40,42},{48,50},{56,58},{64,6... | collective-permute-start | bytes 786440 | tf_op jit(solution)/shard_map/value_far/ppermute | solution.py:425
  19.6 9.7 %collective-permute-start.2 = (bf16[2,64,1024]{2,1,0:T(8,128)(2,1)S(1)}, bf16[2,64,1024]{2,1,0:T(8,128)(2,1)S(1)}, u32[]{:S(2)}, u32[]{:S(2)}) collective-permute-start(bf16[2,64,1024]{2,1,0:T(8,128)(2,1)S(1)} %collective-permute-done.ks_ref.rest_2_), channel_id=1, source_target_pairs={{0,2},{8,10},{16,18},{24,26},{32,34},{40,42},{48,50},{56,58},{64,6... | collective-permute-start | bytes 786440 | tf_op jit(solution)/shard_map/key_far/ppermute | solution.py:425
  30.2 28.8 %copy-start.8 = (s32[8,32]{1,0:T(8,128)S(1)}, s32[8,32]{1,0:T(8,128)}, u32[]{:S(2)}) copy-start(s32[8,32]{1,0:T(8,128)} %cloud_ref.11) | copy-start | bytes 3076
  30.9 21.6 %collective-permute-start.6 = (bf16[9,64,1024]{2,1,0:T(8,128)(2,1)S(1)}, bf16[9,64,1024]{2,1,0:T(8,128)(2,1)S(1)}, u32[]{:S(2)}, u32[]{:S(2)}) collective-permute-start(bf16[9,64,1024]{2,1,0:T(8,128)(2,1)S(1)} %get-tuple-element.59), channel_id=1, source_target_pairs={{0,8},{8,0},{16,24},{24,16},{32,40},{40,32},{48,56},{56,48},{64,72... | collective-permute-start | bytes 3538952 | tf_op jit(solution)/shard_map/faces_twin/ppermute | solution.py:425
  34.8 17.7 %collective-permute-start.10 = (bf16[5,64,1024]{2,1,0:T(8,128)(2,1)S(1)}, bf16[5,64,1024]{2,1,0:T(8,128)(2,1)S(1)}, u32[]{:S(2)}, u32[]{:S(2)}) collective-permute-start(bf16[5,64,1024]{2,1,0:T(8,128)(2,1)S(1)} %get-tuple-element.63), channel_id=1, source_target_pairs={{0,2},{8,10},{16,18},{24,26},{32,34},{40,42},{48,50},{56,58},{64,6... | collective-permute-start | bytes 1966088 | tf_op jit(solution)/shard_map/season_far/ppermute | solution.py:425
  38.4 13.5 %collective-permute-start.8 = (bf16[3,64,1024]{2,1,0:T(8,128)(2,1)S(1)}, bf16[3,64,1024]{2,1,0:T(8,128)(2,1)S(1)}, u32[]{:S(2)}, u32[]{:S(2)}) collective-permute-start(bf16[3,64,1024]{2,1,0:T(8,128)(2,1)S(1)} %get-tuple-element.61), channel_id=1, source_target_pairs={{0,120},{8,16},{16,8},{24,32},{32,24},{40,48},{48,40},{56,64},{64,... | collective-permute-start | bytes 1179656 | tf_op jit(solution)/shard_map/kvs_off/ppermute | solution.py:425
  38.5 13.4 %collective-permute-start.9 = (bf16[2,64,1024]{2,1,0:T(8,128)(2,1)S(1)}, bf16[2,64,1024]{2,1,0:T(8,128)(2,1)S(1)}, u32[]{:S(2)}, u32[]{:S(2)}) collective-permute-start(bf16[2,64,1024]{2,1,0:T(8,128)(2,1)S(1)} %bitcast.29), channel_id=1, source_target_pairs={{0,1},{8,9},{16,17},{24,25},{32,33},{40,41},{48,49},{56,57},{64,65... | collective-permute-start | bytes 786440 | tf_op jit(solution)/shard_map/query_swap/ppermute | solution.py:425
  39.1 8.2 %collective-permute-start.7 = (bf16[1,64,1024]{2,1,0:T(8,128)(2,1)S(1)}, bf16[1,64,1024]{2,1,0:T(8,128)(2,1)S(1)}, u32[]{:S(2)}, u32[]{:S(2)}) collective-permute-start(bf16[1,64,1024]{2,1,0:T(8,128)(2,1)S(1)} %get-tuple-element.72), channel_id=1, source_target_pairs={{0,121},{8,17},{16,9},{24,33},{32,25},{40,49},{48,41},{56,65},{64,... | collective-permute-start | bytes 393224 | tf_op jit(solution)/shard_map/query_cor/ppermute | solution.py:425
  51.9 10.5 %copy-start.7 = (bf16[1,2,64,1024]{3,2,1,0:T(8,128)(2,1)S(1)}, bf16[1,2,64,1024]{3,2,1,0:T(8,128)(2,1)}, u32[]{:S(2)}) copy-start(bf16[1,2,64,1024]{3,2,1,0:T(8,128)(2,1)} %param.9) | copy-start | bytes 786436
  52.5 9.9 %collective-permute-start.11 = (bf16[5,64,1024]{2,1,0:T(8,128)(2,1)S(1)}, bf16[5,64,1024]{2,1,0:T(8,128)(2,1)S(1)}, u32[]{:S(2)}, u32[]{:S(2)}) collective-permute-start(bf16[5,64,1024]{2,1,0:T(8,128)(2,1)S(1)} %collective-permute-done.10.rest_6_.rest_2_), channel_id=1, source_target_pairs={{0,8},{8,0},{16,24},{24,16},{32,40},{40,32},{48,56},{56,48},{64,72... | collective-permute-start | bytes 1966088 | tf_op jit(solution)/shard_map/season_far_twin/ppermute | solution.py:425
  54.8 19.3 %collective-permute-start.16 = (bf16[3,64,1024]{2,1,0:T(8,128)(2,1)S(1)}, bf16[3,64,1024]{2,1,0:T(8,128)(2,1)S(1)}, u32[]{:S(2)}, u32[]{:S(2)}) collective-permute-start(bf16[3,64,1024]{2,1,0:T(8,128)(2,1)S(1)} %join.1), channel_id=1, source_target_pairs={{0,2},{8,10},{16,18},{24,26},{32,34},{40,42},{48,50},{56,58},{64,6... | collective-permute-start | bytes 1179656 | tf_op jit(solution)/shard_map/query_far/ppermute | solution.py:425
  65.4 14.0 %collective-permute-start.12 = (bf16[2,64,1152]{2,1,0:T(8,128)(2,1)S(1)}, bf16[2,64,1152]{2,1,0:T(8,128)(2,1)S(1)}, u32[]{:S(2)}, u32[]{:S(2)}) collective-permute-start(bf16[2,64,1152]{2,1,0:T(8,128)(2,1)S(1)} %get-tuple-element.71.grad_ref.rest_6_), channel_id=1, source_target_pairs={{0,1},{8,9},{16,17},{24,25},{32,33},{40,41},{48,49},{56,57},{64,65... | collective-permute-start | bytes 884744 | tf_op jit(solution)/shard_map/grad_swap/ppermute | solution.py:425
  65.4 14.0 %collective-permute-start.14 = (bf16[1,64,1152]{2,1,0:T(8,128)(2,1)S(1)}, bf16[1,64,1152]{2,1,0:T(8,128)(2,1)S(1)}, u32[]{:S(2)}, u32[]{:S(2)}) collective-permute-start(bf16[1,64,1152]{2,1,0:T(8,128)(2,1)S(1)} %slice.3), channel_id=1, source_target_pairs={{0,120},{8,16},{16,8},{24,32},{32,24},{40,48},{48,40},{56,64},{64,... | collective-permute-start | bytes 442376 | tf_op jit(solution)/shard_map/grad_off/ppermute | solution.py:425
  66.1 13.3 %collective-permute-start.13 = (bf16[1,64,1152]{2,1,0:T(8,128)(2,1)S(1)}, bf16[1,64,1152]{2,1,0:T(8,128)(2,1)S(1)}, u32[]{:S(2)}, u32[]{:S(2)}) collective-permute-start(bf16[1,64,1152]{2,1,0:T(8,128)(2,1)S(1)} %slice.3), channel_id=1, source_target_pairs={{0,121},{8,17},{16,9},{24,33},{32,25},{40,49},{48,41},{56,65},{64,... | collective-permute-start | bytes 442376 | tf_op jit(solution)/shard_map/grad_cor/ppermute | solution.py:425
  69.0 10.4 %collective-permute-start.15 = (bf16[1,64,1024]{2,1,0:T(8,128)(2,1)S(1)}, bf16[1,64,1024]{2,1,0:T(8,128)(2,1)S(1)}, u32[]{:S(2)}, u32[]{:S(2)}) collective-permute-start(bf16[1,64,1024]{2,1,0:T(8,128)(2,1)S(1)} %get-tuple-element.72), channel_id=1, source_target_pairs={{0,120},{8,16},{16,8},{24,32},{32,24},{40,48},{48,40},{56,64},{64,... | collective-permute-start | bytes 393224 | tf_op jit(solution)/shard_map/query_off/ppermute | solution.py:425
  79.5 12.4 %collective-permute-start.17 = (bf16[3,64,1152]{2,1,0:T(8,128)(2,1)S(1)}, bf16[3,64,1152]{2,1,0:T(8,128)(2,1)S(1)}, u32[]{:S(2)}, u32[]{:S(2)}) collective-permute-start(bf16[3,64,1152]{2,1,0:T(8,128)(2,1)S(1)} %get-tuple-element.79), channel_id=1, source_target_pairs={{0,2},{8,10},{16,18},{24,26},{32,34},{40,42},{48,50},{56,58},{64,6... | collective-permute-start | bytes 1327112 | tf_op jit(solution)/shard_map/grad_far/ppermute | solution.py:425
  83.6 7.1 %collective-permute-start.18 = (bf16[3,64,1024]{2,1,0:T(8,128)(2,1)S(1)}, bf16[3,64,1024]{2,1,0:T(8,128)(2,1)S(1)}, u32[]{:S(2)}, u32[]{:S(2)}) collective-permute-start(bf16[3,64,1024]{2,1,0:T(8,128)(2,1)S(1)} %collective-permute-done.16.rest_0_), channel_id=1, source_target_pairs={{0,8},{8,0},{16,24},{24,16},{32,40},{40,32},{48,56},{56,48},{64,72... | collective-permute-start | bytes 1179656 | tf_op jit(solution)/shard_map/query_far_twin/ppermute | solution.py:425
  85.2 2.1 %collective-permute-start.20 = (bf16[2,64,1152]{2,1,0:T(8,128)(2,1)S(1)}, bf16[2,64,1152]{2,1,0:T(8,128)(2,1)S(1)}, u32[]{:S(2)}, u32[]{:S(2)}) collective-permute-start(bf16[2,64,1152]{2,1,0:T(8,128)(2,1)S(1)} %get-tuple-element.85), channel_id=1, source_target_pairs={{0,8},{8,0},{16,24},{24,16},{32,40},{40,32},{48,56},{56,48},{64,72... | collective-permute-start | bytes 884744 | tf_op jit(solution)/shard_map/grad_twin/ppermute | solution.py:425
  85.4 1.9 %collective-permute-start.19 = (bf16[2,64,1024]{2,1,0:T(8,128)(2,1)S(1)}, bf16[2,64,1024]{2,1,0:T(8,128)(2,1)S(1)}, u32[]{:S(2)}, u32[]{:S(2)}) collective-permute-start(bf16[2,64,1024]{2,1,0:T(8,128)(2,1)S(1)} %collective-permute-done.9.refs_0_.rest_1_), channel_id=1, source_target_pairs={{0,8},{8,0},{16,24},{24,16},{32,40},{40,32},{48,56},{56,48},{64,72... | collective-permute-start | bytes 786440 | tf_op jit(solution)/shard_map/query_twin/ppermute | solution.py:425
  91.9 3.7 %collective-permute-start.21 = (bf16[3,64,1152]{2,1,0:T(8,128)(2,1)S(1)}, bf16[3,64,1152]{2,1,0:T(8,128)(2,1)S(1)}, u32[]{:S(2)}, u32[]{:S(2)}) collective-permute-start(bf16[3,64,1152]{2,1,0:T(8,128)(2,1)S(1)} %collective-permute-done.17.rest_1_.rest_2_), channel_id=1, source_target_pairs={{0,8},{8,0},{16,24},{24,16},{32,40},{40,32},{48,56},{56,48},{64,72... | collective-permute-start | bytes 1327112 | tf_op jit(solution)/shard_map/grad_last_twin/ppermute | solution.py:425
